TPU v7x, 128 devices: a whole 4x4x4 slice. The times are simulated.
128 devices in a mesh: gx: 16 (over y, x), yz: 8 (over z, core).
Axes of the slice: x: 4, y: 4, z: 4, core: 2. Of those that a mesh axis runs over, the one named last changes fastest.
Arguments:
- particle_phi: float32 [4, 16, 256, 128, 128], P(None, None, 'gx', 'yz'), may hold values from -6 to 6
- particle_offset: float32 [3, 16, 256, 128, 128], P(None, None, 'gx', 'yz'), may hold values from 0 to 1
- slot_count: int32 [256, 128, 128], P('gx', 'yz'), may hold values from 4 to 16
- velocity: float32 [3, 256, 128, 128], P(None, None, 'gx', 'yz'), may hold values from -6 to 6
- diffusivity: float32 [256, 128, 128], P(None, 'gx', 'yz'), may hold values from 0.1 to 2
- migrant_phi: float32 [4, 262144], P(None, ('gx', 'yz')), may hold values from -6 to 6
- migrant_offset: float32 [3, 262144], P(None, ('gx', 'yz')), may hold values from 0 to 1
- migrant_dest: int32 [262144, 1], P(('gx', 'yz')), may hold values from 0 to 127; in each aligned block of 2048 rows (0 to 2047, 2048 to 4095, ...) at most 64 rows name the same one
- migrant_cell: int32 [262144], P(('gx', 'yz')), may hold values from 0 to 32767
Outputs:
- particle_new: float32 [4, 16, 256, 128, 128], P(None, None, 'gx', 'yz')
- migrant_new: float32 [4, 262144], P(None, ('gx', 'yz'))
Inputs may be any that keep to these rules, and one draw needn't show every extreme that they name: The first slot_count slots of a cell hold particles; the others are padding. `migrant_dest`: brick index gx_index * 8 + yz_index; the rows of one device name one brick at most 64 times, and in every draw some device names some brick exactly 64 times. `migrant_cell`: x * 16 * 128 + y * 128 + z within the new brick.
All inputs are finite; a program needn't handle non-finite values.
Results may differ from a plain program's by a relative error of at most 0.0003.
Values sent between devices are 32-bit elements; how exact they have to be, the bound alone decides.
No kernel may reach another device: no remote copies, remote signals or barrier semaphores. Data moves between devices by JAX's collectives and lax.ppermute only.
A program may use at most 192 MiB of HBM per device.

v0:
```python
import functools

import jax
import jax.numpy as jnp
from jax import lax
from jax.experimental import pallas as pl
from jax.experimental.pallas import tpu as pltpu
from jax.sharding import PartitionSpec as P

time_step = 0.08
mix_coeff = 0.5
f32 = jnp.float32
bf16 = jnp.bfloat16
MB = 2**20
WHOLE = pl.BlockSpec(memory_space=pltpu.VMEM)
SCALARS = pl.BlockSpec(memory_space=pltpu.SMEM)


def iota(shape, dim):
    return lax.broadcasted_iota(jnp.int32, shape, dim)


def split(value):
    top = value.astype(bf16).astype(f32)
    return top, value - top


def dot_nt(left, right):
    return lax.dot_general(left, right, (((1,), (1,)), ((), ())), preferred_element_type=f32)


def dot_nn(left, right):
    return lax.dot_general(left, right, (((1,), (0,)), ((), ())), preferred_element_type=f32)


def call(body, outs, specs, scratch=(), vmem=48, cost=None, name=None):
    return pl.pallas_call(
        body,
        out_shape=tuple(jax.ShapeDtypeStruct(s, d) for s, d in outs),
        in_specs=list(specs),
        out_specs=tuple(WHOLE for _ in outs),
        scratch_shapes=list(scratch),
        compiler_params=pltpu.CompilerParams(vmem_limit_bytes=vmem * MB),
        cost_estimate=cost,
        name=name,
    )


def dispatch_body(dest_ref, cell_ref, phi_ref, off_ref, out_ref, rank_ref, *, bricks, cap):
    rows = dest_ref.shape[1]
    hot = jnp.where(iota((bricks, rows), 0) == dest_ref[...], 1.0, 0.0).astype(bf16)
    step = 256
    before = jnp.where(iota((step, step), 0) < iota((step, step), 1), 1.0, 0.0).astype(bf16)
    carry = jnp.zeros((bricks, 1), f32)
    ranks = []
    for b in range(rows // step):
        part = hot[:, b * step : (b + 1) * step]
        wide = part.astype(f32)
        count = dot_nn(part, before) + carry
        ranks.append(jnp.sum(wide * count, axis=0, keepdims=True))
        carry = carry + jnp.sum(wide, axis=1, keepdims=True)
    rank = jnp.concatenate(ranks, axis=1).astype(jnp.int32)
    rank_ref[...] = rank
    here = iota((cap, rows), 0) == rank
    channels = [phi_ref[c : c + 1, :] for c in range(4)]
    channels += [off_ref[c : c + 1, :] for c in range(3)]
    channels.append((cell_ref[...] + 1).astype(f32))
    tops, rests = [], []
    for row in channels:
        top, rest = split(row)
        tops.append(jnp.where(here, top, 0.0).astype(bf16))
        rests.append(jnp.where(here, rest, 0.0).astype(bf16))
    sent = dot_nt(jnp.concatenate(tops, axis=0), hot) + dot_nt(
        jnp.concatenate(rests, axis=0), hot
    )
    sent = sent.T
    for r in range(4):
        out_ref[:, r, :] = sent[:, 128 * r : 128 * (r + 1)]


def collect_body(dest_ref, rank_ref, back_ref, out_ref, *, bricks, cap):
    rows = dest_ref.shape[1]
    hot = jnp.where(iota((bricks, rows), 0) == dest_ref[...], 1.0, 0.0).astype(bf16)
    table = jnp.concatenate([back_ref[:, 0, :], back_ref[:, 1, :]], axis=1).T
    top, rest = split(table)
    both = jnp.concatenate([top, rest], axis=1).astype(bf16)
    got = dot_nn(both, jnp.concatenate([hot, hot], axis=0))
    here = iota((cap, rows), 0) == rank_ref[...]
    for c in range(4):
        picked = jnp.where(here, got[c * cap : (c + 1) * cap], 0.0)
        out_ref[c : c + 1, :] = jnp.sum(picked, axis=0, keepdims=True)


def local_body(phi_ref, count_ref, out_ref):
    count = count_ref[0]
    for c in range(4):
        total = None
        for s in range(phi_ref.shape[1]):
            value = jnp.where(count > s, phi_ref[c, s, 0], 0.0)
            total = value if total is None else total + value
        out_ref[c, 0] = total


def scatter_body(
    arr_ref, local_ref, count_ref, mean_ref, xs_ref, ehi_ref, elo_ref, e15_ref, e01_ref, acc_ref
):
    half = arr_ref.shape[0] // 2
    lane = iota((half, 128), 1)
    for r in range(4):
        low = arr_ref[0:half, r, :]
        high = arr_ref[half : 2 * half, r, :]
        xs_ref[2 * r] = jnp.where(lane < 64, low, pltpu.roll(high, 64, 1))
        xs_ref[2 * r + 1] = jnp.where(lane < 64, pltpu.roll(low, 64, 1), high)
    acc_ref[...] = jnp.zeros_like(acc_ref)

    def step(i, carry):
        at = pl.multiple_of(i * 8, 8)
        cell = xs_ref[7, pl.ds(at, 8), :].astype(jnp.int32) - 1
        plane = cell >> 7
        depth = cell & 127
        parts = [split(xs_ref[c, pl.ds(at, 8), :]) for c in range(4)]
        lefts, rights = [], []
        for u in range(8):
            at_z = iota((128, 128), 0) == depth[u : u + 1]
            at_p = iota((256, 128), 0) == plane[u : u + 1]
            rights.append(jnp.where(at_p, 1.0, 0.0).astype(bf16))
            blocks = [jnp.where(at_z, 1.0, 0.0).astype(bf16)]
            for top, rest in parts:
                blocks.append(jnp.where(at_z, top[u : u + 1], 0.0).astype(bf16))
                blocks.append(jnp.where(at_z, rest[u : u + 1], 0.0).astype(bf16))
            lefts.append(jnp.concatenate(blocks, axis=0))
        acc_ref[...] += dot_nt(
            jnp.concatenate(lefts, axis=1), jnp.concatenate(rights, axis=1)
        )
        return carry

    lax.fori_loop(0, half // 8, step, 0)
    wx, wy = count_ref.shape[0], count_ref.shape[1]
    number = acc_ref[0:128, :].T.reshape(wx, wy, 128)
    share = 1.0 / (count_ref[...].astype(f32) + number)
    for c in range(4):
        at = 128 + 256 * c
        moved = (acc_ref[at : at + 128, :] + acc_ref[at + 128 : at + 256, :]).T
        mean = (local_ref[c] + moved.reshape(wx, wy, 128)) * share
        mean_ref[c] = mean
        ehi_ref[c] = mean[wx - 1 : wx]
        elo_ref[c] = mean[0:2]
        e15_ref[c] = mean[:, wy - 1, :]
        e01_ref[0, c] = mean[:, 0, :]
        e01_ref[1, c] = mean[:, 1, :]


def edge_body(lo_ref, hi_ref, e15_ref, e01_ref, up_ref, down_ref):
    wy = lo_ref.shape[2]
    for ref, source, y in (
        (up_ref, lambda c: e15_ref[c], wy - 1),
        (down_ref.at[0], lambda c: e01_ref[0, c], 0),
        (down_ref.at[1], lambda c: e01_ref[1, c], 1),
    ):
        for c in range(4):
            ref[c, 0:16, :] = source(c)
            ref[c, 16:24, :] = jnp.concatenate(
                [
                    hi_ref[c, 0, y : y + 1, :],
                    hi_ref[c, 1, y : y + 1, :],
                    lo_ref[c, 0, y : y + 1, :],
                    jnp.zeros((5, 128), f32),
                ],
                axis=0,
            )


def pencil_x_body(vel_ref, gam_ref, out_ref):
    groups = out_ref.shape[0]
    pieces = [vel_ref[c].reshape(128, vel_ref.shape[3]).T for c in range(3)]
    pieces.append(gam_ref[...].reshape(128, gam_ref.shape[2]).T)
    rows = jnp.concatenate(pieces, axis=1)
    row = iota((8, 512), 0)
    zero = jnp.zeros((8, 512), f32)
    for p in range(groups):
        out_ref[p, 0:16, :] = rows[16 * p : 16 * p + 16]
        above = rows[16 * p + 16 : 16 * p + 24] if p < groups - 1 else zero
        below = pltpu.roll(rows[16 * p - 8 : 16 * p], 3, 0) if p > 0 else zero
        out_ref[p, 16:24, :] = jnp.where(
            row < 2, above, jnp.where(row == 2, below, 0.0)
        )


def pencil_y_body(in_ref, out_ref):
    groups = out_ref.shape[0]
    lane = iota((24, 128), 1)
    zero = jnp.zeros((24, 128), f32)
    for q in range(groups):
        out_ref[q, :, 0:512] = in_ref[2 * q]
        out_ref[q, :, 512:1024] = in_ref[2 * q + 1]
        pieces = []
        for c in range(4):
            lanes = slice(128 * c, 128 * c + 128)
            above = in_ref[2 * q + 2, :, lanes] if q < groups - 1 else zero
            below = pltpu.roll(in_ref[2 * q - 1, :, lanes], 48, 1) if q > 0 else zero
            pieces.append(jnp.where(lane < 32, above, jnp.where(lane < 48, below, 0.0)))
        for e in (0, 1):
            out_ref[q, :, 1024 + 128 * e : 1152 + 128 * e] = jnp.where(
                lane < 64, pieces[2 * e], pltpu.roll(pieces[2 * e + 1], 64, 1)
            )


def brick_body(in_ref, brick_ref, col_ref, tall_ref):
    lane = iota((8, 128), 1)
    for tile in range(10):
        for xt in range(3):
            group = [in_ref[j, 8 * xt : 8 * xt + 8, 128 * tile : 128 * tile + 128] for j in range(8)]
            for bit in (4, 2, 1):
                shift = 16 * bit
                high = (lane // shift) % 2 == 1
                fresh = list(group)
                for j in range(8):
                    if j & bit:
                        continue
                    first, second = group[j], group[j | bit]
                    fresh[j] = jnp.where(high, pltpu.roll(second, shift, 1), first)
                    fresh[j | bit] = jnp.where(high, second, pltpu.roll(first, 128 - shift, 1))
                group = fresh
            for g in range(8):
                if tile < 8:
                    c, y = tile % 4, 8 * (tile // 4) + g
                    at = (c * 16 + y) * 24 + 8 * xt
                    tall_ref[at : at + 8, :] = group[g]
                elif g % 4 < 3:
                    c, y = 2 * (tile - 8) + g // 4, g % 4
                    col_ref[c, y, 8 * xt : 8 * xt + 8, :] = group[g]
    for c in range(4):
        for x in range(19):
            for yt in (0, 8):
                brick_ref[c, x, yt : yt + 8, :] = tall_ref[
                    pl.ds((c * 16 + yt) * 24 + x, 8, stride=24), :
                ]


def z_shift(value, up):
    lane = iota(value.shape, value.ndim - 1)
    if up:
        return jnp.where(lane == 127, 0.0, pltpu.roll(value, 127, value.ndim - 1))
    return jnp.where(lane == 0, 0.0, pltpu.roll(value, 1, value.ndim - 1))


def flux(centre, gamma, sides, velocity):
    total = None
    drift = None
    for (up, gamma_up, down, gamma_down), speed in zip(sides, velocity):
        term = (gamma + gamma_up) * (up - centre) + (gamma + gamma_down) * (down - centre)
        total = term if total is None else total + term
        move = speed * (up - down)
        drift = move if drift is None else drift + move
    return (0.5 * time_step) * (total - drift)


def slot_terms(xs_ref, at):
    def row(c):
        return jnp.concatenate([xs_ref[c, pl.ds(at + e, 1), :] for e in (0, 1)], axis=1)

    cell = row(7).astype(jnp.int32) - 1
    filled = cell >= 0
    depth = cell & 127
    x = jnp.where(filled, cell >> 11, -2)
    y = (cell >> 7) & 15
    return row, x, y, depth


def hat(number, at, frac):
    spot = iota((number, at.shape[1]), 0)
    return jnp.where(spot == at, 1.0 - frac, 0.0) + jnp.where(spot == at + 1, frac, 0.0)


def depth_weights(depth, frac):
    top, rest = split(hat(128, depth, frac))
    top = top.astype(bf16)
    return jnp.concatenate([top, top, rest.astype(bf16)], axis=0)


def widen(tab_ref, lhs_ref):
    top, rest = split(tab_ref[...])
    top = top.astype(bf16)
    lhs_ref[:, 0:128] = top
    lhs_ref[:, 128:256] = rest.astype(bf16)
    lhs_ref[:, 256:384] = top


def total_y(value):
    return jnp.sum(value, axis=0, keepdims=True)


def blend_inner_body(mean_ref, brick_ref, col_ref, xs_ref, out_ref, tab_ref, lhs_ref):
    for c in range(4):
        tab_ref[256 * c : 256 * c + 256, :] = mean_ref[c].reshape(256, 128)
    tab_ref[1024:1280, :] = brick_ref[3, 0:16].reshape(256, 128)
    tab_ref[1280:1296, :] = brick_ref[3, 16]
    tab_ref[1296:1320, :] = col_ref[3, 0]
    tab_ref[1320:1328, :] = jnp.zeros((8, 128), f32)
    widen(tab_ref, lhs_ref)

    def step(i, carry):
        row, x, y, depth = slot_terms(xs_ref, 2 * i)
        along = dot_nn(lhs_ref[...], depth_weights(depth, row(6)))
        wx = hat(24, x, row(4))
        wy = hat(24, y, row(5))
        sums = [None] * 5
        for k in range(16):
            weight = wx[k : k + 1] * wy[0:16]
            for c in range(5):
                at = 256 * c + 16 * k
                term = along[at : at + 16] * weight
                sums[c] = term if sums[c] is None else sums[c] + term
        sums[4] = sums[4] + along[1280:1296] * (wx[16:17] * wy[0:16])
        got = [total_y(value) for value in sums]
        got[4] = got[4] + total_y(along[1296:1320] * (wx * wy[16:17]))
        for c in range(5):
            for e in (0, 1):
                out_ref[c, pl.ds(2 * i + e, 1), :] = got[c][:, 128 * e : 128 * e + 128]
        return carry

    lax.fori_loop(0, xs_ref.shape[1] // 2, step, 0)


def transport_body(
    last_ref, mean_ref, lo_ref, hi_ref, ylo_ref, yhi_ref, brick_ref, col_ref, f_ref, tcol_ref, mp_ref, gp_ref
):
    x_in = jnp.where(last_ref[0] == 1, 0.0, 1.0).astype(f32)
    y_in = jnp.where(last_ref[1] == 1, 0.0, 1.0).astype(f32)
    for c in range(4):
        mp_ref[c, 0:16, 8:24, :] = mean_ref[c]
        mp_ref[c, 16:18, 8:24, :] = hi_ref[c]
        mp_ref[c, 18, 8:24, :] = lo_ref[c, 0]
        mp_ref[c, :, 7, :] = ylo_ref[c, 0:19, :]
        mp_ref[c, :, 24, :] = yhi_ref[0, c, 0:19, :]
    gp_ref[:, 8:24, :] = brick_ref[3]
    gp_ref[:, 7, :] = col_ref[3, 2, 0:19, :]
    gp_ref[:, 24, :] = col_ref[3, 0, 0:19, :]

    def plane(x, carry):
        below = jnp.where(x == 0, 18, x - 1)
        keep = jnp.where(x == 16, x_in, 1.0)
        gamma = gp_ref[x, 8:24, :]
        gammas = [
            (gp_ref[x + 1, 8:24, :], gp_ref[below, 8:24, :]),
            (gp_ref[x, 9:25, :], gp_ref[x, 7:23, :]),
            (z_shift(gamma, True), z_shift(gamma, False)),
        ]
        velocity = [brick_ref[d, x] for d in range(3)]
        for c in range(4):
            centre = mp_ref[c, x, 8:24, :]
            means = [
                (mp_ref[c, x + 1, 8:24, :], mp_ref[c, below, 8:24, :]),
                (mp_ref[c, x, 9:25, :], mp_ref[c, x, 7:23, :]),
                (z_shift(centre, True), z_shift(centre, False)),
            ]
            sides = [(m[0], g[0], m[1], g[1]) for m, g in zip(means, gammas)]
            f_ref[c, x, 0:16, :] = centre
            f_ref[4 + c, x, 0:16, :] = flux(centre, gamma, sides, velocity) * keep
        f_ref[8, x, 0:16, :] = gamma
        return carry

    lax.fori_loop(0, 17, plane, 0)
    row = iota((24, 128), 0)

    def x_up(value):
        return pltpu.roll(value, 23, 0)

    def x_down(value):
        return jnp.where(row == 0, value[18:19], pltpu.roll(value, 1, 0))

    keep = jnp.where(row == 16, x_in, 1.0) * y_in
    gamma = col_ref[3, 0]
    gamma_low = jnp.concatenate([gp_ref[:, 23, :], jnp.zeros((5, 128), f32)], axis=0)
    gammas = [
        (x_up(gamma), x_down(gamma)),
        (col_ref[3, 1], gamma_low),
        (z_shift(gamma, True), z_shift(gamma, False)),
    ]
    velocity = [col_ref[d, 0] for d in range(3)]
    for c in range(4):
        centre = yhi_ref[0, c]
        low = jnp.concatenate([mp_ref[c, :, 23, :], jnp.zeros((5, 128), f32)], axis=0)
        means = [
            (x_up(centre), x_down(centre)),
            (yhi_ref[1, c], low),
            (z_shift(centre, True), z_shift(centre, False)),
        ]
        sides = [(m[0], g[0], m[1], g[1]) for m, g in zip(means, gammas)]
        moved = flux(centre, gamma, sides, velocity) * keep
        tcol_ref[c] = centre
        tcol_ref[4 + c] = moved
        f_ref[c, :, 16, :] = centre[0:17]
        f_ref[4 + c, :, 16, :] = moved[0:17]
    f_ref[8, :, 16, :] = gamma[0:17]


def blend_outer_body(f_ref, tcol_ref, inner_ref, xs_ref, out_ref, tab_ref, lhs_ref, new_ref):
    for c in range(4):
        tab_ref[256 * c : 256 * c + 256, :] = f_ref[4 + c, 0:16, 0:16, :].reshape(256, 128)
    for c in range(8):
        tab_ref[1024 + 16 * c : 1040 + 16 * c, :] = f_ref[c, 16, 0:16, :]
        tab_ref[1152 + 24 * c : 1176 + 24 * c, :] = tcol_ref[c]
    widen(tab_ref, lhs_ref)

    def step(i, carry):
        row, x, y, depth = slot_terms(xs_ref, 2 * i)
        along = dot_nn(lhs_ref[...], depth_weights(depth, row(6)))
        wx = hat(24, x, row(4))
        wy = hat(24, y, row(5))
        sums = [None] * 4
        for k in range(16):
            weight = wx[k : k + 1] * wy[0:16]
            for c in range(4):
                at = 256 * c + 16 * k
                term = along[at : at + 16] * weight
                sums[c] = term if sums[c] is None else sums[c] + term
        top = wx[16:17] * wy[0:16]
        side = wx * wy[16:17]
        got = []
        for c in range(8):
            value = total_y(along[1024 + 16 * c : 1040 + 16 * c] * top)
            value = value + total_y(along[1152 + 24 * c : 1176 + 24 * c] * side)
            if c >= 4:
                value = value + total_y(sums[c - 4])
            got.append(value)

        def inner(c):
            return jnp.concatenate([inner_ref[c, pl.ds(2 * i + e, 1), :] for e in (0, 1)], axis=1)

        rate = mix_coeff * inner(4)
        for c in range(4):
            phi = row(c)
            fresh = phi + got[4 + c] - rate * (phi - (got[c] + inner(c)))
            for e in (0, 1):
                new_ref[c, pl.ds(2 * i + e, 1), :] = fresh[:, 128 * e : 128 * e + 128]
        return carry

    half = xs_ref.shape[1]
    lax.fori_loop(0, half // 2, step, 0)
    lane = iota((half, 128), 1)
    for r in range(2):
        low, high = new_ref[2 * r], new_ref[2 * r + 1]
        out_ref[0:half, r, :] = jnp.where(lane < 64, low, pltpu.roll(high, 64, 1))
        out_ref[half : 2 * half, r, :] = jnp.where(lane < 64, pltpu.roll(low, 64, 1), high)


def update_body(phi_ref, off_ref, count_ref, f_ref, out_ref, coef_ref):
    x = pl.program_id(0)
    slots = phi_ref.shape[1]
    for yt in (0, 8):
        for ch in range(9):
            corner = {}
            for sx in (0, 1):
                for sy in (0, 1):
                    value = f_ref[ch, x + sx, yt + sy : yt + sy + 8, :]
                    corner[sx, sy, 0] = value
                    corner[sx, sy, 1] = z_shift(value, True) - value
            for sz in (0, 1):
                c00, c01 = corner[0, 0, sz], corner[0, 1, sz]
                c10, c11 = corner[1, 0, sz], corner[1, 1, sz]
                dx = c10 - c00
                coef_ref[ch, sz] = c00
                coef_ref[ch, 2 + sz] = c01 - c00
                coef_ref[ch, 4 + sz] = dx
                coef_ref[ch, 6 + sz] = (c11 - c01) - dx
        count = count_ref[0, yt : yt + 8, :]
        rows = slice(yt, yt + 8)
        width = 4

        def group(i, carry):
            at = [i * width + s for s in range(width)]
            a = [off_ref[0, s, 0, rows, :] for s in at]
            b = [off_ref[1, s, 0, rows, :] for s in at]
            d = [off_ref[2, s, 0, rows, :] for s in at]

            def blend(ch):
                k = [coef_ref[ch, n] for n in range(8)]
                return [
                    ((k[7] * d[n] + k[6]) * b[n] + (k[5] * d[n] + k[4])) * a[n]
                    + ((k[3] * d[n] + k[2]) * b[n] + (k[1] * d[n] + k[0]))
                    for n in range(width)
                ]

            rate = [mix_coeff * value for value in blend(8)]
            for c in range(4):
                mean = blend(c)
                moved = blend(4 + c)
                for n in range(width):
                    phi = phi_ref[c, at[n], 0, rows, :]
                    fresh = phi + moved[n] - rate[n] * (phi - mean[n])
                    out_ref[c, at[n], 0, rows, :] = jnp.where(count > at[n], fresh, 0.0)
            return carry

        lax.fori_loop(0, slots // width, group, 0)


def shifted(value, axis, by):
    count = lax.axis_size(axis)
    pairs = [(i, i + by) for i in range(count) if 0 <= i + by < count]
    return lax.ppermute(value, axis, pairs)


def exchange(value, axis):
    return lax.all_to_all(value, axis, split_axis=0, concat_axis=0, tiled=True)


def shards(phi, offset, count, velocity, diffusivity, m_phi, m_offset, m_dest, m_cell):
    slots, wx, wy, depth = phi.shape[1:]
    groups_x, groups_y = lax.axis_size("gx"), lax.axis_size("yz")
    bricks = groups_x * groups_y
    rows = m_phi.shape[1]
    cap = 4 * rows // bricks
    half = bricks // 2

    dest = m_dest.reshape(1, rows)
    cell = m_cell.reshape(1, rows)
    sent, rank = call(
        functools.partial(dispatch_body, bricks=bricks, cap=cap),
        [((bricks, 4, 128), f32), ((1, rows), jnp.int32)],
        [WHOLE] * 4,
        name="dispatch",
    )(dest, cell, m_phi, m_offset)

    pencil, = call(
        pencil_x_body, [((groups_x, 24, 512), f32)], [WHOLE] * 2, name="pencil_x"
    )(jnp.transpose(velocity, (0, 2, 3, 1)), jnp.transpose(diffusivity, (1, 2, 0)))
    pencil = exchange(pencil, "gx")
    arrived = exchange(sent, ("gx", "yz"))

    block_phi = pl.BlockSpec((4, slots, 1, wy, depth), lambda i: (0, 0, i, 0, 0))
    block_off = pl.BlockSpec((3, slots, 1, wy, depth), lambda i: (0, 0, i, 0, 0))
    block_count = pl.BlockSpec((1, wy, depth), lambda i: (i, 0, 0))
    local_sum = pl.pallas_call(
        local_body,
        out_shape=jax.ShapeDtypeStruct((4, wx, wy, depth), f32),
        grid=(wx,),
        in_specs=[block_phi, block_count],
        out_specs=pl.BlockSpec((4, 1, wy, depth), lambda i: (0, i, 0, 0)),
        compiler_params=pltpu.CompilerParams(vmem_limit_bytes=16 * MB),
        cost_estimate=pl.CostEstimate(flops=4 * 10**6, bytes_accessed=9 * 10**6, transcendentals=0),
        name="local_sum",
    )(phi, count)

    wide, = call(pencil_y_body, [((groups_y, 24, 1280), f32)], [WHOLE], name="pencil_y")(pencil)
    wide = exchange(wide, "yz")
    brick, col = call(
        brick_body,
        [((4, 19, wy, depth), f32), ((4, 3, 24, depth), f32)],
        [WHOLE],
        [pltpu.VMEM((4 * 16 * 24, 128), f32)],
        name="brick",
    )(wide)

    mean, xs, ehi, elo, e15, e01 = call(
        scatter_body,
        [
            ((4, wx, wy, depth), f32),
            ((8, half, 128), f32),
            ((4, 1, wy, depth), f32),
            ((4, 2, wy, depth), f32),
            ((4, wx, depth), f32),
            ((2, 4, wx, depth), f32),
        ],
        [WHOLE] * 3,
        [pltpu.VMEM((9 * 128, 256), f32)],
        name="scatter",
    )(arrived, local_sum, count)

    lo = shifted(ehi, "gx", 1)
    hi = shifted(elo, "gx", -1)
    inner, = call(
        blend_inner_body,
        [((5, half, 128), f32)],
        [WHOLE] * 4,
        [pltpu.VMEM((1328, 128), f32), pltpu.VMEM((1328, 384), bf16)],
        cost=pl.CostEstimate(flops=8 * 10**9, bytes_accessed=3 * 10**6, transcendentals=0),
        name="blend_inner",
    )(mean, brick, col, xs)
    up, down = call(
        edge_body,
        [((4, 24, depth), f32), ((2, 4, 24, depth), f32)],
        [WHOLE] * 4,
        name="edge",
    )(lo, hi, e15, e01)
    ylo = shifted(up, "yz", 1)
    yhi = shifted(down, "yz", -1)

    last = jnp.stack(
        [
            (lax.axis_index("gx") == groups_x - 1).astype(jnp.int32),
            (lax.axis_index("yz") == groups_y - 1).astype(jnp.int32),
        ]
    )
    fields, edge = call(
        transport_body,
        [((9, 17, 24, depth), f32), ((8, 24, depth), f32)],
        [SCALARS] + [WHOLE] * 7,
        [pltpu.VMEM((4, 19, 32, 128), f32), pltpu.VMEM((19, 32, 128), f32)],
        name="transport",
    )(last, mean, lo, hi, ylo, yhi, brick, col)
    moved_new, = call(
        blend_outer_body,
        [((bricks, 2, 128), f32)],
        [WHOLE] * 4,
        [
            pltpu.VMEM((1344, 128), f32),
            pltpu.VMEM((1344, 384), bf16),
            pltpu.VMEM((4, half, 128), f32),
        ],
        name="blend_outer",
    )(fields, edge, inner, xs)
    back = exchange(moved_new, ("gx", "yz"))

    particle_new = pl.pallas_call(
        update_body,
        out_shape=jax.ShapeDtypeStruct(phi.shape, f32),
        grid=(wx,),
        in_specs=[
            block_phi,
            block_off,
            block_count,
            pl.BlockSpec((9, 17, 24, depth), lambda i: (0, 0, 0, 0)),
        ],
        out_specs=block_phi,
        scratch_shapes=[pltpu.VMEM((9, 8, 8, 128), f32)],
        compiler_params=pltpu.CompilerParams(vmem_limit_bytes=24 * MB),
        cost_estimate=pl.CostEstimate(flops=8 * 10**7, bytes_accessed=25 * 10**6, transcendentals=0),
        name="update",
    )(phi, offset, count, fields)

    migrant_new, = call(
        functools.partial(collect_body, bricks=bricks, cap=cap),
        [((4, rows), f32)],
        [WHOLE] * 3,
        name="collect",
    )(dest, rank, back)
    return particle_new, migrant_new


def solution(mesh):
    placed = (
        P(None, None, "gx", "yz", None),
        P(None, None, "gx", "yz", None),
        P("gx", "yz", None),
        P(None, None, "gx", "yz"),
        P(None, "gx", "yz"),
        P(None, ("gx", "yz")),
        P(None, ("gx", "yz")),
        P(("gx", "yz"), None),
        P(("gx", "yz")),
    )
    return jax.shard_map(
        shards,
        mesh=mesh,
        in_specs=placed,
        out_specs=(P(None, None, "gx", "yz", None), P(None, ("gx", "yz"))),
        check_vma=False,
    )
```

profile of v0, /device:TPU:1, one launch (start us, length us, event | category | flops | bytes accessed | tf_op | source)
XLA Modules:
  0.0 151.5 jit_solution(684256749510336964)
XLA Ops:
  0.7 1.0 copy-done.5
  1.7 0.9 copy-done.6
  2.6 1.1 pencil_x.1
  3.7 7.6 %all-to-all-start.1 = ((f32[16,24,512]{2,1,0:T(8,128)}), f32[16,24,512]{2,1,0:T(8,128)S(1)}, u32[]{:S(2)}, u32[]{:S(2)}) async-start(f32[16,24,512]{2,1,0:T(8,128)} %pencil_x.1), calls=%async_computation.1 | async-start | bytes 1572864 | tf_op jit(solution)/shard_map/all_to_all | solution.py:505
  11.3 0.7 copy-done.7
  12.0 0.8 copy-done.9
  12.7 0.8 copy-done.10
  13.5 0.7 copy-done.11
  14.2 2.4 %dispatch.1 = (f32[128,4,128]{2,1,0:T(4,128)}, s32[1,2048]{1,0:T(1,128)S(1)}) custom-call(s32[1,2048]{1,0:T(1,128)S(1)} %bitcast.8, s32[1,2048]{1,0:T(1,128)S(1)} %bitcast.10, f32[4,2048]{1,0:T(4,128)S(1)} %copy-done.9, f32[3,2048]{1,0:T(4,128)S(1)} %copy-done.10), custom_call_target="tpu_custom_call" | custom-call | tf_op jit(solution)/shard_map/dispatch/pallas_call | solution.py:518
  16.6 7.9 %all-to-all-done.1.in_ref = f32[16,24,512]{2,1,0:T(8,128)S(1)} async-done(((f32[16,24,512]{2,1,0:T(8,128)}), f32[16,24,512]{2,1,0:T(8,128)S(1)}, u32[]{:S(2)}, u32[]{:S(2)}) %all-to-all-start.1) | async-done | bytes 786464 | tf_op jit(solution)/shard_map/all_to_all | solution.py:505
  24.4 8.1 %all-to-all-start = ((f32[128,4,128]{2,1,0:T(4,128)}), f32[128,4,128]{2,1,0:T(4,128)S(1)}, u32[]{:S(2)}, u32[]{:S(2)}) async-start(f32[128,4,128]{2,1,0:T(4,128)} %get-tuple-element.16), calls=%async_computation | async-start | bytes 524288 | tf_op jit(solution)/shard_map/all_to_all | solution.py:505
  32.5 1.2 pencil_y.1
  33.7 9.6 %all-to-all-done.arr_ref = f32[128,4,128]{2,1,0:T(4,128)S(1)} async-done(((f32[128,4,128]{2,1,0:T(4,128)}), f32[128,4,128]{2,1,0:T(4,128)S(1)}, u32[]{:S(2)}, u32[]{:S(2)}) %all-to-all-start) | async-done | bytes 262176 | tf_op jit(solution)/shard_map/all_to_all | solution.py:505
  43.4 4.6 %all-to-all-start.2 = ((f32[8,24,1280]{2,1,0:T(8,128)}), f32[8,24,1280]{2,1,0:T(8,128)S(1)}, u32[]{:S(2)}, u32[]{:S(2)}) async-start(f32[8,24,1280]{2,1,0:T(8,128)} %pencil_y.1), calls=%async_computation.2 | async-start | bytes 1966080 | tf_op jit(solution)/shard_map/all_to_all | solution.py:505
  48.0 3.4 %copy-done = f32[4,16,16,16,128]{4,3,2,1,0:T(8,128)S(1)} copy-done((f32[4,16,16,16,128]{4,3,2,1,0:T(8,128)S(1)}, f32[4,16,16,16,128]{4,3,2,1,0:T(8,128)}, u32[]{:S(2)}) %copy-start) | copy-done | bytes 8388632
  51.3 0.9 copy-done.3
  52.2 1.7 %local_sum.1.local_ref = f32[4,16,16,128]{3,2,1,0:T(8,128)S(1)} custom-call(f32[4,16,16,16,128]{4,3,2,1,0:T(8,128)S(1)} %copy-done, s32[16,16,128]{2,1,0:T(8,128)S(1)} %copy-done.3), custom_call_target="tpu_custom_call" | custom-call | flops 4000000 | bytes 9000000 | tf_op jit(solution)/shard_map/local_sum/pallas_call | solution.py:534
  54.0 7.0 %scatter.1 = (f32[4,16,16,128]{3,2,1,0:T(8,128)S(1)}, f32[8,64,128]{2,1,0:T(8,128)S(1)}, f32[4,1,16,128]{3,2,1,0:T(8,128)S(1)}, f32[4,2,16,128]{3,2,1,0:T(8,128)...) custom-call(f32[128,4,128]{2,1,0:T(4,128)S(1)} %all-to-all-done.arr_ref, ...), custom_call_target="tpu_custom_call" | custom-call | tf_op jit(solution)/shard_map/scatter/pallas_call | solution.py:555
  61.0 2.2 %collective-permute-start = (f32[4,1,16,128]{3,2,1,0:T(8,128)S(1)}, f32[4,1,16,128]{3,2,1,0:T(8,128)S(1)}, u32[]{:S(2)}, u32[]{:S(2)}) collective-permute-start(f32[4,1,16,128]{3,2,1,0:T(8,128)S(1)} %get-tuple-element.18), channel_id=1, source_target_pairs={{0,8},{8,16},{16,24},{24,32},{32,40},{40,48},{48,56},{56,64},{64,7... | collective-permute-start | bytes 98312 | tf_op jit(solution)/shard_map/ppermute | solution.py:501
  63.3 1.3 collective-permute-start.1
  64.7 3.6 %collective-permute-done.1.hi_ref = f32[4,2,16,128]{3,2,1,0:T(8,128)S(1)} collective-permute-done((f32[4,2,16,128]{3,2,1,0:T(8,128)S(1)}, f32[4,2,16,128]{3,2,1,0:T(8,128)S(1)}, u32[]{:S(2)}, u32[]{:S(2)}) %collective-permute-start.1) | collective-permute-done | bytes 65568 | tf_op jit(solution)/shard_map/ppermute | solution.py:501
  68.3 5.0 %collective-permute-start.2 = (f32[4,24,128]{2,1,0:T(8,128)S(1)}, f32[4,24,128]{2,1,0:T(8,128)S(1)}, u32[]{:S(2)}, u32[]{:S(2)}) collective-permute-start(f32[4,24,128]{2,1,0:T(8,128)S(1)} %get-tuple-element.22), channel_id=1, source_target_pairs={{0,1},{1,2},{2,3},{3,4},{4,5},{5,6},{6,7},{8,9},{9,10},{10,11},{11... | collective-permute-start | bytes 147464 | tf_op jit(solution)/shard_map/ppermute | solution.py:501
  73.3 1.9 %collective-permute-start.3 = (f32[2,4,24,128]{3,2,1,0:T(8,128)S(1)}, f32[2,4,24,128]{3,2,1,0:T(8,128)S(1)}, u32[]{:S(2)}, u32[]{:S(2)}) collective-permute-start(f32[2,4,24,128]{3,2,1,0:T(8,128)S(1)} %get-tuple-element.23), channel_id=1, source_target_pairs={{1,0},{2,1},{3,2},{4,3},{5,4},{6,5},{7,6},{9,8},{10,9},{11,10},{12... | collective-permute-start | bytes 294920 | tf_op jit(solution)/shard_map/ppermute | solution.py:501
  75.2 3.6 %brick.1 = (f32[4,19,16,128]{3,2,1,0:T(8,128)S(1)}, f32[4,3,24,128]{3,2,1,0:T(8,128)S(1)}) custom-call(f32[8,24,1280]{2,1,0:T(8,128)S(1)} %all-to-all-done.2.in_ref), custom_call_target="tpu_custom_call" | custom-call | tf_op jit(solution)/shard_map/brick/pallas_call | solution.py:547
  78.9 17.4 %blend_inner.1.inner_ref = f32[5,64,128]{2,1,0:T(8,128)S(1)} custom-call(f32[4,16,16,128]{3,2,1,0:T(8,128)S(1)} %get-tuple-element.17.mean_ref, f32[4,19,16,128]{3,2,1,0:T(8,128)S(1)} %get-tuple-element.24.brick_ref, f32[4,3,24,128]{3,2,1,0:T(8,128)S(1)} %get-tuple-element.25.col_ref, f32[8,64,128]{2,1,0:T(8,128)S(1)} %get-tuple-element.29.xs_ref), custom_call_target="tpu_custom_call" | custom-call | flops 8000000000 | bytes 3000000 | tf_op jit(solution)/shard_map/blend_inner/pallas_call | solution.py:572
  96.3 2.5 %transport.1 = (f32[9,17,24,128]{3,2,1,0:T(8,128)S(1)}, f32[8,24,128]{2,1,0:T(8,128)S(1)}) custom-call(s32[2]{0:T(128)S(1)} %add_convert_fusion.last_ref, f32[4,16,16,128]{3,2,1,0:T(8,128)S(1)} %get-tuple-element.17.mean_ref, f32[4,1,16,128]{3,2,1,0:T(8,128)S(1)} %collective-permute-done.lo_ref, f32[4,2,16,128]{3,2,1,0:T(8,128)S(1)} %collective-permute-done.1.hi_ref, ...), custom_call_target="tpu_custom_call" | custom-call | tf_op jit(solution)/shard_map/transport/pallas_call | solution.py:595
  98.8 18.5 %blend_outer.1 = f32[128,2,128]{2,1,0:T(2,128)} custom-call(f32[9,17,24,128]{3,2,1,0:T(8,128)S(1)} %get-tuple-element.26.f_ref, f32[8,24,128]{2,1,0:T(8,128)S(1)} %get-tuple-element.28.tcol_ref, f32[5,64,128]{2,1,0:T(8,128)S(1)} %blend_inner.1.inner_ref, f32[8,64,128]{2,1,0:T(8,128)S(1)} %get-tuple-element.29.xs_ref), custom_call_target="tpu_custom_call" | custom-call | tf_op jit(solution)/shard_map/blend_outer/pallas_call | solution.py:602
  117.3 10.1 %all-to-all-start.3 = ((f32[128,2,128]{2,1,0:T(2,128)}), f32[128,2,128]{2,1,0:T(2,128)S(1)}, u32[]{:S(2)}, u32[]{:S(2)}) async-start(f32[128,2,128]{2,1,0:T(2,128)} %blend_outer.1), calls=%async_computation.3 | async-start | bytes 262144 | tf_op jit(solution)/shard_map/all_to_all | solution.py:505
  127.4 3.4 %copy-done.1 = f32[4,16,16,16,128]{4,3,2,1,0:T(8,128)S(1)} copy-done((f32[4,16,16,16,128]{4,3,2,1,0:T(8,128)S(1)}, f32[4,16,16,16,128]{4,3,2,1,0:T(8,128)}, u32[]{:S(2)}) %copy-start.1) | copy-done | bytes 8388632
  130.8 2.8 %copy-done.2 = f32[3,16,16,16,128]{4,3,2,1,0:T(8,128)S(1)} copy-done((f32[3,16,16,16,128]{4,3,2,1,0:T(8,128)S(1)}, f32[3,16,16,16,128]{4,3,2,1,0:T(8,128)}, u32[]{:S(2)}) %copy-start.2) | copy-done | bytes 6291480
  133.6 16.7 %update.1 = f32[4,16,16,16,128]{4,3,2,1,0:T(8,128)} custom-call(f32[4,16,16,16,128]{4,3,2,1,0:T(8,128)S(1)} %copy-done.1, f32[3,16,16,16,128]{4,3,2,1,0:T(8,128)S(1)} %copy-done.2, s32[16,16,128]{2,1,0:T(8,128)S(1)} %copy-done.4, f32[9,17,24,128]{3,2,1,0:T(8,128)S(1)} %get-tuple-element.26.f_ref), custom_call_target="tpu_custom_call" | custom-call | flops 80000000 | bytes 25000000 | tf_op jit(solution)/shard_map/update/pallas_call | solution.py:615
  150.2 1.2 collect.1
  (21 shorter events, 0.1 us)
Async XLA Ops:
  0.6 53.3 %copy-start.4 = (s32[16,16,128]{2,1,0:T(8,128)S(1)}, s32[16,16,128]{2,1,0:T(8,128)}, u32[]{:S(2)}) copy-start(s32[16,16,128]{2,1,0:T(8,128)} %count_ref.5) | copy-start | bytes 393220
  0.6 1.0 copy-start.5
  1.7 0.9 copy-start.6
  3.7 20.8 %all-to-all-start.1 = ((f32[16,24,512]{2,1,0:T(8,128)}), f32[16,24,512]{2,1,0:T(8,128)S(1)}, u32[]{:S(2)}, u32[]{:S(2)}) async-start(f32[16,24,512]{2,1,0:T(8,128)} %pencil_x.1), calls=%async_computation.1 | async-start | bytes 1572864 | tf_op jit(solution)/shard_map/all_to_all | solution.py:505
  11.3 0.7 copy-start.7
  12.0 0.8 copy-start.9
  12.7 0.8 copy-start.10
  13.5 0.7 copy-start.11
  24.4 18.9 %all-to-all-start = ((f32[128,4,128]{2,1,0:T(4,128)}), f32[128,4,128]{2,1,0:T(4,128)S(1)}, u32[]{:S(2)}, u32[]{:S(2)}) async-start(f32[128,4,128]{2,1,0:T(4,128)} %get-tuple-element.16), calls=%async_computation | async-start | bytes 524288 | tf_op jit(solution)/shard_map/all_to_all | solution.py:505
  43.4 31.8 %all-to-all-start.2 = ((f32[8,24,1280]{2,1,0:T(8,128)}), f32[8,24,1280]{2,1,0:T(8,128)S(1)}, u32[]{:S(2)}, u32[]{:S(2)}) async-start(f32[8,24,1280]{2,1,0:T(8,128)} %pencil_y.1), calls=%async_computation.2 | async-start | bytes 1966080 | tf_op jit(solution)/shard_map/all_to_all | solution.py:505
  48.0 3.4 %copy-start = (f32[4,16,16,16,128]{4,3,2,1,0:T(8,128)S(1)}, f32[4,16,16,16,128]{4,3,2,1,0:T(8,128)}, u32[]{:S(2)}) copy-start(f32[4,16,16,16,128]{4,3,2,1,0:T(8,128)} %phi_ref.5) | copy-start | bytes 25165828
  51.3 0.9 copy-start.3
  61.0 3.6 %collective-permute-start = (f32[4,1,16,128]{3,2,1,0:T(8,128)S(1)}, f32[4,1,16,128]{3,2,1,0:T(8,128)S(1)}, u32[]{:S(2)}, u32[]{:S(2)}) collective-permute-start(f32[4,1,16,128]{3,2,1,0:T(8,128)S(1)} %get-tuple-element.18), channel_id=1, source_target_pairs={{0,8},{8,16},{16,24},{24,32},{32,40},{40,48},{48,56},{56,64},{64,7... | collective-permute-start | bytes 98312 | tf_op jit(solution)/shard_map/ppermute | solution.py:501
  63.3 5.0 %collective-permute-start.1 = (f32[4,2,16,128]{3,2,1,0:T(8,128)S(1)}, f32[4,2,16,128]{3,2,1,0:T(8,128)S(1)}, u32[]{:S(2)}, u32[]{:S(2)}) collective-permute-start(f32[4,2,16,128]{3,2,1,0:T(8,128)S(1)} %get-tuple-element.19), channel_id=1, source_target_pairs={{8,0},{16,8},{24,16},{32,24},{40,32},{48,40},{56,48},{64,56},{72,6... | collective-permute-start | bytes 196616 | tf_op jit(solution)/shard_map/ppermute | solution.py:501
  68.3 28.0 %collective-permute-start.2 = (f32[4,24,128]{2,1,0:T(8,128)S(1)}, f32[4,24,128]{2,1,0:T(8,128)S(1)}, u32[]{:S(2)}, u32[]{:S(2)}) collective-permute-start(f32[4,24,128]{2,1,0:T(8,128)S(1)} %get-tuple-element.22), channel_id=1, source_target_pairs={{0,1},{1,2},{2,3},{3,4},{4,5},{5,6},{6,7},{8,9},{9,10},{10,11},{11... | collective-permute-start | bytes 147464 | tf_op jit(solution)/shard_map/ppermute | solution.py:501
  73.3 23.0 %collective-permute-start.3 = (f32[2,4,24,128]{3,2,1,0:T(8,128)S(1)}, f32[2,4,24,128]{3,2,1,0:T(8,128)S(1)}, u32[]{:S(2)}, u32[]{:S(2)}) collective-permute-start(f32[2,4,24,128]{3,2,1,0:T(8,128)S(1)} %get-tuple-element.23), channel_id=1, source_target_pairs={{1,0},{2,1},{3,2},{4,3},{5,4},{6,5},{7,6},{9,8},{10,9},{11,10},{12... | collective-permute-start | bytes 294920 | tf_op jit(solution)/shard_map/ppermute | solution.py:501
  117.3 33.0 %all-to-all-start.3 = ((f32[128,2,128]{2,1,0:T(2,128)}), f32[128,2,128]{2,1,0:T(2,128)S(1)}, u32[]{:S(2)}, u32[]{:S(2)}) async-start(f32[128,2,128]{2,1,0:T(2,128)} %blend_outer.1), calls=%async_computation.3 | async-start | bytes 262144 | tf_op jit(solution)/shard_map/all_to_all | solution.py:505
  127.4 3.4 %copy-start.1 = (f32[4,16,16,16,128]{4,3,2,1,0:T(8,128)S(1)}, f32[4,16,16,16,128]{4,3,2,1,0:T(8,128)}, u32[]{:S(2)}) copy-start(f32[4,16,16,16,128]{4,3,2,1,0:T(8,128)} %phi_ref.5) | copy-start | bytes 25165828
  130.8 2.8 %copy-start.2 = (f32[3,16,16,16,128]{4,3,2,1,0:T(8,128)S(1)}, f32[3,16,16,16,128]{4,3,2,1,0:T(8,128)}, u32[]{:S(2)}) copy-start(f32[3,16,16,16,128]{4,3,2,1,0:T(8,128)} %off_ref.3) | copy-start | bytes 18874372
  133.6 16.7 %copy-start.8 = (s32[2048,1]{0,1:T(1,128)S(1)}, s32[2048,1]{0,1:T(1,128)}, u32[]{:S(2)}) copy-start(s32[2048,1]{0,1:T(1,128)} %param.16) | copy-start | bytes 24580
where the time goes:
time: 152 us; the launch traced here: 151 us
  Pallas kernels  73.4 us (48%)
  starting transfers between devices  40.8 us (27%)
  waiting for transfers between devices  21.1 us (14%)
  local copies, waits for them, and re-layouts  15.3 us (10%)
    all_to_all x4, starting transfers between devices, exchange(): return lax.all_to_all(value, axis, split_axis=0, concat_axis=0, tiled=True)  30.3 us
    pallas_call x1, Pallas kernels, shards(): call(blend_outer_body, [((bricks, 2, 128), f32)], [WHOLE] * 4, [pltpu.VME...  18.5 us
    all_to_all x4, waiting for transfers between devices, exchange(): return lax.all_to_all(value, axis, split_axis=0, concat_axis=0, tiled=True)  17.5 us
    pallas_call x1, Pallas kernels, shards(): call(blend_inner_body, [((5, half, 128), f32)], [WHOLE] * 4, [pltpu.VMEM(...  17.4 us
    pallas_call x1, Pallas kernels, shards(): pl.pallas_call(update_body, out_shape=jax.ShapeDtypeStruct(phi.shape, f32...  16.7 us
    unnamed x24, local copies, waits for them, and re-layouts  15.3 us
    ppermute x4, starting transfers between devices, shifted(): return lax.ppermute(value, axis, pairs)  10.4 us
    pallas_call x1, Pallas kernels, shards(): call(scatter_body, [((4, wx, wy, depth), f32), ((8, half, 128), f32), ((4...  7.04 us
  transfers between devices with their start and end apart: 8, of which 3 were waited for; matrix products, arithmetic and copies ran while one was open for 0% of the time, Pallas kernels for 33%

commit v1 on v0

--- a/solution.py
+++ b/solution.py
@@ -9,6 +9,7 @@
 
 time_step = 0.08
 mix_coeff = 0.5
+span = 8
 f32 = jnp.float32
 bf16 = jnp.bfloat16
 MB = 2**20
@@ -31,6 +32,20 @@
 
 def dot_nn(left, right):
     return lax.dot_general(left, right, (((1,), (0,)), ((), ())), preferred_element_type=f32)
+
+
+def places(number, width):
+    return iota((number, width), 0).astype(f32).astype(bf16)
+
+
+def tall(row, number):
+    part = jnp.broadcast_to(row, (16, row.shape[1])).astype(bf16)
+    return jnp.concatenate([part] * (number // 16), axis=0)
+
+
+def marked(spots, row):
+    one, none = jnp.ones((), bf16), jnp.zeros((), bf16)
+    return jnp.where(spots == tall(row, spots.shape[0]), one, none)
 
 
 def call(body, outs, specs, scratch=(), vmem=48, cost=None, name=None):
@@ -49,16 +64,15 @@
 def dispatch_body(dest_ref, cell_ref, phi_ref, off_ref, out_ref, rank_ref, *, bricks, cap):
     rows = dest_ref.shape[1]
     hot = jnp.where(iota((bricks, rows), 0) == dest_ref[...], 1.0, 0.0).astype(bf16)
+    key = cell_ref[...] * rows + iota((1, rows), 1)
+    key_down = jnp.broadcast_to(key, (8, rows)).T[:, 0:1]
     step = 256
-    before = jnp.where(iota((step, step), 0) < iota((step, step), 1), 1.0, 0.0).astype(bf16)
-    carry = jnp.zeros((bricks, 1), f32)
     ranks = []
     for b in range(rows // step):
-        part = hot[:, b * step : (b + 1) * step]
-        wide = part.astype(f32)
-        count = dot_nn(part, before) + carry
-        ranks.append(jnp.sum(wide * count, axis=0, keepdims=True))
-        carry = carry + jnp.sum(wide, axis=1, keepdims=True)
+        cut = slice(b * step, (b + 1) * step)
+        before = jnp.where(key_down < key[:, cut], 1.0, 0.0).astype(bf16)
+        count = dot_nn(hot, before)
+        ranks.append(jnp.sum(hot[:, cut].astype(f32) * count, axis=0, keepdims=True))
     rank = jnp.concatenate(ranks, axis=1).astype(jnp.int32)
     rank_ref[...] = rank
     here = iota((cap, rows), 0) == rank
@@ -92,49 +106,52 @@
 
 
 def local_body(phi_ref, count_ref, out_ref):
-    count = count_ref[0]
-    for c in range(4):
-        total = None
-        for s in range(phi_ref.shape[1]):
-            value = jnp.where(count > s, phi_ref[c, s, 0], 0.0)
-            total = value if total is None else total + value
-        out_ref[c, 0] = total
+    for x in range(count_ref.shape[0]):
+        count = count_ref[x]
+        for c in range(4):
+            total = None
+            for s in range(phi_ref.shape[1]):
+                value = jnp.where(count > s, phi_ref[c, s, x], 0.0)
+                total = value if total is None else total + value
+            out_ref[c, x] = total
 
 
 def scatter_body(
-    arr_ref, local_ref, count_ref, mean_ref, xs_ref, ehi_ref, elo_ref, e15_ref, e01_ref, acc_ref
+    arr_ref, local_ref, count_ref, mean_ref, xs_ref, bound_ref, ehi_ref, elo_ref, e15_ref, e01_ref, acc_ref
 ):
-    half = arr_ref.shape[0] // 2
-    lane = iota((half, 128), 1)
+    half = xs_ref.shape[1]
     for r in range(4):
-        low = arr_ref[0:half, r, :]
-        high = arr_ref[half : 2 * half, r, :]
-        xs_ref[2 * r] = jnp.where(lane < 64, low, pltpu.roll(high, 64, 1))
-        xs_ref[2 * r + 1] = jnp.where(lane < 64, pltpu.roll(low, 64, 1), high)
+        turned = arr_ref[:, r, :].T
+        xs_ref[2 * r] = turned[0:half]
+        xs_ref[2 * r + 1] = turned[half : 2 * half]
+    code = arr_ref[:, 3, :].astype(jnp.int32) - 1
+    line = code >> 11
+    bound_ref[0:1, :] = jnp.min(jnp.where(code >= 0, line, 16), axis=0, keepdims=True)
+    bound_ref[1:2, :] = jnp.max(jnp.where(code >= 0, line, -1), axis=0, keepdims=True)
     acc_ref[...] = jnp.zeros_like(acc_ref)
+    spots = places(256, 128)
 
     def step(i, carry):
-        at = pl.multiple_of(i * 8, 8)
-        cell = xs_ref[7, pl.ds(at, 8), :].astype(jnp.int32) - 1
-        plane = cell >> 7
-        depth = cell & 127
-        parts = [split(xs_ref[c, pl.ds(at, 8), :]) for c in range(4)]
+        at = pl.multiple_of(i * 16, 16)
+        cell = xs_ref[7, pl.ds(at, 16), :].astype(jnp.int32) - 1
+        plane = (cell >> 7).astype(f32)
+        depth = (cell & 127).astype(f32)
+        parts = [split(xs_ref[c, pl.ds(at, 16), :]) for c in range(4)]
         lefts, rights = [], []
-        for u in range(8):
-            at_z = iota((128, 128), 0) == depth[u : u + 1]
-            at_p = iota((256, 128), 0) == plane[u : u + 1]
-            rights.append(jnp.where(at_p, 1.0, 0.0).astype(bf16))
-            blocks = [jnp.where(at_z, 1.0, 0.0).astype(bf16)]
+        for u in range(16):
+            rights.append(marked(spots, plane[u : u + 1]))
+            at_z = marked(spots[0:128], depth[u : u + 1])
+            pieces = [at_z]
             for top, rest in parts:
-                blocks.append(jnp.where(at_z, top[u : u + 1], 0.0).astype(bf16))
-                blocks.append(jnp.where(at_z, rest[u : u + 1], 0.0).astype(bf16))
-            lefts.append(jnp.concatenate(blocks, axis=0))
+                pieces.append(at_z * tall(top[u : u + 1], 128))
+                pieces.append(at_z * tall(rest[u : u + 1], 128))
+            lefts.append(jnp.concatenate(pieces, axis=0))
         acc_ref[...] += dot_nt(
             jnp.concatenate(lefts, axis=1), jnp.concatenate(rights, axis=1)
         )
         return carry
 
-    lax.fori_loop(0, half // 8, step, 0)
+    lax.fori_loop(0, half // 16, step, 0)
     wx, wy = count_ref.shape[0], count_ref.shape[1]
     number = acc_ref[0:128, :].T.reshape(wx, wy, 128)
     share = 1.0 / (count_ref[...].astype(f32) + number)
@@ -272,10 +289,17 @@
     return jnp.where(spot == at, 1.0 - frac, 0.0) + jnp.where(spot == at + 1, frac, 0.0)
 
 
-def depth_weights(depth, frac):
-    top, rest = split(hat(128, depth, frac))
-    top = top.astype(bf16)
-    return jnp.concatenate([top, top, rest.astype(bf16)], axis=0)
+def depth_weights(spots, depth, frac):
+    at = depth.astype(f32)
+    here = spots == tall(at, 128)
+    above = spots == tall(at + 1.0, 128)
+    none = jnp.zeros((), bf16)
+    parts = []
+    for low, high in zip(split(1.0 - frac), split(frac)):
+        parts.append(
+            jnp.where(here, tall(low, 128), jnp.where(above, tall(high, 128), none))
+        )
+    return jnp.concatenate([parts[0], parts[0], parts[1]], axis=0)
 
 
 def widen(tab_ref, lhs_ref):
@@ -290,40 +314,78 @@
     return jnp.sum(value, axis=0, keepdims=True)
 
 
-def blend_inner_body(mean_ref, brick_ref, col_ref, xs_ref, out_ref, tab_ref, lhs_ref):
+def tile_terms(spots, xs_ref, bound_ref, i):
+    row, x, y, depth = slot_terms(xs_ref, 2 * i)
+    half = xs_ref.shape[1]
+    low = jnp.minimum(bound_ref[0, half + 2 * i], bound_ref[0, half + 2 * i + 1])
+    high = jnp.maximum(bound_ref[1, half + 2 * i], bound_ref[1, half + 2 * i + 1])
+    windows = (high + 1 - low + span) >> 3
+    rows_z = depth_weights(spots, depth, row(6))
+    wy = hat(24, y, row(5))
+    return row, x, low, windows, rows_z, wy
+
+
+def window_sums(lhs_ref, per, blocks, low, x, frac, rows_z, wy, sums):
+    at = pl.multiple_of(low * per, 16)
+    along = dot_nn(lhs_ref[pl.ds(at, span * per), :], rows_z)
+    wx = hat(span, x - low, frac)
+    sums = list(sums)
+    for k in range(span):
+        inside = wx[k : k + 1] * wy[0:16]
+        for n in range(blocks):
+            sums[n] = sums[n] + along[per * k + 16 * n : per * k + 16 * n + 16] * inside
+        if len(sums) > blocks:
+            rim = wx[k : k + 1] * wy[16:17]
+            sums[blocks] = sums[blocks] + along[per * k + 16 * blocks : per * (k + 1)] * rim
+    return tuple(sums)
+
+
+def blend_tiles(lhs_ref, per, blocks, xs_ref, bound_ref, tiles, finish):
+    spots = places(128, 256)
+
+    def group(g, carry):
+        held = []
+        for e in range(tiles):
+            i = g * tiles + e
+            row, x, low, windows, rows_z, wy = tile_terms(spots, xs_ref, bound_ref, i)
+            zero = tuple(jnp.zeros((16, 256), f32) for _ in range(per // 16))
+            sums = window_sums(lhs_ref, per, blocks, low, x, row(4), rows_z, wy, zero)
+            held.append((i, row, x, low, windows, rows_z, wy, sums))
+        for i, row, x, low, windows, rows_z, wy, sums in held:
+
+            def more(w, now):
+                return window_sums(
+                    lhs_ref, per, blocks, low + span * w, x, row(4), rows_z, wy, now
+                )
+
+            finish(i, row, lax.fori_loop(1, windows, more, sums))
+        return carry
+
+    lax.fori_loop(0, xs_ref.shape[1] // (2 * tiles), group, 0)
+
+
+def keep_row(ref, c, i, value):
+    for e in (0, 1):
+        ref[c, pl.ds(2 * i + e, 1), :] = value[:, 128 * e : 128 * e + 128]
+
+
+def blend_inner_body(bound_ref, mean_ref, hi_ref, xs_ref, out_ref, tab_ref, lhs_ref):
     for c in range(4):
-        tab_ref[256 * c : 256 * c + 256, :] = mean_ref[c].reshape(256, 128)
-    tab_ref[1024:1280, :] = brick_ref[3, 0:16].reshape(256, 128)
-    tab_ref[1280:1296, :] = brick_ref[3, 16]
-    tab_ref[1296:1320, :] = col_ref[3, 0]
-    tab_ref[1320:1328, :] = jnp.zeros((8, 128), f32)
+        for x in range(16):
+            tab_ref[64 * x + 16 * c : 64 * x + 16 * c + 16, :] = mean_ref[c, x]
+        tab_ref[1024 + 16 * c : 1040 + 16 * c, :] = hi_ref[c, 0]
+    tab_ref[1088:, :] = jnp.zeros((64 * (span - 1), 128), f32)
     widen(tab_ref, lhs_ref)
 
-    def step(i, carry):
-        row, x, y, depth = slot_terms(xs_ref, 2 * i)
-        along = dot_nn(lhs_ref[...], depth_weights(depth, row(6)))
-        wx = hat(24, x, row(4))
-        wy = hat(24, y, row(5))
-        sums = [None] * 5
-        for k in range(16):
-            weight = wx[k : k + 1] * wy[0:16]
-            for c in range(5):
-                at = 256 * c + 16 * k
-                term = along[at : at + 16] * weight
-                sums[c] = term if sums[c] is None else sums[c] + term
-        sums[4] = sums[4] + along[1280:1296] * (wx[16:17] * wy[0:16])
-        got = [total_y(value) for value in sums]
-        got[4] = got[4] + total_y(along[1296:1320] * (wx * wy[16:17]))
-        for c in range(5):
-            for e in (0, 1):
-                out_ref[c, pl.ds(2 * i + e, 1), :] = got[c][:, 128 * e : 128 * e + 128]
-        return carry
-
-    lax.fori_loop(0, xs_ref.shape[1] // 2, step, 0)
+    def finish(i, row, sums):
+        for c in range(4):
+            keep_row(out_ref, c, i, total_y(sums[c]))
+
+    blend_tiles(lhs_ref, 64, 4, xs_ref, bound_ref, 8, finish)
 
 
 def transport_body(
-    last_ref, mean_ref, lo_ref, hi_ref, ylo_ref, yhi_ref, brick_ref, col_ref, f_ref, tcol_ref, mp_ref, gp_ref
+    last_ref, mean_ref, lo_ref, hi_ref, ylo_ref, yhi_ref, brick_ref, col_ref, f_ref, rise_ref, mp_ref, gp_ref
 ):
     x_in = jnp.where(last_ref[0] == 1, 0.0, 1.0).astype(f32)
     y_in = jnp.where(last_ref[1] == 1, 0.0, 1.0).astype(f32)
@@ -355,9 +417,13 @@
                 (z_shift(centre, True), z_shift(centre, False)),
             ]
             sides = [(m[0], g[0], m[1], g[1]) for m, g in zip(means, gammas)]
+            moved = flux(centre, gamma, sides, velocity) * keep
             f_ref[c, x, 0:16, :] = centre
-            f_ref[4 + c, x, 0:16, :] = flux(centre, gamma, sides, velocity) * keep
+            f_ref[4 + c, x, 0:16, :] = moved
+            rise_ref[c, x, 0:16, :] = means[2][0] - centre
+            rise_ref[4 + c, x, 0:16, :] = z_shift(moved, True) - moved
         f_ref[8, x, 0:16, :] = gamma
+        rise_ref[8, x, 0:16, :] = gammas[2][0] - gamma
         return carry
 
     lax.fori_loop(0, 17, plane, 0)
@@ -388,91 +454,67 @@
         ]
         sides = [(m[0], g[0], m[1], g[1]) for m, g in zip(means, gammas)]
         moved = flux(centre, gamma, sides, velocity) * keep
-        tcol_ref[c] = centre
-        tcol_ref[4 + c] = moved
         f_ref[c, :, 16, :] = centre[0:17]
         f_ref[4 + c, :, 16, :] = moved[0:17]
+        rise_ref[c, :, 16, :] = (means[2][0] - centre)[0:17]
+        rise_ref[4 + c, :, 16, :] = (z_shift(moved, True) - moved)[0:17]
     f_ref[8, :, 16, :] = gamma[0:17]
-
-
-def blend_outer_body(f_ref, tcol_ref, inner_ref, xs_ref, out_ref, tab_ref, lhs_ref, new_ref):
-    for c in range(4):
-        tab_ref[256 * c : 256 * c + 256, :] = f_ref[4 + c, 0:16, 0:16, :].reshape(256, 128)
-    for c in range(8):
-        tab_ref[1024 + 16 * c : 1040 + 16 * c, :] = f_ref[c, 16, 0:16, :]
-        tab_ref[1152 + 24 * c : 1176 + 24 * c, :] = tcol_ref[c]
+    rise_ref[8, :, 16, :] = (gammas[2][0] - gamma)[0:17]
+
+
+def blend_outer_body(bound_ref, f_ref, inner_ref, xs_ref, out_ref, tab_ref, lhs_ref, new_ref):
+    for x in range(17):
+        for c in range(5):
+            tab_ref[96 * x + 16 * c : 96 * x + 16 * c + 16, :] = f_ref[4 + c, x, 0:16, :]
+        tab_ref[96 * x + 80 : 96 * x + 96, :] = jnp.concatenate(
+            [f_ref[c, x, 16:17, :] for c in range(9)] + [jnp.zeros((7, 128), f32)], axis=0
+        )
+    tab_ref[96 * 17 :, :] = jnp.zeros((96 * (span - 1), 128), f32)
     widen(tab_ref, lhs_ref)
 
-    def step(i, carry):
-        row, x, y, depth = slot_terms(xs_ref, 2 * i)
-        along = dot_nn(lhs_ref[...], depth_weights(depth, row(6)))
-        wx = hat(24, x, row(4))
-        wy = hat(24, y, row(5))
-        sums = [None] * 4
-        for k in range(16):
-            weight = wx[k : k + 1] * wy[0:16]
-            for c in range(4):
-                at = 256 * c + 16 * k
-                term = along[at : at + 16] * weight
-                sums[c] = term if sums[c] is None else sums[c] + term
-        top = wx[16:17] * wy[0:16]
-        side = wx * wy[16:17]
-        got = []
-        for c in range(8):
-            value = total_y(along[1024 + 16 * c : 1040 + 16 * c] * top)
-            value = value + total_y(along[1152 + 24 * c : 1176 + 24 * c] * side)
-            if c >= 4:
-                value = value + total_y(sums[c - 4])
-            got.append(value)
-
+    def finish(i, row, sums):
         def inner(c):
             return jnp.concatenate([inner_ref[c, pl.ds(2 * i + e, 1), :] for e in (0, 1)], axis=1)
 
-        rate = mix_coeff * inner(4)
+        rim = sums[5]
+        rate = mix_coeff * (total_y(sums[4]) + rim[8:9])
         for c in range(4):
             phi = row(c)
-            fresh = phi + got[4 + c] - rate * (phi - (got[c] + inner(c)))
-            for e in (0, 1):
-                new_ref[c, pl.ds(2 * i + e, 1), :] = fresh[:, 128 * e : 128 * e + 128]
-        return carry
-
+            mean = inner(c) + rim[c : c + 1]
+            moved = total_y(sums[c]) + rim[4 + c : 5 + c]
+            keep_row(new_ref, c, i, phi + moved - rate * (phi - mean))
+
+    blend_tiles(lhs_ref, 96, 5, xs_ref, bound_ref, 8, finish)
     half = xs_ref.shape[1]
-    lax.fori_loop(0, half // 2, step, 0)
-    lane = iota((half, 128), 1)
     for r in range(2):
-        low, high = new_ref[2 * r], new_ref[2 * r + 1]
-        out_ref[0:half, r, :] = jnp.where(lane < 64, low, pltpu.roll(high, 64, 1))
-        out_ref[half : 2 * half, r, :] = jnp.where(lane < 64, pltpu.roll(low, 64, 1), high)
-
-
-def update_body(phi_ref, off_ref, count_ref, f_ref, out_ref, coef_ref):
-    x = pl.program_id(0)
+        both = jnp.concatenate([new_ref[2 * r], new_ref[2 * r + 1]], axis=0)
+        out_ref[:, r, :] = both.T
+
+
+def update_body(phi_ref, off_ref, count_ref, f_ref, rise_ref, out_ref, coef_ref):
+    deep, wy = count_ref.shape[0], count_ref.shape[1]
+    first = pl.program_id(0) * deep
     slots = phi_ref.shape[1]
-    for yt in (0, 8):
+    width = 4
+    for x in range(deep):
         for ch in range(9):
-            corner = {}
-            for sx in (0, 1):
-                for sy in (0, 1):
-                    value = f_ref[ch, x + sx, yt + sy : yt + sy + 8, :]
-                    corner[sx, sy, 0] = value
-                    corner[sx, sy, 1] = z_shift(value, True) - value
-            for sz in (0, 1):
-                c00, c01 = corner[0, 0, sz], corner[0, 1, sz]
-                c10, c11 = corner[1, 0, sz], corner[1, 1, sz]
+            for sz, ref in enumerate((f_ref, rise_ref)):
+                c00 = ref[ch, first + x, 0:wy, :]
+                c01 = ref[ch, first + x, 1 : wy + 1, :]
+                c10 = ref[ch, first + x + 1, 0:wy, :]
+                c11 = ref[ch, first + x + 1, 1 : wy + 1, :]
                 dx = c10 - c00
                 coef_ref[ch, sz] = c00
                 coef_ref[ch, 2 + sz] = c01 - c00
                 coef_ref[ch, 4 + sz] = dx
                 coef_ref[ch, 6 + sz] = (c11 - c01) - dx
-        count = count_ref[0, yt : yt + 8, :]
-        rows = slice(yt, yt + 8)
-        width = 4
+        count = count_ref[x]
 
         def group(i, carry):
             at = [i * width + s for s in range(width)]
-            a = [off_ref[0, s, 0, rows, :] for s in at]
-            b = [off_ref[1, s, 0, rows, :] for s in at]
-            d = [off_ref[2, s, 0, rows, :] for s in at]
+            a = [off_ref[0, s, x] for s in at]
+            b = [off_ref[1, s, x] for s in at]
+            d = [off_ref[2, s, x] for s in at]
 
             def blend(ch):
                 k = [coef_ref[ch, n] for n in range(8)]
@@ -487,9 +529,9 @@
                 mean = blend(c)
                 moved = blend(4 + c)
                 for n in range(width):
-                    phi = phi_ref[c, at[n], 0, rows, :]
+                    phi = phi_ref[c, at[n], x]
                     fresh = phi + moved[n] - rate[n] * (phi - mean[n])
-                    out_ref[c, at[n], 0, rows, :] = jnp.where(count > at[n], fresh, 0.0)
+                    out_ref[c, at[n], x] = jnp.where(count > at[n], fresh, 0.0)
             return carry
 
         lax.fori_loop(0, slots // width, group, 0)
@@ -511,7 +553,6 @@
     bricks = groups_x * groups_y
     rows = m_phi.shape[1]
     cap = 4 * rows // bricks
-    half = bricks // 2
 
     dest = m_dest.reshape(1, rows)
     cell = m_cell.reshape(1, rows)
@@ -519,44 +560,39 @@
         functools.partial(dispatch_body, bricks=bricks, cap=cap),
         [((bricks, 4, 128), f32), ((1, rows), jnp.int32)],
         [WHOLE] * 4,
+        vmem=60,
         name="dispatch",
     )(dest, cell, m_phi, m_offset)
+    arrived = exchange(sent, ("gx", "yz"))
 
     pencil, = call(
-        pencil_x_body, [((groups_x, 24, 512), f32)], [WHOLE] * 2, name="pencil_x"
+        pencil_x_body, [((groups_x, 24, 512), f32)], [WHOLE] * 2, vmem=8, name="pencil_x"
     )(jnp.transpose(velocity, (0, 2, 3, 1)), jnp.transpose(diffusivity, (1, 2, 0)))
-    pencil = exchange(pencil, "gx")
-    arrived = exchange(sent, ("gx", "yz"))
-
-    block_phi = pl.BlockSpec((4, slots, 1, wy, depth), lambda i: (0, 0, i, 0, 0))
-    block_off = pl.BlockSpec((3, slots, 1, wy, depth), lambda i: (0, 0, i, 0, 0))
-    block_count = pl.BlockSpec((1, wy, depth), lambda i: (i, 0, 0))
+    def blocks(first, deep):
+        return pl.BlockSpec((first, slots, deep, wy, depth), lambda i: (0, 0, i, 0, 0))
+
+    def cells(deep):
+        return pl.BlockSpec((deep, wy, depth), lambda i: (i, 0, 0))
+
     local_sum = pl.pallas_call(
         local_body,
         out_shape=jax.ShapeDtypeStruct((4, wx, wy, depth), f32),
-        grid=(wx,),
-        in_specs=[block_phi, block_count],
-        out_specs=pl.BlockSpec((4, 1, wy, depth), lambda i: (0, i, 0, 0)),
-        compiler_params=pltpu.CompilerParams(vmem_limit_bytes=16 * MB),
+        grid=(wx // 8,),
+        in_specs=[blocks(4, 8), cells(8)],
+        out_specs=pl.BlockSpec((4, 8, wy, depth), lambda i: (0, i, 0, 0)),
+        compiler_params=pltpu.CompilerParams(vmem_limit_bytes=60 * MB),
         cost_estimate=pl.CostEstimate(flops=4 * 10**6, bytes_accessed=9 * 10**6, transcendentals=0),
         name="local_sum",
     )(phi, count)
 
-    wide, = call(pencil_y_body, [((groups_y, 24, 1280), f32)], [WHOLE], name="pencil_y")(pencil)
-    wide = exchange(wide, "yz")
-    brick, col = call(
-        brick_body,
-        [((4, 19, wy, depth), f32), ((4, 3, 24, depth), f32)],
-        [WHOLE],
-        [pltpu.VMEM((4 * 16 * 24, 128), f32)],
-        name="brick",
-    )(wide)
-
-    mean, xs, ehi, elo, e15, e01 = call(
+    arrived, local_sum, pencil = lax.optimization_barrier((arrived, local_sum, pencil))
+    pencil = exchange(pencil, "gx")
+    mean, xs, bound, ehi, elo, e15, e01 = call(
         scatter_body,
         [
             ((4, wx, wy, depth), f32),
-            ((8, half, 128), f32),
+            ((8, cap, 128), f32),
+            ((2, 128), jnp.int32),
             ((4, 1, wy, depth), f32),
             ((4, 2, wy, depth), f32),
             ((4, wx, depth), f32),
@@ -564,27 +600,45 @@
         ],
         [WHOLE] * 3,
         [pltpu.VMEM((9 * 128, 256), f32)],
+        vmem=16,
+        cost=pl.CostEstimate(flops=4 * 10**9, bytes_accessed=2 * 10**6, transcendentals=0),
         name="scatter",
     )(arrived, local_sum, count)
 
+    pencil, xs = lax.optimization_barrier((pencil, xs))
     lo = shifted(ehi, "gx", 1)
     hi = shifted(elo, "gx", -1)
-    inner, = call(
-        blend_inner_body,
-        [((5, half, 128), f32)],
-        [WHOLE] * 4,
-        [pltpu.VMEM((1328, 128), f32), pltpu.VMEM((1328, 384), bf16)],
-        cost=pl.CostEstimate(flops=8 * 10**9, bytes_accessed=3 * 10**6, transcendentals=0),
-        name="blend_inner",
-    )(mean, brick, col, xs)
+    wide, = call(
+        pencil_y_body, [((groups_y, 24, 1280), f32)], [WHOLE], vmem=8, name="pencil_y"
+    )(pencil)
     up, down = call(
         edge_body,
         [((4, 24, depth), f32), ((2, 4, 24, depth), f32)],
         [WHOLE] * 4,
+        vmem=4,
         name="edge",
     )(lo, hi, e15, e01)
     ylo = shifted(up, "yz", 1)
     yhi = shifted(down, "yz", -1)
+    wide = exchange(wide, "yz")
+    inner, = call(
+        blend_inner_body,
+        [((4, cap, 128), f32)],
+        [SCALARS] + [WHOLE] * 3,
+        [pltpu.VMEM((1536, 128), f32), pltpu.VMEM((1536, 384), bf16)],
+        vmem=16,
+        cost=pl.CostEstimate(flops=8 * 10**9, bytes_accessed=3 * 10**6, transcendentals=0),
+        name="blend_inner",
+    )(bound, mean, hi, xs)
+    wide, inner = lax.optimization_barrier((wide, inner))
+    brick, col = call(
+        brick_body,
+        [((4, 19, wy, depth), f32), ((4, 3, 24, depth), f32)],
+        [WHOLE],
+        [pltpu.VMEM((4 * 16 * 24, 128), f32)],
+        vmem=8,
+        name="brick",
+    )(wide)
 
     last = jnp.stack(
         [
@@ -592,47 +646,46 @@
             (lax.axis_index("yz") == groups_y - 1).astype(jnp.int32),
         ]
     )
-    fields, edge = call(
+    fields, rises = call(
         transport_body,
-        [((9, 17, 24, depth), f32), ((8, 24, depth), f32)],
+        [((9, 17, 24, depth), f32), ((9, 17, 24, depth), f32)],
         [SCALARS] + [WHOLE] * 7,
         [pltpu.VMEM((4, 19, 32, 128), f32), pltpu.VMEM((19, 32, 128), f32)],
+        vmem=12,
         name="transport",
     )(last, mean, lo, hi, ylo, yhi, brick, col)
     moved_new, = call(
         blend_outer_body,
         [((bricks, 2, 128), f32)],
-        [WHOLE] * 4,
+        [SCALARS] + [WHOLE] * 3,
         [
-            pltpu.VMEM((1344, 128), f32),
-            pltpu.VMEM((1344, 384), bf16),
-            pltpu.VMEM((4, half, 128), f32),
+            pltpu.VMEM((2304, 128), f32),
+            pltpu.VMEM((2304, 384), bf16),
+            pltpu.VMEM((4, cap, 128), f32),
         ],
+        vmem=16,
         name="blend_outer",
-    )(fields, edge, inner, xs)
+    )(bound, fields, inner, xs)
     back = exchange(moved_new, ("gx", "yz"))
 
+    whole = pl.BlockSpec((9, 17, 24, depth), lambda i: (0, 0, 0, 0))
     particle_new = pl.pallas_call(
         update_body,
         out_shape=jax.ShapeDtypeStruct(phi.shape, f32),
-        grid=(wx,),
-        in_specs=[
-            block_phi,
-            block_off,
-            block_count,
-            pl.BlockSpec((9, 17, 24, depth), lambda i: (0, 0, 0, 0)),
-        ],
-        out_specs=block_phi,
-        scratch_shapes=[pltpu.VMEM((9, 8, 8, 128), f32)],
-        compiler_params=pltpu.CompilerParams(vmem_limit_bytes=24 * MB),
+        grid=(wx // 2,),
+        in_specs=[blocks(4, 2), blocks(3, 2), cells(2), whole, whole],
+        out_specs=blocks(4, 2),
+        scratch_shapes=[pltpu.VMEM((9, 8, wy, depth), f32)],
+        compiler_params=pltpu.CompilerParams(vmem_limit_bytes=60 * MB),
         cost_estimate=pl.CostEstimate(flops=8 * 10**7, bytes_accessed=25 * 10**6, transcendentals=0),
         name="update",
-    )(phi, offset, count, fields)
+    )(phi, offset, count, fields, rises)
 
     migrant_new, = call(
         functools.partial(collect_body, bricks=bricks, cap=cap),
         [((4, rows), f32)],
         [WHOLE] * 3,
+        vmem=12,
         name="collect",
     )(dest, rank, back)
     return particle_new, migrant_new

time: 152 us -> 119 us (0.78)
  waiting for transfers between devices: 21.1 us -> 4.24 us
  local copies, waits for them, and re-layouts: 15.3 us -> 4.17 us
  Pallas kernels: 73.4 us -> 65.9 us
  starting transfers between devices: 40.8 us -> 42.7 us
    all_to_all x4, waiting for transfers between devices: 17.5 us -> 4.23 us  [exchange(): return lax.all_to_all(value, axis, split_axis=0, concat_axis=0, tiled=True)]
    pallas_call x6, Pallas kernels: 47.7 us -> 35.1 us  [the longest x1 13.4 us: shards(): call(blend_outer_body, [((bricks, 2, 128), f32)], [SCALARS] + [WHOLE] * 3...]
    unnamed x24 -> x16, local copies, waits for them, and re-layouts: 15.3 us -> 4.17 us
    ppermute x4, waiting for transfers between devices: 3.63 us -> 0.01 us  [shifted(): return lax.ppermute(value, axis, pairs)]
    pallas_call x1, Pallas kernels: 1.73 us -> 4.59 us  [shards(): pl.pallas_call(local_body, out_shape=jax.ShapeDtypeStruct((4, wx, wy, dep...]
    all_to_all x4, starting transfers between devices: 30.3 us -> 32.7 us  [exchange(): return lax.all_to_all(value, axis, split_axis=0, concat_axis=0, tiled=True)]
    pallas_call x1, Pallas kernels: 2.4 us -> 4.61 us  [shards(): call(functools.partial(dispatch_body, bricks=bricks, cap=cap), [((bricks,...]
  transfers between devices with their start and end apart: 8 -> 8, of which waited for: 3 -> 2; matrix products, arithmetic and copies ran while one was open for 0% -> 0% of each run, Pallas kernels for 33% -> 36%
where the time goes in v1:
time: 119 us; the launch traced here: 118 us
  Pallas kernels  65.9 us (55%)
  starting transfers between devices  42.7 us (36%)
  waiting for transfers between devices  4.24 us (4%)
  local copies, waits for them, and re-layouts  4.17 us (4%)
    all_to_all x4, starting transfers between devices, exchange(): return lax.all_to_all(value, axis, split_axis=0, concat_axis=0, tiled=True)  32.7 us
    pallas_call x1, Pallas kernels, shards(): pl.pallas_call(update_body, out_shape=jax.ShapeDtypeStruct(phi.shape, f32...  16.7 us
    pallas_call x1, Pallas kernels, shards(): call(blend_outer_body, [((bricks, 2, 128), f32)], [SCALARS] + [WHOLE] * 3...  13.4 us
    ppermute x4, starting transfers between devices, shifted(): return lax.ppermute(value, axis, pairs)  10.1 us
    pallas_call x1, Pallas kernels, shards(): call(blend_inner_body, [((4, cap, 128), f32)], [SCALARS] + [WHOLE] * 3, [...  9.12 us
    pallas_call x1, Pallas kernels, shards(): call(scatter_body, [((4, wx, wy, depth), f32), ((8, cap, 128), f32), ((2,...  6.53 us
    pallas_call x1, Pallas kernels, shards(): call(functools.partial(dispatch_body, bricks=bricks, cap=cap), [((bricks,...  4.61 us
    pallas_call x1, Pallas kernels, shards(): pl.pallas_call(local_body, out_shape=jax.ShapeDtypeStruct((4, wx, wy, dep...  4.59 us
  transfers between devices with their start and end apart: 8, of which 2 were waited for; matrix products, arithmetic and copies ran while one was open for 0% of the time, Pallas kernels for 36%

profile of v1, /device:TPU:1, one launch (start us, length us, event | category | flops | bytes accessed | tf_op | source)
XLA Modules:
  0.0 117.9 jit_solution(7610454243974249908)
XLA Ops:
  0.6 0.0 copy-start.2
  0.6 4.6 %dispatch.1 = (f32[128,4,128]{2,1,0:T(4,128)}, s32[1,2048]{1,0:T(1,128)}) custom-call(s32[1,2048]{1,0:T(1,128)} %bitcast.8, s32[1,2048]{1,0:T(1,128)} %bitcast.10, f32[4,2048]{1,0:T(4,128)} %phi_ref.3, f32[3,2048]{1,0:T(4,128)} %off_ref.2), custom_call_target="tpu_custom_call" | custom-call | tf_op jit(solution)/shard_map/dispatch/pallas_call | solution.py:559
  5.3 11.5 %all-to-all-start = ((f32[128,4,128]{2,1,0:T(4,128)}), f32[128,4,128]{2,1,0:T(4,128)S(1)}, u32[]{:S(2)}, u32[]{:S(2)}) async-start(f32[128,4,128]{2,1,0:T(4,128)} %get-tuple-element.24), calls=%async_computation | async-start | bytes 524288 | tf_op jit(solution)/shard_map/all_to_all | solution.py:547
  16.8 0.0 copy-start.4
  16.8 1.0 copy-done.4
  17.8 0.9 copy-done.5
  18.7 1.1 pencil_x.1
  19.7 4.6 %local_sum.1.local_ref = f32[4,16,16,128]{3,2,1,0:T(8,128)} custom-call(f32[4,16,16,16,128]{4,3,2,1,0:T(8,128)} %phi_ref.5, s32[16,16,128]{2,1,0:T(8,128)} %count_ref.5), custom_call_target="tpu_custom_call" | custom-call | flops 4000000 | bytes 9000000 | tf_op jit(solution)/shard_map/local_sum/pallas_call | solution.py:577
  24.3 3.3 %all-to-all-done.arr_ref = f32[128,4,128]{2,1,0:T(4,128)S(1)} async-done(((f32[128,4,128]{2,1,0:T(4,128)}), f32[128,4,128]{2,1,0:T(4,128)S(1)}, u32[]{:S(2)}, u32[]{:S(2)}) %all-to-all-start) | async-done | bytes 262176 | tf_op jit(solution)/shard_map/all_to_all | solution.py:547
  27.6 3.6 %all-to-all-start.1 = ((f32[16,24,512]{2,1,0:T(8,128)}), f32[16,24,512]{2,1,0:T(8,128)S(1)}, u32[]{:S(2)}, u32[]{:S(2)}) async-start(f32[16,24,512]{2,1,0:T(8,128)} %pencil_x.1), calls=%async_computation.1 | async-start | bytes 1572864 | tf_op jit(solution)/shard_map/all_to_all | solution.py:547
  31.3 1.0 copy-done.3
  32.3 6.5 %scatter.1 = (f32[4,16,16,128]{3,2,1,0:T(8,128)S(1)}, f32[8,64,128]{2,1,0:T(8,128)S(1)}, s32[2,128]{1,0:T(2,128)S(1)}, f32[4,1,16,128]{3,2,1,0:T(8,128)S(1)}, f3...) custom-call(f32[128,4,128]{2,1,0:T(4,128)S(1)} %all-to-all-done.arr_ref, ...), custom_call_target="tpu_custom_call" | custom-call | flops 4000000000 | bytes 2000000 | tf_op jit(solution)/shard_map/scatter/pallas_call | solution.py:590
  38.9 3.1 %collective-permute-start = (f32[4,1,16,128]{3,2,1,0:T(8,128)S(1)}, f32[4,1,16,128]{3,2,1,0:T(8,128)S(1)}, u32[]{:S(2)}, u32[]{:S(2)}) collective-permute-start(f32[4,1,16,128]{3,2,1,0:T(8,128)S(1)} %get-tuple-element.28), channel_id=1, source_target_pairs={{0,8},{8,16},{16,24},{24,32},{32,40},{40,48},{48,56},{56,64},{64,7... | collective-permute-start | bytes 98312 | tf_op jit(solution)/shard_map/ppermute | solution.py:543
  42.0 1.3 %collective-permute-start.1 = (f32[4,2,16,128]{3,2,1,0:T(8,128)S(1)}, f32[4,2,16,128]{3,2,1,0:T(8,128)S(1)}, u32[]{:S(2)}, u32[]{:S(2)}) collective-permute-start(f32[4,2,16,128]{3,2,1,0:T(8,128)S(1)} %get-tuple-element.29), channel_id=1, source_target_pairs={{8,0},{16,8},{24,16},{32,24},{40,32},{48,40},{56,48},{64,56},{72,6... | collective-permute-start | bytes 196616 | tf_op jit(solution)/shard_map/ppermute | solution.py:543
  43.3 0.9 all-to-all-done.1.in_ref
  44.2 1.2 %pencil_y.1 = f32[8,24,1280]{2,1,0:T(8,128)} custom-call(f32[16,24,512]{2,1,0:T(8,128)S(1)} %all-to-all-done.1.in_ref), custom_call_target="tpu_custom_call" | custom-call | tf_op jit(solution)/shard_map/pencil_y/pallas_call | solution.py:611
  45.5 6.9 %all-to-all-start.2 = ((f32[8,24,1280]{2,1,0:T(8,128)}), f32[8,24,1280]{2,1,0:T(8,128)S(1)}, u32[]{:S(2)}, u32[]{:S(2)}) async-start(f32[8,24,1280]{2,1,0:T(8,128)} %pencil_y.1), calls=%async_computation.2 | async-start | bytes 1966080 | tf_op jit(solution)/shard_map/all_to_all | solution.py:547
  52.4 0.1 add_convert_fusion.last_ref
  52.5 3.5 %collective-permute-start.2 = (f32[4,24,128]{2,1,0:T(8,128)S(1)}, f32[4,24,128]{2,1,0:T(8,128)S(1)}, u32[]{:S(2)}, u32[]{:S(2)}) collective-permute-start(f32[4,24,128]{2,1,0:T(8,128)S(1)} %get-tuple-element.32), channel_id=1, source_target_pairs={{0,1},{1,2},{2,3},{3,4},{4,5},{5,6},{6,7},{8,9},{9,10},{10,11},{11... | collective-permute-start | bytes 147464 | tf_op jit(solution)/shard_map/ppermute | solution.py:543
  56.0 2.1 %collective-permute-start.3 = (f32[2,4,24,128]{3,2,1,0:T(8,128)S(1)}, f32[2,4,24,128]{3,2,1,0:T(8,128)S(1)}, u32[]{:S(2)}, u32[]{:S(2)}) collective-permute-start(f32[2,4,24,128]{3,2,1,0:T(8,128)S(1)} %get-tuple-element.33), channel_id=1, source_target_pairs={{1,0},{2,1},{3,2},{4,3},{5,4},{6,5},{7,6},{9,8},{10,9},{11,10},{12... | collective-permute-start | bytes 294920 | tf_op jit(solution)/shard_map/ppermute | solution.py:543
  58.1 9.1 %blend_inner.1.inner_ref = f32[4,64,128]{2,1,0:T(8,128)S(1)} custom-call(s32[2,128]{1,0:T(2,128)S(1)} %get-tuple-element.37.bound_ref, f32[4,16,16,128]{3,2,1,0:T(8,128)S(1)} %get-tuple-element.27.mean_ref, f32[4,2,16,128]{3,2,1,0:T(8,128)S(1)} %collective-permute-done.1.hi_ref, f32[8,64,128]{2,1,0:T(8,128)S(1)} %get-tuple-element.38.xs_ref), custom_call_target="tpu_custom_call" | custom-call | flops 8000000000 | bytes 3000000 | tf_op jit(solution)/shard_map/blend_inner/pallas_call | solution.py:624
  67.3 3.6 %brick.1 = (f32[4,19,16,128]{3,2,1,0:T(8,128)S(1)}, f32[4,3,24,128]{3,2,1,0:T(8,128)S(1)}) custom-call(f32[8,24,1280]{2,1,0:T(8,128)S(1)} %all-to-all-done.2.in_ref), custom_call_target="tpu_custom_call" | custom-call | tf_op jit(solution)/shard_map/brick/pallas_call | solution.py:634
  70.9 0.0 collective-permute-done.2.ylo_ref
  70.9 0.0 collective-permute-done.3.yhi_ref
  70.9 3.7 %transport.1 = (f32[9,17,24,128]{3,2,1,0:T(8,128)S(1)}, f32[9,17,24,128]{3,2,1,0:T(8,128)S(1)}) custom-call(s32[2]{0:T(128)S(1)} %add_convert_fusion.last_ref, f32[4,16,16,128]{3,2,1,0:T(8,128)S(1)} %get-tuple-element.27.mean_ref, f32[4,1,16,128]{3,2,1,0:T(8,128)S(1)} %collective-permute-done.lo_ref, f32[4,2,16,128]{3,2,1,0:T(8,128)S(1)} %collective-permute-done.1.hi_ref, ...), custom_call_target="tpu_custom_call" | custom-call | tf_op jit(solution)/shard_map/transport/pallas_call | solution.py:649
  74.6 1.2 %copy-done.1 = f32[9,17,24,128]{3,2,1,0:T(8,128)} copy-done((f32[9,17,24,128]{3,2,1,0:T(8,128)}, f32[9,17,24,128]{3,2,1,0:T(8,128)S(1)}, u32[]{:S(2)}) %copy-start.1) | copy-done | bytes 1880088
  75.9 13.4 %blend_outer.1 = f32[128,2,128]{2,1,0:T(2,128)} custom-call(s32[2,128]{1,0:T(2,128)S(1)} %get-tuple-element.37.bound_ref, f32[9,17,24,128]{3,2,1,0:T(8,128)S(1)} %get-tuple-element.42.f_ref, f32[4,64,128]{2,1,0:T(8,128)S(1)} %blend_inner.1.inner_ref, f32[8,64,128]{2,1,0:T(8,128)S(1)} %get-tuple-element.38.xs_ref), custom_call_target="tpu_custom_call" | custom-call | tf_op jit(solution)/shard_map/blend_outer/pallas_call | solution.py:657
  89.3 10.7 %all-to-all-start.3 = ((f32[128,2,128]{2,1,0:T(2,128)}), f32[128,2,128]{2,1,0:T(2,128)S(1)}, u32[]{:S(2)}, u32[]{:S(2)}) async-start(f32[128,2,128]{2,1,0:T(2,128)} %blend_outer.1), calls=%async_computation.3 | async-start | bytes 262144 | tf_op jit(solution)/shard_map/all_to_all | solution.py:547
  100.0 0.0 copy-start.6
  100.0 0.0 copy-start.7
  100.0 16.7 %update.1 = f32[4,16,16,16,128]{4,3,2,1,0:T(8,128)} custom-call(f32[4,16,16,16,128]{4,3,2,1,0:T(8,128)} %phi_ref.5, f32[3,16,16,16,128]{4,3,2,1,0:T(8,128)} %off_ref.3, s32[16,16,128]{2,1,0:T(8,128)} %count_ref.5, f32[9,17,24,128]{3,2,1,0:T(8,128)} %copy-done, f32[9,17,24,128]{3,2,1,0:T(8,128)} %copy-done.1), custom_call_target="tpu_custom_call" | custom-call | flops 80000000 | bytes 25000000 | tf_op jit(solution)/shard_map/update/pallas_call | solution.py:672
  116.7 1.2 %collect.1 = f32[4,2048]{1,0:T(4,128)} custom-call(s32[1,2048]{1,0:T(1,128)S(1)} %bitcast.9, s32[1,2048]{1,0:T(1,128)S(1)} %copy-done.7, f32[128,2,128]{2,1,0:T(2,128)S(1)} %all-to-all-done.3.back_ref), custom_call_target="tpu_custom_call" | custom-call | tf_op jit(solution)/shard_map/collect/pallas_call | solution.py:684
  (13 shorter events, 0.0 us)
Async XLA Ops:
  0.6 30.6 %copy-start.2 = (s32[16,16,128]{2,1,0:T(8,128)S(1)}, s32[16,16,128]{2,1,0:T(8,128)}, u32[]{:S(2)}) copy-start(s32[16,16,128]{2,1,0:T(8,128)} %count_ref.5) | copy-start | bytes 393220
  5.3 22.4 %all-to-all-start = ((f32[128,4,128]{2,1,0:T(4,128)}), f32[128,4,128]{2,1,0:T(4,128)S(1)}, u32[]{:S(2)}, u32[]{:S(2)}) async-start(f32[128,4,128]{2,1,0:T(4,128)} %get-tuple-element.24), calls=%async_computation | async-start | bytes 524288 | tf_op jit(solution)/shard_map/all_to_all | solution.py:547
  16.8 1.0 copy-start.4
  17.8 0.9 copy-start.5
  27.6 16.6 %all-to-all-start.1 = ((f32[16,24,512]{2,1,0:T(8,128)}), f32[16,24,512]{2,1,0:T(8,128)S(1)}, u32[]{:S(2)}, u32[]{:S(2)}) async-start(f32[16,24,512]{2,1,0:T(8,128)} %pencil_x.1), calls=%async_computation.1 | async-start | bytes 1572864 | tf_op jit(solution)/shard_map/all_to_all | solution.py:547
  31.3 1.0 copy-start.3
  38.9 13.6 %collective-permute-start = (f32[4,1,16,128]{3,2,1,0:T(8,128)S(1)}, f32[4,1,16,128]{3,2,1,0:T(8,128)S(1)}, u32[]{:S(2)}, u32[]{:S(2)}) collective-permute-start(f32[4,1,16,128]{3,2,1,0:T(8,128)S(1)} %get-tuple-element.28), channel_id=1, source_target_pairs={{0,8},{8,16},{16,24},{24,32},{32,40},{40,48},{48,56},{56,64},{64,7... | collective-permute-start | bytes 98312 | tf_op jit(solution)/shard_map/ppermute | solution.py:543
  42.0 10.4 %collective-permute-start.1 = (f32[4,2,16,128]{3,2,1,0:T(8,128)S(1)}, f32[4,2,16,128]{3,2,1,0:T(8,128)S(1)}, u32[]{:S(2)}, u32[]{:S(2)}) collective-permute-start(f32[4,2,16,128]{3,2,1,0:T(8,128)S(1)} %get-tuple-element.29), channel_id=1, source_target_pairs={{8,0},{16,8},{24,16},{32,24},{40,32},{48,40},{56,48},{64,56},{72,6... | collective-permute-start | bytes 196616 | tf_op jit(solution)/shard_map/ppermute | solution.py:543
  45.5 21.8 %all-to-all-start.2 = ((f32[8,24,1280]{2,1,0:T(8,128)}), f32[8,24,1280]{2,1,0:T(8,128)S(1)}, u32[]{:S(2)}, u32[]{:S(2)}) async-start(f32[8,24,1280]{2,1,0:T(8,128)} %pencil_y.1), calls=%async_computation.2 | async-start | bytes 1966080 | tf_op jit(solution)/shard_map/all_to_all | solution.py:547
  52.5 18.5 %collective-permute-start.2 = (f32[4,24,128]{2,1,0:T(8,128)S(1)}, f32[4,24,128]{2,1,0:T(8,128)S(1)}, u32[]{:S(2)}, u32[]{:S(2)}) collective-permute-start(f32[4,24,128]{2,1,0:T(8,128)S(1)} %get-tuple-element.32), channel_id=1, source_target_pairs={{0,1},{1,2},{2,3},{3,4},{4,5},{5,6},{6,7},{8,9},{9,10},{10,11},{11... | collective-permute-start | bytes 147464 | tf_op jit(solution)/shard_map/ppermute | solution.py:543
  56.0 14.9 %collective-permute-start.3 = (f32[2,4,24,128]{3,2,1,0:T(8,128)S(1)}, f32[2,4,24,128]{3,2,1,0:T(8,128)S(1)}, u32[]{:S(2)}, u32[]{:S(2)}) collective-permute-start(f32[2,4,24,128]{3,2,1,0:T(8,128)S(1)} %get-tuple-element.33), channel_id=1, source_target_pairs={{1,0},{2,1},{3,2},{4,3},{5,4},{6,5},{7,6},{9,8},{10,9},{11,10},{12... | collective-permute-start | bytes 294920 | tf_op jit(solution)/shard_map/ppermute | solution.py:543
  74.6 1.2 %copy-start.1 = (f32[9,17,24,128]{3,2,1,0:T(8,128)}, f32[9,17,24,128]{3,2,1,0:T(8,128)S(1)}, u32[]{:S(2)}) copy-start(f32[9,17,24,128]{3,2,1,0:T(8,128)S(1)} %get-tuple-element.43.rise_ref) | copy-start | bytes 5640196
  75.9 24.1 %copy-start = (f32[9,17,24,128]{3,2,1,0:T(8,128)}, f32[9,17,24,128]{3,2,1,0:T(8,128)S(1)}, u32[]{:S(2)}) copy-start(f32[9,17,24,128]{3,2,1,0:T(8,128)S(1)} %get-tuple-element.42.f_ref) | copy-start | bytes 5640196
  89.3 27.4 %all-to-all-start.3 = ((f32[128,2,128]{2,1,0:T(2,128)}), f32[128,2,128]{2,1,0:T(2,128)S(1)}, u32[]{:S(2)}, u32[]{:S(2)}) async-start(f32[128,2,128]{2,1,0:T(2,128)} %blend_outer.1), calls=%async_computation.3 | async-start | bytes 262144 | tf_op jit(solution)/shard_map/all_to_all | solution.py:547
  100.0 16.7 %copy-start.6 = (s32[2048,1]{0,1:T(1,128)S(1)}, s32[2048,1]{0,1:T(1,128)}, u32[]{:S(2)}) copy-start(s32[2048,1]{0,1:T(1,128)} %param.16) | copy-start | bytes 24580
  100.0 16.7 %copy-start.7 = (s32[1,2048]{1,0:T(1,128)S(1)}, s32[1,2048]{1,0:T(1,128)}, u32[]{:S(2)}) copy-start(s32[1,2048]{1,0:T(1,128)} %get-tuple-element.44.rank_ref) | copy-start | bytes 24580

commit v2 on v1

--- a/solution.py
+++ b/solution.py
@@ -10,6 +10,8 @@
 time_step = 0.08
 mix_coeff = 0.5
 span = 8
+further = 4
+tiles_held = 8
 f32 = jnp.float32
 bf16 = jnp.bfloat16
 MB = 2**20
@@ -64,15 +66,35 @@
 def dispatch_body(dest_ref, cell_ref, phi_ref, off_ref, out_ref, rank_ref, *, bricks, cap):
     rows = dest_ref.shape[1]
     hot = jnp.where(iota((bricks, rows), 0) == dest_ref[...], 1.0, 0.0).astype(bf16)
-    key = cell_ref[...] * rows + iota((1, rows), 1)
-    key_down = jnp.broadcast_to(key, (8, rows)).T[:, 0:1]
+    lines = 16
+    line = cell_ref[...] >> 11
+    on_line = jnp.where(iota((lines, rows), 0) == line, 1.0, 0.0)
+    lined = on_line.astype(bf16)
+    bucket = (dest_ref[...] * lines + line).astype(f32)
+    bucket_down = jnp.broadcast_to(bucket, (8, rows)).T[:, 0:1]
+    total = dot_nt(lined, hot)
+    lasts = [None] * lines
+    left = jnp.full((1, bricks), float(cap), f32)
+    for k in range(lines - 1, -1, -1):
+        left = left - total[k : k + 1]
+        lasts[k] = left
+    free = jnp.zeros((1, bricks), f32)
+    starts = []
+    for k in range(lines):
+        free = jnp.maximum(free, float(k * cap // lines))
+        starts.append(jnp.minimum(free, lasts[k]))
+        free = free + total[k : k + 1]
+    base = jnp.concatenate(starts, axis=0)
     step = 256
+    earlier = iota((step, step), 0) < iota((step, step), 1)
     ranks = []
     for b in range(rows // step):
         cut = slice(b * step, (b + 1) * step)
-        before = jnp.where(key_down < key[:, cut], 1.0, 0.0).astype(bf16)
-        count = dot_nn(hot, before)
-        ranks.append(jnp.sum(hot[:, cut].astype(f32) * count, axis=0, keepdims=True))
+        start = dot_nn(base.astype(bf16), hot[:, cut])
+        start = jnp.sum(start * on_line[:, cut], axis=0, keepdims=True)
+        same = (bucket_down[cut] == bucket[:, cut]) & earlier
+        ranks.append(start + jnp.sum(jnp.where(same, 1.0, 0.0), axis=0, keepdims=True))
+        base = base + dot_nt(lined[:, cut], hot[:, cut])
     rank = jnp.concatenate(ranks, axis=1).astype(jnp.int32)
     rank_ref[...] = rank
     here = iota((cap, rows), 0) == rank
@@ -127,7 +149,13 @@
     code = arr_ref[:, 3, :].astype(jnp.int32) - 1
     line = code >> 11
     bound_ref[0:1, :] = jnp.min(jnp.where(code >= 0, line, 16), axis=0, keepdims=True)
-    bound_ref[1:2, :] = jnp.max(jnp.where(code >= 0, line, -1), axis=0, keepdims=True)
+    most = jnp.max(jnp.where(code >= 0, line, -1), axis=0, keepdims=True)
+    bound_ref[1:2, :] = most
+    place = iota((1, 128), 1) - half
+    in_use = jnp.where((place >= 0) & (most >= 0), place + 1, 0)
+    used = jnp.max(in_use, axis=1, keepdims=True)
+    used = (used + 2 * tiles_held - 1) // (2 * tiles_held)
+    bound_ref[2:3, :] = jnp.broadcast_to(used, (1, 128))
     acc_ref[...] = jnp.zeros_like(acc_ref)
     spots = places(256, 128)
 
@@ -206,48 +234,87 @@
 def pencil_y_body(in_ref, out_ref):
     groups = out_ref.shape[0]
     lane = iota((24, 128), 1)
+    line = lane[0:16]
     zero = jnp.zeros((24, 128), f32)
     for q in range(groups):
-        out_ref[q, :, 0:512] = in_ref[2 * q]
-        out_ref[q, :, 512:1024] = in_ref[2 * q + 1]
+        out_ref[q, :, 0:512] = in_ref[2 * q, 0:16, :]
+        out_ref[q, :, 512:1024] = in_ref[2 * q + 1, 0:16, :]
         pieces = []
         for c in range(4):
             lanes = slice(128 * c, 128 * c + 128)
             above = in_ref[2 * q + 2, :, lanes] if q < groups - 1 else zero
-            below = pltpu.roll(in_ref[2 * q - 1, :, lanes], 48, 1) if q > 0 else zero
+            below = zero
+            if c == 3 and q > 0:
+                below = pltpu.roll(in_ref[2 * q - 1, :, lanes], 48, 1)
             pieces.append(jnp.where(lane < 32, above, jnp.where(lane < 48, below, 0.0)))
-        for e in (0, 1):
-            out_ref[q, :, 1024 + 128 * e : 1152 + 128 * e] = jnp.where(
-                lane < 64, pieces[2 * e], pltpu.roll(pieces[2 * e + 1], 64, 1)
+        first, second, third, fourth = pieces
+        second = pltpu.roll(second, 16, 1)
+        third = pltpu.roll(third, 32, 1)
+        speeds = jnp.where(lane < 16, first, jnp.where(lane < 32, second, third))
+        rows = [
+            in_ref[2 * q + h, 16:17, 128 * c : 128 * c + 128] for c in range(3) for h in (0, 1)
+        ]
+        rows += [
+            in_ref[2 * q + h, 16 + e : 17 + e, 384:512] for e in range(3) for h in (0, 1)
+        ]
+        rows.append(speeds[16:17])
+        rows.append(fourth[16:19])
+        out_ref[q, :, 1024:1152] = jnp.concatenate(rows, axis=0)
+        out_ref[q, :, 1152:1280] = jnp.where(
+            line < 48, speeds[0:16], pltpu.roll(fourth[0:16], 48, 1)
+        )
+
+
+def turned_lanes(group, lane):
+    for bit in (4, 2, 1):
+        shift = 16 * bit
+        high = (lane // shift) % 2 == 1
+        fresh = list(group)
+        for j in range(8):
+            if j & bit:
+                continue
+            first, second = group[j], group[j | bit]
+            if bit == 4:
+                moved = pltpu.roll(jnp.where(high, first, second), shift, 1)
+                fresh[j] = jnp.where(high, moved, first)
+                fresh[j | bit] = jnp.where(high, second, moved)
+            else:
+                fresh[j] = jnp.where(high, pltpu.roll(second, shift, 1), first)
+                fresh[j | bit] = jnp.where(high, second, pltpu.roll(first, 128 - shift, 1))
+        group = fresh
+    return group
+
+
+def brick_part(in_ref, brick_ref, col_ref, tall_ref):
+    lane = iota((8, 128), 1)
+    col_ref[...] = jnp.zeros_like(col_ref)
+    for tile in range(10):
+        for xt in range(2):
+            group = turned_lanes(
+                [in_ref[j, 8 * xt : 8 * xt + 8, 128 * tile : 128 * tile + 128] for j in range(8)],
+                lane,
             )
-
-
-def brick_body(in_ref, brick_ref, col_ref, tall_ref):
-    lane = iota((8, 128), 1)
-    for tile in range(10):
-        for xt in range(3):
-            group = [in_ref[j, 8 * xt : 8 * xt + 8, 128 * tile : 128 * tile + 128] for j in range(8)]
-            for bit in (4, 2, 1):
-                shift = 16 * bit
-                high = (lane // shift) % 2 == 1
-                fresh = list(group)
-                for j in range(8):
-                    if j & bit:
-                        continue
-                    first, second = group[j], group[j | bit]
-                    fresh[j] = jnp.where(high, pltpu.roll(second, shift, 1), first)
-                    fresh[j | bit] = jnp.where(high, second, pltpu.roll(first, 128 - shift, 1))
-                group = fresh
             for g in range(8):
                 if tile < 8:
-                    c, y = tile % 4, 8 * (tile // 4) + g
-                    at = (c * 16 + y) * 24 + 8 * xt
+                    at = (16 * (tile % 4) + 8 * (tile // 4) + g) * 24 + 8 * xt
                     tall_ref[at : at + 8, :] = group[g]
-                elif g % 4 < 3:
-                    c, y = 2 * (tile - 8) + g // 4, g % 4
-                    col_ref[c, y, 8 * xt : 8 * xt + 8, :] = group[g]
+                elif tile == 9:
+                    if g < 6:
+                        c, y = (g, 0) if g < 3 else (3, g - 3)
+                        col_ref[c, y, 8 * xt : 8 * xt + 8, :] = group[g]
+                else:
+                    for k in range(8):
+                        n = 8 * xt + k
+                        if n < 12:
+                            c, e = (n // 2, 0) if n < 6 else (3, (n - 6) // 2)
+                            at = (16 * c + 8 * (n % 2) + g) * 24 + 16 + e
+                            tall_ref[at : at + 1, :] = group[g][k : k + 1]
+                        elif n == 12 and g < 3:
+                            col_ref[g, 0, 16:17, :] = group[g][k : k + 1]
+                        elif n > 12 and g < 3:
+                            col_ref[3, g, n + 3 : n + 4, :] = group[g][k : k + 1]
     for c in range(4):
-        for x in range(19):
+        for x in range(19 if c == 3 else 17):
             for yt in (0, 8):
                 brick_ref[c, x, yt : yt + 8, :] = tall_ref[
                     pl.ds((c * 16 + yt) * 24 + x, 8, stride=24), :
@@ -319,18 +386,18 @@
     half = xs_ref.shape[1]
     low = jnp.minimum(bound_ref[0, half + 2 * i], bound_ref[0, half + 2 * i + 1])
     high = jnp.maximum(bound_ref[1, half + 2 * i], bound_ref[1, half + 2 * i + 1])
-    windows = (high + 1 - low + span) >> 3
+    windows = (high + 1 - low - span + further) >> 2
     rows_z = depth_weights(spots, depth, row(6))
     wy = hat(24, y, row(5))
     return row, x, low, windows, rows_z, wy
 
 
-def window_sums(lhs_ref, per, blocks, low, x, frac, rows_z, wy, sums):
+def window_sums(lhs_ref, planes, per, blocks, low, x, frac, rows_z, wy, sums):
     at = pl.multiple_of(low * per, 16)
-    along = dot_nn(lhs_ref[pl.ds(at, span * per), :], rows_z)
-    wx = hat(span, x - low, frac)
+    along = dot_nn(lhs_ref[pl.ds(at, planes * per), :], rows_z)
+    wx = hat(8, x - low, frac)
     sums = list(sums)
-    for k in range(span):
+    for k in range(planes):
         inside = wx[k : k + 1] * wy[0:16]
         for n in range(blocks):
             sums[n] = sums[n] + along[per * k + 16 * n : per * k + 16 * n + 16] * inside
@@ -342,26 +409,27 @@
 
 def blend_tiles(lhs_ref, per, blocks, xs_ref, bound_ref, tiles, finish):
     spots = places(128, 256)
+    zero = tuple(jnp.zeros((16, 256), f32) for _ in range(per // 16))
 
     def group(g, carry):
         held = []
         for e in range(tiles):
             i = g * tiles + e
             row, x, low, windows, rows_z, wy = tile_terms(spots, xs_ref, bound_ref, i)
-            zero = tuple(jnp.zeros((16, 256), f32) for _ in range(per // 16))
-            sums = window_sums(lhs_ref, per, blocks, low, x, row(4), rows_z, wy, zero)
-            held.append((i, row, x, low, windows, rows_z, wy, sums))
-        for i, row, x, low, windows, rows_z, wy, sums in held:
+            args = (x, row(4), rows_z, wy)
+            sums = window_sums(lhs_ref, span, per, blocks, low, *args, zero)
+            held.append((i, row, low + span, windows, args, sums))
+        for i, row, start, windows, args, sums in held:
 
             def more(w, now):
                 return window_sums(
-                    lhs_ref, per, blocks, low + span * w, x, row(4), rows_z, wy, now
+                    lhs_ref, further, per, blocks, start + further * w, *args, now
                 )
 
-            finish(i, row, lax.fori_loop(1, windows, more, sums))
+            finish(i, row, lax.fori_loop(0, windows, more, sums))
         return carry
 
-    lax.fori_loop(0, xs_ref.shape[1] // (2 * tiles), group, 0)
+    lax.fori_loop(0, bound_ref[2, 0], group, 0)
 
 
 def keep_row(ref, c, i, value):
@@ -376,15 +444,16 @@
         tab_ref[1024 + 16 * c : 1040 + 16 * c, :] = hi_ref[c, 0]
     tab_ref[1088:, :] = jnp.zeros((64 * (span - 1), 128), f32)
     widen(tab_ref, lhs_ref)
+    out_ref[...] = jnp.zeros_like(out_ref)
 
     def finish(i, row, sums):
         for c in range(4):
             keep_row(out_ref, c, i, total_y(sums[c]))
 
-    blend_tiles(lhs_ref, 64, 4, xs_ref, bound_ref, 8, finish)
-
-
-def transport_body(
+    blend_tiles(lhs_ref, 64, 4, xs_ref, bound_ref, tiles_held, finish)
+
+
+def transport_part(
     last_ref, mean_ref, lo_ref, hi_ref, ylo_ref, yhi_ref, brick_ref, col_ref, f_ref, rise_ref, mp_ref, gp_ref
 ):
     x_in = jnp.where(last_ref[0] == 1, 0.0, 1.0).astype(f32)
@@ -462,7 +531,7 @@
     rise_ref[8, :, 16, :] = (gammas[2][0] - gamma)[0:17]
 
 
-def blend_outer_body(bound_ref, f_ref, inner_ref, xs_ref, out_ref, tab_ref, lhs_ref, new_ref):
+def outer_part(bound_ref, f_ref, inner_ref, xs_ref, out_ref, tab_ref, lhs_ref, new_ref):
     for x in range(17):
         for c in range(5):
             tab_ref[96 * x + 16 * c : 96 * x + 16 * c + 16, :] = f_ref[4 + c, x, 0:16, :]
@@ -471,6 +540,7 @@
         )
     tab_ref[96 * 17 :, :] = jnp.zeros((96 * (span - 1), 128), f32)
     widen(tab_ref, lhs_ref)
+    new_ref[...] = jnp.zeros_like(new_ref)
 
     def finish(i, row, sums):
         def inner(c):
@@ -484,11 +554,23 @@
             moved = total_y(sums[c]) + rim[4 + c : 5 + c]
             keep_row(new_ref, c, i, phi + moved - rate * (phi - mean))
 
-    blend_tiles(lhs_ref, 96, 5, xs_ref, bound_ref, 8, finish)
+    blend_tiles(lhs_ref, 96, 5, xs_ref, bound_ref, tiles_held, finish)
     half = xs_ref.shape[1]
     for r in range(2):
         both = jnp.concatenate([new_ref[2 * r], new_ref[2 * r + 1]], axis=0)
         out_ref[:, r, :] = both.T
+
+
+def fields_body(
+    last_ref, bound_ref, wide_ref, mean_ref, lo_ref, hi_ref, ylo_ref, yhi_ref, inner_ref, xs_ref,
+    f_ref, rise_ref, out_ref,
+    brick_ref, col_ref, tall_ref, mp_ref, gp_ref, tab_ref, lhs_ref, new_ref,
+):
+    brick_part(wide_ref, brick_ref, col_ref, tall_ref)
+    transport_part(
+        last_ref, mean_ref, lo_ref, hi_ref, ylo_ref, yhi_ref, brick_ref, col_ref, f_ref, rise_ref, mp_ref, gp_ref
+    )
+    outer_part(bound_ref, f_ref, inner_ref, xs_ref, out_ref, tab_ref, lhs_ref, new_ref)
 
 
 def update_body(phi_ref, off_ref, count_ref, f_ref, rise_ref, out_ref, coef_ref):
@@ -580,7 +662,7 @@
         grid=(wx // 8,),
         in_specs=[blocks(4, 8), cells(8)],
         out_specs=pl.BlockSpec((4, 8, wy, depth), lambda i: (0, i, 0, 0)),
-        compiler_params=pltpu.CompilerParams(vmem_limit_bytes=60 * MB),
+        compiler_params=pltpu.CompilerParams(vmem_limit_bytes=54 * MB),
         cost_estimate=pl.CostEstimate(flops=4 * 10**6, bytes_accessed=9 * 10**6, transcendentals=0),
         name="local_sum",
     )(phi, count)
@@ -592,7 +674,7 @@
         [
             ((4, wx, wy, depth), f32),
             ((8, cap, 128), f32),
-            ((2, 128), jnp.int32),
+            ((3, 128), jnp.int32),
             ((4, 1, wy, depth), f32),
             ((4, 2, wy, depth), f32),
             ((4, wx, depth), f32),
@@ -609,8 +691,9 @@
     lo = shifted(ehi, "gx", 1)
     hi = shifted(elo, "gx", -1)
     wide, = call(
-        pencil_y_body, [((groups_y, 24, 1280), f32)], [WHOLE], vmem=8, name="pencil_y"
+        pencil_y_body, [((groups_y, 16, 1280), f32)], [WHOLE], vmem=8, name="pencil_y"
     )(pencil)
+    e15, _ = lax.optimization_barrier((e15, wide))
     up, down = call(
         edge_body,
         [((4, 24, depth), f32), ((2, 4, 24, depth), f32)],
@@ -631,52 +714,44 @@
         name="blend_inner",
     )(bound, mean, hi, xs)
     wide, inner = lax.optimization_barrier((wide, inner))
-    brick, col = call(
-        brick_body,
-        [((4, 19, wy, depth), f32), ((4, 3, 24, depth), f32)],
-        [WHOLE],
-        [pltpu.VMEM((4 * 16 * 24, 128), f32)],
-        vmem=8,
-        name="brick",
-    )(wide)
-
     last = jnp.stack(
         [
             (lax.axis_index("gx") == groups_x - 1).astype(jnp.int32),
             (lax.axis_index("yz") == groups_y - 1).astype(jnp.int32),
         ]
     )
-    fields, rises = call(
-        transport_body,
-        [((9, 17, 24, depth), f32), ((9, 17, 24, depth), f32)],
-        [SCALARS] + [WHOLE] * 7,
-        [pltpu.VMEM((4, 19, 32, 128), f32), pltpu.VMEM((19, 32, 128), f32)],
-        vmem=12,
-        name="transport",
-    )(last, mean, lo, hi, ylo, yhi, brick, col)
-    moved_new, = call(
-        blend_outer_body,
-        [((bricks, 2, 128), f32)],
-        [SCALARS] + [WHOLE] * 3,
-        [
+    fields, rises, moved_new = pl.pallas_call(
+        fields_body,
+        out_shape=(
+            jax.ShapeDtypeStruct((9, 17, 24, depth), f32),
+            jax.ShapeDtypeStruct((9, 17, 24, depth), f32),
+            jax.ShapeDtypeStruct((bricks, 2, 128), f32),
+        ),
+        in_specs=[SCALARS] * 2 + [WHOLE] * 8,
+        out_specs=(WHOLE, WHOLE, WHOLE),
+        scratch_shapes=[
+            pltpu.VMEM((4, 19, wy, depth), f32),
+            pltpu.VMEM((4, 3, 24, depth), f32),
+            pltpu.VMEM((4 * 16 * 24, 128), f32),
+            pltpu.VMEM((4, 19, 32, 128), f32),
+            pltpu.VMEM((19, 32, 128), f32),
             pltpu.VMEM((2304, 128), f32),
             pltpu.VMEM((2304, 384), bf16),
             pltpu.VMEM((4, cap, 128), f32),
         ],
-        vmem=16,
-        name="blend_outer",
-    )(bound, fields, inner, xs)
+        compiler_params=pltpu.CompilerParams(vmem_limit_bytes=28 * MB),
+        name="fields",
+    )(last, bound, wide, mean, lo, hi, ylo, yhi, inner, xs)
     back = exchange(moved_new, ("gx", "yz"))
 
-    whole = pl.BlockSpec((9, 17, 24, depth), lambda i: (0, 0, 0, 0))
     particle_new = pl.pallas_call(
         update_body,
         out_shape=jax.ShapeDtypeStruct(phi.shape, f32),
         grid=(wx // 2,),
-        in_specs=[blocks(4, 2), blocks(3, 2), cells(2), whole, whole],
+        in_specs=[blocks(4, 2), blocks(3, 2), cells(2), WHOLE, WHOLE],
         out_specs=blocks(4, 2),
         scratch_shapes=[pltpu.VMEM((9, 8, wy, depth), f32)],
-        compiler_params=pltpu.CompilerParams(vmem_limit_bytes=60 * MB),
+        compiler_params=pltpu.CompilerParams(vmem_limit_bytes=54 * MB),
         cost_estimate=pl.CostEstimate(flops=8 * 10**7, bytes_accessed=25 * 10**6, transcendentals=0),
         name="update",
     )(phi, offset, count, fields, rises)

time: 119 us -> 108 us (0.908)
  Pallas kernels: 65.9 us -> 56.3 us
  starting transfers between devices: 42.7 us -> 40.5 us
  local copies, waits for them, and re-layouts: 4.17 us -> 5.45 us
    pallas_call x5 -> x3, Pallas kernels: 28.5 us -> 22.4 us  [the longest x1 14.8 us: shards(): pl.pallas_call(fields_body, out_shape=(jax.ShapeDtypeStruct((9, 17, 24, d...]
    pallas_call x1, Pallas kernels: 9.12 us -> 6.24 us  [shards(): call(blend_inner_body, [((4, cap, 128), f32)], [SCALARS] + [WHOLE] * 3, [...]
    all_to_all x4, starting transfers between devices: 32.7 us -> 30.7 us  [exchange(): return lax.all_to_all(value, axis, split_axis=0, concat_axis=0, tiled=True)]
    unnamed x16, local copies, waits for them, and re-layouts: 4.17 us -> 5.45 us
  transfers between devices with their start and end apart: 8 -> 8, of which waited for: 2 -> 2; matrix products, arithmetic and copies ran while one was open for 0% -> 0% of each run, Pallas kernels for 36% -> 34%
where the time goes in v2:
time: 108 us; the launch traced here: 107 us
  Pallas kernels  56.3 us (52%)
  starting transfers between devices  40.5 us (38%)
  local copies, waits for them, and re-layouts  5.45 us (5%)
  waiting for transfers between devices  4.18 us (4%)
    all_to_all x4, starting transfers between devices, exchange(): return lax.all_to_all(value, axis, split_axis=0, concat_axis=0, tiled=True)  30.7 us
    pallas_call x1, Pallas kernels, shards(): pl.pallas_call(update_body, out_shape=jax.ShapeDtypeStruct(phi.shape, f32...  16.7 us
    pallas_call x1, Pallas kernels, shards(): pl.pallas_call(fields_body, out_shape=(jax.ShapeDtypeStruct((9, 17, 24, d...  14.8 us
    ppermute x4, starting transfers between devices, shifted(): return lax.ppermute(value, axis, pairs)  9.89 us
    pallas_call x1, Pallas kernels, shards(): call(scatter_body, [((4, wx, wy, depth), f32), ((8, cap, 128), f32), ((3,...  6.53 us
    pallas_call x1, Pallas kernels, shards(): call(blend_inner_body, [((4, cap, 128), f32)], [SCALARS] + [WHOLE] * 3, [...  6.24 us
    unnamed x16, local copies, waits for them, and re-layouts  5.45 us
    pallas_call x1, Pallas kernels, shards(): pl.pallas_call(local_body, out_shape=jax.ShapeDtypeStruct((4, wx, wy, dep...  4.58 us
  transfers between devices with their start and end apart: 8, of which 2 were waited for; matrix products, arithmetic and copies ran while one was open for 0% of the time, Pallas kernels for 34%

profile of v2, /device:TPU:1, one launch (start us, length us, event | category | flops | bytes accessed | tf_op | source)
XLA Modules:
  0.0 107.4 jit_solution(3701709090062576359)
XLA Ops:
  0.6 0.0 copy-start.2
  0.6 4.1 %dispatch.1 = (f32[128,4,128]{2,1,0:T(4,128)}, s32[1,2048]{1,0:T(1,128)}) custom-call(s32[1,2048]{1,0:T(1,128)} %bitcast.8, s32[1,2048]{1,0:T(1,128)} %bitcast.10, f32[4,2048]{1,0:T(4,128)} %phi_ref.3, f32[3,2048]{1,0:T(4,128)} %off_ref.2), custom_call_target="tpu_custom_call" | custom-call | tf_op jit(solution)/shard_map/dispatch/pallas_call | solution.py:641
  4.7 11.5 %all-to-all-start = ((f32[128,4,128]{2,1,0:T(4,128)}), f32[128,4,128]{2,1,0:T(4,128)S(1)}, u32[]{:S(2)}, u32[]{:S(2)}) async-start(f32[128,4,128]{2,1,0:T(4,128)} %get-tuple-element.24), calls=%async_computation | async-start | bytes 524288 | tf_op jit(solution)/shard_map/all_to_all | solution.py:629
  16.2 0.0 copy-start.4
  16.2 1.0 copy-done.4
  17.2 0.9 copy-done.5
  18.1 1.1 %pencil_x.1 = f32[16,24,512]{2,1,0:T(8,128)} custom-call(f32[3,8,16,256]{3,2,1,0:T(8,128)S(1)} %bitcast.6, f32[8,16,256]{2,1,0:T(8,128)S(1)} %bitcast.7), custom_call_target="tpu_custom_call" | custom-call | tf_op jit(solution)/shard_map/pencil_x/pallas_call | solution.py:650
  19.2 4.6 %local_sum.1.local_ref = f32[4,16,16,128]{3,2,1,0:T(8,128)} custom-call(f32[4,16,16,16,128]{4,3,2,1,0:T(8,128)} %phi_ref.5, s32[16,16,128]{2,1,0:T(8,128)} %count_ref.5), custom_call_target="tpu_custom_call" | custom-call | flops 4000000 | bytes 9000000 | tf_op jit(solution)/shard_map/local_sum/pallas_call | solution.py:659
  23.8 3.3 %all-to-all-done.arr_ref = f32[128,4,128]{2,1,0:T(4,128)S(1)} async-done(((f32[128,4,128]{2,1,0:T(4,128)}), f32[128,4,128]{2,1,0:T(4,128)S(1)}, u32[]{:S(2)}, u32[]{:S(2)}) %all-to-all-start) | async-done | bytes 262176 | tf_op jit(solution)/shard_map/all_to_all | solution.py:629
  27.1 3.6 %all-to-all-start.1 = ((f32[16,24,512]{2,1,0:T(8,128)}), f32[16,24,512]{2,1,0:T(8,128)S(1)}, u32[]{:S(2)}, u32[]{:S(2)}) async-start(f32[16,24,512]{2,1,0:T(8,128)} %pencil_x.1), calls=%async_computation.1 | async-start | bytes 1572864 | tf_op jit(solution)/shard_map/all_to_all | solution.py:629
  30.8 1.0 copy-done.3
  31.8 6.5 %scatter.1 = (f32[4,16,16,128]{3,2,1,0:T(8,128)S(1)}, f32[8,64,128]{2,1,0:T(8,128)S(1)}, s32[3,128]{1,0:T(4,128)S(1)}, f32[4,1,16,128]{3,2,1,0:T(8,128)S(1)}, f3...) custom-call(f32[128,4,128]{2,1,0:T(4,128)S(1)} %all-to-all-done.arr_ref, ...), custom_call_target="tpu_custom_call" | custom-call | flops 4000000000 | bytes 2000000 | tf_op jit(solution)/shard_map/scatter/pallas_call | solution.py:672
  38.3 3.1 %collective-permute-start.1 = (f32[4,1,16,128]{3,2,1,0:T(8,128)S(1)}, f32[4,1,16,128]{3,2,1,0:T(8,128)S(1)}, u32[]{:S(2)}, u32[]{:S(2)}) collective-permute-start(f32[4,1,16,128]{3,2,1,0:T(8,128)S(1)} %get-tuple-element.35), channel_id=1, source_target_pairs={{0,8},{8,16},{16,24},{24,32},{32,40},{40,48},{48,56},{56,64},{64,7... | collective-permute-start | bytes 98312 | tf_op jit(solution)/shard_map/ppermute | solution.py:625
  41.5 1.3 %collective-permute-start = (f32[4,2,16,128]{3,2,1,0:T(8,128)S(1)}, f32[4,2,16,128]{3,2,1,0:T(8,128)S(1)}, u32[]{:S(2)}, u32[]{:S(2)}) collective-permute-start(f32[4,2,16,128]{3,2,1,0:T(8,128)S(1)} %get-tuple-element.32), channel_id=1, source_target_pairs={{8,0},{16,8},{24,16},{32,24},{40,32},{48,40},{56,48},{64,56},{72,6... | collective-permute-start | bytes 196616 | tf_op jit(solution)/shard_map/ppermute | solution.py:625
  42.8 0.1 add_convert_fusion.last_ref
  42.9 0.8 all-to-all-done.1.in_ref
  43.7 1.0 pencil_y.1
  44.7 6.9 %all-to-all-start.2 = ((f32[8,16,1280]{2,1,0:T(8,128)}), f32[8,16,1280]{2,1,0:T(8,128)S(1)}, u32[]{:S(2)}, u32[]{:S(2)}) async-start(f32[8,16,1280]{2,1,0:T(8,128)} %pencil_y.1), calls=%async_computation.2 | async-start | bytes 1310720 | tf_op jit(solution)/shard_map/all_to_all | solution.py:629
  51.6 0.0 collective-permute-done.hi_ref
  51.6 3.5 %collective-permute-start.2 = (f32[4,24,128]{2,1,0:T(8,128)S(1)}, f32[4,24,128]{2,1,0:T(8,128)S(1)}, u32[]{:S(2)}, u32[]{:S(2)}) collective-permute-start(f32[4,24,128]{2,1,0:T(8,128)S(1)} %get-tuple-element.39), channel_id=1, source_target_pairs={{0,1},{1,2},{2,3},{3,4},{4,5},{5,6},{6,7},{8,9},{9,10},{10,11},{11... | collective-permute-start | bytes 147464 | tf_op jit(solution)/shard_map/ppermute | solution.py:625
  55.2 1.9 %collective-permute-start.3 = (f32[2,4,24,128]{3,2,1,0:T(8,128)S(1)}, f32[2,4,24,128]{3,2,1,0:T(8,128)S(1)}, u32[]{:S(2)}, u32[]{:S(2)}) collective-permute-start(f32[2,4,24,128]{3,2,1,0:T(8,128)S(1)} %get-tuple-element.40), channel_id=1, source_target_pairs={{1,0},{2,1},{3,2},{4,3},{5,4},{6,5},{7,6},{9,8},{10,9},{11,10},{12... | collective-permute-start | bytes 294920 | tf_op jit(solution)/shard_map/ppermute | solution.py:625
  57.1 6.2 %blend_inner.1.inner_ref = f32[4,64,128]{2,1,0:T(8,128)S(1)} custom-call(s32[3,128]{1,0:T(4,128)S(1)} %get-tuple-element.27.bound_ref, f32[4,16,16,128]{3,2,1,0:T(8,128)S(1)} %get-tuple-element.31.mean_ref, f32[4,2,16,128]{3,2,1,0:T(8,128)S(1)} %collective-permute-done.hi_ref, f32[8,64,128]{2,1,0:T(8,128)S(1)} %get-tuple-element.33.xs_ref), custom_call_target="tpu_custom_call" | custom-call | flops 8000000000 | bytes 3000000 | tf_op jit(solution)/shard_map/blend_inner/pallas_call | solution.py:707
  63.3 0.0 all-to-all-done.2.wide_ref
  63.4 0.0 collective-permute-done.3.yhi_ref
  63.4 14.8 %fields.1 = (f32[9,17,24,128]{3,2,1,0:T(8,128)S(1)}, f32[9,17,24,128]{3,2,1,0:T(8,128)S(1)}, f32[128,2,128]{2,1,0:T(2,128)}) custom-call(s32[2]{0:T(128)S(1)} %add_convert_fusion.last_ref, s32[3,128]{1,0:T(4,128)S(1)} %get-tuple-element.27.bound_ref, f32[8,16,1280]{2,1,0:T(8,128)S(1)} %all-to-all-done.2.wide_ref, ...), custom_call_target="tpu_custom_call" | custom-call | tf_op jit(solution)/shard_map/fields/pallas_call | solution.py:723
  78.2 1.3 %copy-done = f32[9,17,24,128]{3,2,1,0:T(8,128)} copy-done((f32[9,17,24,128]{3,2,1,0:T(8,128)}, f32[9,17,24,128]{3,2,1,0:T(8,128)S(1)}, u32[]{:S(2)}) %copy-start) | copy-done | bytes 1880088
  79.5 1.2 %copy-done.1 = f32[9,17,24,128]{3,2,1,0:T(8,128)} copy-done((f32[9,17,24,128]{3,2,1,0:T(8,128)}, f32[9,17,24,128]{3,2,1,0:T(8,128)S(1)}, u32[]{:S(2)}) %copy-start.1) | copy-done | bytes 1880088
  80.7 8.7 %all-to-all-start.3 = ((f32[128,2,128]{2,1,0:T(2,128)}), f32[128,2,128]{2,1,0:T(2,128)S(1)}, u32[]{:S(2)}, u32[]{:S(2)}) async-start(f32[128,2,128]{2,1,0:T(2,128)} %get-tuple-element.45), calls=%async_computation.3 | async-start | bytes 262144 | tf_op jit(solution)/shard_map/all_to_all | solution.py:629
  89.4 0.0 copy-start.6
  89.4 0.0 copy-start.7
  89.4 16.7 %update.1 = f32[4,16,16,16,128]{4,3,2,1,0:T(8,128)} custom-call(f32[4,16,16,16,128]{4,3,2,1,0:T(8,128)} %phi_ref.5, f32[3,16,16,16,128]{4,3,2,1,0:T(8,128)} %off_ref.3, s32[16,16,128]{2,1,0:T(8,128)} %count_ref.5, f32[9,17,24,128]{3,2,1,0:T(8,128)} %copy-done, f32[9,17,24,128]{3,2,1,0:T(8,128)} %copy-done.1), custom_call_target="tpu_custom_call" | custom-call | flops 80000000 | bytes 25000000 | tf_op jit(solution)/shard_map/update/pallas_call | solution.py:747
  106.1 1.2 %collect.1 = f32[4,2048]{1,0:T(4,128)} custom-call(s32[1,2048]{1,0:T(1,128)S(1)} %bitcast.9, s32[1,2048]{1,0:T(1,128)S(1)} %copy-done.7, f32[128,2,128]{2,1,0:T(2,128)S(1)} %all-to-all-done.3.back_ref), custom_call_target="tpu_custom_call" | custom-call | tf_op jit(solution)/shard_map/collect/pallas_call | solution.py:759
  (11 shorter events, 0.0 us)
Async XLA Ops:
  0.6 30.1 %copy-start.2 = (s32[16,16,128]{2,1,0:T(8,128)S(1)}, s32[16,16,128]{2,1,0:T(8,128)}, u32[]{:S(2)}) copy-start(s32[16,16,128]{2,1,0:T(8,128)} %count_ref.5) | copy-start | bytes 393220
  4.7 22.4 %all-to-all-start = ((f32[128,4,128]{2,1,0:T(4,128)}), f32[128,4,128]{2,1,0:T(4,128)S(1)}, u32[]{:S(2)}, u32[]{:S(2)}) async-start(f32[128,4,128]{2,1,0:T(4,128)} %get-tuple-element.24), calls=%async_computation | async-start | bytes 524288 | tf_op jit(solution)/shard_map/all_to_all | solution.py:629
  16.2 1.0 copy-start.4
  17.2 0.9 copy-start.5
  27.1 16.6 %all-to-all-start.1 = ((f32[16,24,512]{2,1,0:T(8,128)}), f32[16,24,512]{2,1,0:T(8,128)S(1)}, u32[]{:S(2)}, u32[]{:S(2)}) async-start(f32[16,24,512]{2,1,0:T(8,128)} %pencil_x.1), calls=%async_computation.1 | async-start | bytes 1572864 | tf_op jit(solution)/shard_map/all_to_all | solution.py:629
  30.8 1.0 copy-start.3
  38.3 13.2 %collective-permute-start.1 = (f32[4,1,16,128]{3,2,1,0:T(8,128)S(1)}, f32[4,1,16,128]{3,2,1,0:T(8,128)S(1)}, u32[]{:S(2)}, u32[]{:S(2)}) collective-permute-start(f32[4,1,16,128]{3,2,1,0:T(8,128)S(1)} %get-tuple-element.35), channel_id=1, source_target_pairs={{0,8},{8,16},{16,24},{24,32},{32,40},{40,48},{48,56},{56,64},{64,7... | collective-permute-start | bytes 98312 | tf_op jit(solution)/shard_map/ppermute | solution.py:625
  41.5 10.1 %collective-permute-start = (f32[4,2,16,128]{3,2,1,0:T(8,128)S(1)}, f32[4,2,16,128]{3,2,1,0:T(8,128)S(1)}, u32[]{:S(2)}, u32[]{:S(2)}) collective-permute-start(f32[4,2,16,128]{3,2,1,0:T(8,128)S(1)} %get-tuple-element.32), channel_id=1, source_target_pairs={{8,0},{16,8},{24,16},{32,24},{40,32},{48,40},{56,48},{64,56},{72,6... | collective-permute-start | bytes 196616 | tf_op jit(solution)/shard_map/ppermute | solution.py:625
  44.7 18.6 %all-to-all-start.2 = ((f32[8,16,1280]{2,1,0:T(8,128)}), f32[8,16,1280]{2,1,0:T(8,128)S(1)}, u32[]{:S(2)}, u32[]{:S(2)}) async-start(f32[8,16,1280]{2,1,0:T(8,128)} %pencil_y.1), calls=%async_computation.2 | async-start | bytes 1310720 | tf_op jit(solution)/shard_map/all_to_all | solution.py:629
  51.6 11.7 %collective-permute-start.2 = (f32[4,24,128]{2,1,0:T(8,128)S(1)}, f32[4,24,128]{2,1,0:T(8,128)S(1)}, u32[]{:S(2)}, u32[]{:S(2)}) collective-permute-start(f32[4,24,128]{2,1,0:T(8,128)S(1)} %get-tuple-element.39), channel_id=1, source_target_pairs={{0,1},{1,2},{2,3},{3,4},{4,5},{5,6},{6,7},{8,9},{9,10},{10,11},{11... | collective-permute-start | bytes 147464 | tf_op jit(solution)/shard_map/ppermute | solution.py:625
  55.2 8.2 %collective-permute-start.3 = (f32[2,4,24,128]{3,2,1,0:T(8,128)S(1)}, f32[2,4,24,128]{3,2,1,0:T(8,128)S(1)}, u32[]{:S(2)}, u32[]{:S(2)}) collective-permute-start(f32[2,4,24,128]{3,2,1,0:T(8,128)S(1)} %get-tuple-element.40), channel_id=1, source_target_pairs={{1,0},{2,1},{3,2},{4,3},{5,4},{6,5},{7,6},{9,8},{10,9},{11,10},{12... | collective-permute-start | bytes 294920 | tf_op jit(solution)/shard_map/ppermute | solution.py:625
  78.2 1.3 %copy-start = (f32[9,17,24,128]{3,2,1,0:T(8,128)}, f32[9,17,24,128]{3,2,1,0:T(8,128)S(1)}, u32[]{:S(2)}) copy-start(f32[9,17,24,128]{3,2,1,0:T(8,128)S(1)} %get-tuple-element.42.f_ref) | copy-start | bytes 5640196
  79.5 1.2 %copy-start.1 = (f32[9,17,24,128]{3,2,1,0:T(8,128)}, f32[9,17,24,128]{3,2,1,0:T(8,128)S(1)}, u32[]{:S(2)}) copy-start(f32[9,17,24,128]{3,2,1,0:T(8,128)S(1)} %get-tuple-element.43.rise_ref) | copy-start | bytes 5640196
  80.7 25.4 %all-to-all-start.3 = ((f32[128,2,128]{2,1,0:T(2,128)}), f32[128,2,128]{2,1,0:T(2,128)S(1)}, u32[]{:S(2)}, u32[]{:S(2)}) async-start(f32[128,2,128]{2,1,0:T(2,128)} %get-tuple-element.45), calls=%async_computation.3 | async-start | bytes 262144 | tf_op jit(solution)/shard_map/all_to_all | solution.py:629
  89.4 16.7 %copy-start.6 = (s32[2048,1]{0,1:T(1,128)S(1)}, s32[2048,1]{0,1:T(1,128)}, u32[]{:S(2)}) copy-start(s32[2048,1]{0,1:T(1,128)} %param.16) | copy-start | bytes 24580
  89.4 16.7 %copy-start.7 = (s32[1,2048]{1,0:T(1,128)S(1)}, s32[1,2048]{1,0:T(1,128)}, u32[]{:S(2)}) copy-start(s32[1,2048]{1,0:T(1,128)} %get-tuple-element.44.rank_ref) | copy-start | bytes 24580

commit v3 on v2

--- a/solution.py
+++ b/solution.py
@@ -563,28 +563,36 @@
 
 def fields_body(
     last_ref, bound_ref, wide_ref, mean_ref, lo_ref, hi_ref, ylo_ref, yhi_ref, inner_ref, xs_ref,
-    f_ref, rise_ref, out_ref,
-    brick_ref, col_ref, tall_ref, mp_ref, gp_ref, tab_ref, lhs_ref, new_ref,
+    both_ref, out_ref,
+    f_ref, rise_ref, brick_ref, col_ref, tall_ref, mp_ref, gp_ref, tab_ref, lhs_ref, new_ref, sems,
 ):
     brick_part(wide_ref, brick_ref, col_ref, tall_ref)
     transport_part(
         last_ref, mean_ref, lo_ref, hi_ref, ylo_ref, yhi_ref, brick_ref, col_ref, f_ref, rise_ref, mp_ref, gp_ref
     )
+    first = pltpu.make_async_copy(f_ref, both_ref.at[0], sems.at[0])
+    second = pltpu.make_async_copy(rise_ref, both_ref.at[1], sems.at[1])
+    first.start()
+    second.start()
     outer_part(bound_ref, f_ref, inner_ref, xs_ref, out_ref, tab_ref, lhs_ref, new_ref)
-
-
-def update_body(phi_ref, off_ref, count_ref, f_ref, rise_ref, out_ref, coef_ref):
+    first.wait()
+    second.wait()
+
+
+def update_body(
+    phi_ref, off_ref, count_ref, f_ref, f_next_ref, rise_ref, rise_next_ref, out_ref, coef_ref
+):
     deep, wy = count_ref.shape[0], count_ref.shape[1]
-    first = pl.program_id(0) * deep
     slots = phi_ref.shape[1]
     width = 4
     for x in range(deep):
         for ch in range(9):
-            for sz, ref in enumerate((f_ref, rise_ref)):
-                c00 = ref[ch, first + x, 0:wy, :]
-                c01 = ref[ch, first + x, 1 : wy + 1, :]
-                c10 = ref[ch, first + x + 1, 0:wy, :]
-                c11 = ref[ch, first + x + 1, 1 : wy + 1, :]
+            for sz, (ref, after) in enumerate(((f_ref, f_next_ref), (rise_ref, rise_next_ref))):
+                high, k = (ref, x + 1) if x + 1 < deep else (after, 0)
+                c00 = ref[ch, x, 0:wy, :]
+                c01 = ref[ch, x, 1 : wy + 1, :]
+                c10 = high[ch, k, 0:wy, :]
+                c11 = high[ch, k, 1 : wy + 1, :]
                 dx = c10 - c00
                 coef_ref[ch, sz] = c00
                 coef_ref[ch, 2 + sz] = c01 - c00
@@ -662,7 +670,7 @@
         grid=(wx // 8,),
         in_specs=[blocks(4, 8), cells(8)],
         out_specs=pl.BlockSpec((4, 8, wy, depth), lambda i: (0, i, 0, 0)),
-        compiler_params=pltpu.CompilerParams(vmem_limit_bytes=54 * MB),
+        compiler_params=pltpu.CompilerParams(vmem_limit_bytes=40 * MB),
         cost_estimate=pl.CostEstimate(flops=4 * 10**6, bytes_accessed=9 * 10**6, transcendentals=0),
         name="local_sum",
     )(phi, count)
@@ -720,16 +728,17 @@
             (lax.axis_index("yz") == groups_y - 1).astype(jnp.int32),
         ]
     )
-    fields, rises, moved_new = pl.pallas_call(
+    both, moved_new = pl.pallas_call(
         fields_body,
         out_shape=(
-            jax.ShapeDtypeStruct((9, 17, 24, depth), f32),
-            jax.ShapeDtypeStruct((9, 17, 24, depth), f32),
+            jax.ShapeDtypeStruct((8, 9, 17, 24, depth), f32),
             jax.ShapeDtypeStruct((bricks, 2, 128), f32),
         ),
         in_specs=[SCALARS] * 2 + [WHOLE] * 8,
-        out_specs=(WHOLE, WHOLE, WHOLE),
+        out_specs=(pl.BlockSpec(memory_space=pl.ANY), WHOLE),
         scratch_shapes=[
+            pltpu.VMEM((9, 17, 24, depth), f32),
+            pltpu.VMEM((9, 17, 24, depth), f32),
             pltpu.VMEM((4, 19, wy, depth), f32),
             pltpu.VMEM((4, 3, 24, depth), f32),
             pltpu.VMEM((4 * 16 * 24, 128), f32),
@@ -738,23 +747,30 @@
             pltpu.VMEM((2304, 128), f32),
             pltpu.VMEM((2304, 384), bf16),
             pltpu.VMEM((4, cap, 128), f32),
+            pltpu.SemaphoreType.DMA((2,)),
         ],
-        compiler_params=pltpu.CompilerParams(vmem_limit_bytes=28 * MB),
+        compiler_params=pltpu.CompilerParams(vmem_limit_bytes=48 * MB),
         name="fields",
     )(last, bound, wide, mean, lo, hi, ylo, yhi, inner, xs)
     back = exchange(moved_new, ("gx", "yz"))
+
+    def planes(entry):
+        return (
+            pl.BlockSpec((None, 9, 2, 24, depth), lambda i: (entry, 0, i, 0, 0)),
+            pl.BlockSpec((None, 9, 1, 24, depth), lambda i: (entry, 0, 2 * i + 2, 0, 0)),
+        )
 
     particle_new = pl.pallas_call(
         update_body,
         out_shape=jax.ShapeDtypeStruct(phi.shape, f32),
         grid=(wx // 2,),
-        in_specs=[blocks(4, 2), blocks(3, 2), cells(2), WHOLE, WHOLE],
+        in_specs=[blocks(4, 2), blocks(3, 2), cells(2), *planes(0), *planes(1)],
         out_specs=blocks(4, 2),
         scratch_shapes=[pltpu.VMEM((9, 8, wy, depth), f32)],
-        compiler_params=pltpu.CompilerParams(vmem_limit_bytes=54 * MB),
+        compiler_params=pltpu.CompilerParams(vmem_limit_bytes=60 * MB),
         cost_estimate=pl.CostEstimate(flops=8 * 10**7, bytes_accessed=25 * 10**6, transcendentals=0),
         name="update",
-    )(phi, offset, count, fields, rises)
+    )(phi, offset, count, both, both, both, both)
 
     migrant_new, = call(
         functools.partial(collect_body, bricks=bricks, cap=cap),

time: 108 us -> 105 us (0.972)
  Pallas kernels: 56.3 us -> 52.7 us
    pallas_call x1, Pallas kernels: 4.58 us -> 1.34 us  [shards(): pl.pallas_call(local_body, out_shape=jax.ShapeDtypeStruct((4, wx, wy, dep...]
    unnamed x16 -> x14, local copies, waits for them, and re-layouts: 5.45 us -> 6.2 us
  transfers between devices with their start and end apart: 8 -> 8, of which waited for: 2 -> 2; matrix products, arithmetic and copies ran while one was open for 0% -> 0% of each run, Pallas kernels for 34% -> 31%
where the time goes in v3:
time: 105 us; the launch traced here: 104 us
  Pallas kernels  52.7 us (50%)
  starting transfers between devices  40.1 us (38%)
  local copies, waits for them, and re-layouts  6.2 us (6%)
  waiting for transfers between devices  4.59 us (4%)
    all_to_all x4, starting transfers between devices, exchange(): return lax.all_to_all(value, axis, split_axis=0, concat_axis=0, tiled=True)  30.1 us
    pallas_call x1, Pallas kernels, shards(): pl.pallas_call(update_body, out_shape=jax.ShapeDtypeStruct(phi.shape, f32...  16.3 us
    pallas_call x1, Pallas kernels, shards(): pl.pallas_call(fields_body, out_shape=(jax.ShapeDtypeStruct((8, 9, 17, 24...  14.8 us
    ppermute x4, starting transfers between devices, shifted(): return lax.ppermute(value, axis, pairs)  10 us
    pallas_call x1, Pallas kernels, shards(): call(scatter_body, [((4, wx, wy, depth), f32), ((8, cap, 128), f32), ((3,...  6.55 us
    pallas_call x1, Pallas kernels, shards(): call(blend_inner_body, [((4, cap, 128), f32)], [SCALARS] + [WHOLE] * 3, [...  6.24 us
    unnamed x14, local copies, waits for them, and re-layouts  6.2 us
    all_to_all x4, waiting for transfers between devices, exchange(): return lax.all_to_all(value, axis, split_axis=0, concat_axis=0, tiled=True)  4.58 us
  transfers between devices with their start and end apart: 8, of which 2 were waited for; matrix products, arithmetic and copies ran while one was open for 0% of the time, Pallas kernels for 31%

profile of v3, /device:TPU:1, one launch (start us, length us, event | category | flops | bytes accessed | tf_op | source)
XLA Modules:
  0.0 104.5 jit_solution(2502284533854541944)
XLA Ops:
  0.6 0.0 copy-start.2
  0.6 4.1 %dispatch.1 = (f32[128,4,128]{2,1,0:T(4,128)}, s32[1,2048]{1,0:T(1,128)}) custom-call(s32[1,2048]{1,0:T(1,128)} %bitcast.8, s32[1,2048]{1,0:T(1,128)} %bitcast.10, f32[4,2048]{1,0:T(4,128)} %phi_ref.3, f32[3,2048]{1,0:T(4,128)} %off_ref.2), custom_call_target="tpu_custom_call" | custom-call | tf_op jit(solution)/shard_map/dispatch/pallas_call | solution.py:649
  4.7 11.5 %all-to-all-start = ((f32[128,4,128]{2,1,0:T(4,128)}), f32[128,4,128]{2,1,0:T(4,128)S(1)}, u32[]{:S(2)}, u32[]{:S(2)}) async-start(f32[128,4,128]{2,1,0:T(4,128)} %get-tuple-element.23), calls=%async_computation | async-start | bytes 524288 | tf_op jit(solution)/shard_map/all_to_all | solution.py:637
  16.2 0.0 copy-start.3
  16.2 1.0 copy-done.3
  17.2 0.9 copy-done.4
  18.1 1.1 %pencil_x.1 = f32[16,24,512]{2,1,0:T(8,128)} custom-call(f32[3,8,16,256]{3,2,1,0:T(8,128)S(1)} %bitcast.6, f32[8,16,256]{2,1,0:T(8,128)S(1)} %bitcast.7), custom_call_target="tpu_custom_call" | custom-call | tf_op jit(solution)/shard_map/pencil_x/pallas_call | solution.py:658
  19.2 3.4 %copy-done = f32[4,16,16,16,128]{4,3,2,1,0:T(8,128)S(1)} copy-done((f32[4,16,16,16,128]{4,3,2,1,0:T(8,128)S(1)}, f32[4,16,16,16,128]{4,3,2,1,0:T(8,128)}, u32[]{:S(2)}) %copy-start) | copy-done | bytes 8388632
  22.6 0.9 copy-done.1
  23.5 1.3 %local_sum.1.local_ref = f32[4,16,16,128]{3,2,1,0:T(8,128)S(1)} custom-call(f32[4,16,16,16,128]{4,3,2,1,0:T(8,128)S(1)} %copy-done, s32[16,16,128]{2,1,0:T(8,128)S(1)} %copy-done.1), custom_call_target="tpu_custom_call" | custom-call | flops 4000000 | bytes 9000000 | tf_op jit(solution)/shard_map/local_sum/pallas_call | solution.py:667
  24.9 2.3 %all-to-all-done.arr_ref = f32[128,4,128]{2,1,0:T(4,128)S(1)} async-done(((f32[128,4,128]{2,1,0:T(4,128)}), f32[128,4,128]{2,1,0:T(4,128)S(1)}, u32[]{:S(2)}, u32[]{:S(2)}) %all-to-all-start) | async-done | bytes 262176 | tf_op jit(solution)/shard_map/all_to_all | solution.py:637
  27.1 4.5 %all-to-all-start.1 = ((f32[16,24,512]{2,1,0:T(8,128)}), f32[16,24,512]{2,1,0:T(8,128)S(1)}, u32[]{:S(2)}, u32[]{:S(2)}) async-start(f32[16,24,512]{2,1,0:T(8,128)} %pencil_x.1), calls=%async_computation.1 | async-start | bytes 1572864 | tf_op jit(solution)/shard_map/all_to_all | solution.py:637
  31.6 6.5 %scatter.1 = (f32[4,16,16,128]{3,2,1,0:T(8,128)S(1)}, f32[8,64,128]{2,1,0:T(8,128)S(1)}, s32[3,128]{1,0:T(4,128)S(1)}, f32[4,1,16,128]{3,2,1,0:T(8,128)S(1)}, f3...) custom-call(f32[128,4,128]{2,1,0:T(4,128)S(1)} %all-to-all-done.arr_ref, ...), custom_call_target="tpu_custom_call" | custom-call | flops 4000000000 | bytes 2000000 | tf_op jit(solution)/shard_map/scatter/pallas_call | solution.py:680
  38.2 3.3 %collective-permute-start.1 = (f32[4,1,16,128]{3,2,1,0:T(8,128)S(1)}, f32[4,1,16,128]{3,2,1,0:T(8,128)S(1)}, u32[]{:S(2)}, u32[]{:S(2)}) collective-permute-start(f32[4,1,16,128]{3,2,1,0:T(8,128)S(1)} %get-tuple-element.34), channel_id=1, source_target_pairs={{0,8},{8,16},{16,24},{24,32},{32,40},{40,48},{48,56},{56,64},{64,7... | collective-permute-start | bytes 98312 | tf_op jit(solution)/shard_map/ppermute | solution.py:633
  41.4 1.3 %collective-permute-start = (f32[4,2,16,128]{3,2,1,0:T(8,128)S(1)}, f32[4,2,16,128]{3,2,1,0:T(8,128)S(1)}, u32[]{:S(2)}, u32[]{:S(2)}) collective-permute-start(f32[4,2,16,128]{3,2,1,0:T(8,128)S(1)} %get-tuple-element.31), channel_id=1, source_target_pairs={{8,0},{16,8},{24,16},{32,24},{40,32},{48,40},{56,48},{64,56},{72,6... | collective-permute-start | bytes 196616 | tf_op jit(solution)/shard_map/ppermute | solution.py:633
  42.7 0.1 add_convert_fusion.last_ref
  42.8 2.3 %all-to-all-done.1.in_ref = f32[16,24,512]{2,1,0:T(8,128)S(1)} async-done(((f32[16,24,512]{2,1,0:T(8,128)}), f32[16,24,512]{2,1,0:T(8,128)S(1)}, u32[]{:S(2)}, u32[]{:S(2)}) %all-to-all-start.1) | async-done | bytes 786464 | tf_op jit(solution)/shard_map/all_to_all | solution.py:637
  45.1 1.0 pencil_y.1
  46.1 6.5 %all-to-all-start.2 = ((f32[8,16,1280]{2,1,0:T(8,128)}), f32[8,16,1280]{2,1,0:T(8,128)S(1)}, u32[]{:S(2)}, u32[]{:S(2)}) async-start(f32[8,16,1280]{2,1,0:T(8,128)} %pencil_y.1), calls=%async_computation.2 | async-start | bytes 1310720 | tf_op jit(solution)/shard_map/all_to_all | solution.py:637
  52.7 0.0 collective-permute-done.1.lo_ref
  52.7 3.5 %collective-permute-start.2 = (f32[4,24,128]{2,1,0:T(8,128)S(1)}, f32[4,24,128]{2,1,0:T(8,128)S(1)}, u32[]{:S(2)}, u32[]{:S(2)}) collective-permute-start(f32[4,24,128]{2,1,0:T(8,128)S(1)} %get-tuple-element.38), channel_id=1, source_target_pairs={{0,1},{1,2},{2,3},{3,4},{4,5},{5,6},{6,7},{8,9},{9,10},{10,11},{11... | collective-permute-start | bytes 147464 | tf_op jit(solution)/shard_map/ppermute | solution.py:633
  56.3 1.9 %collective-permute-start.3 = (f32[2,4,24,128]{3,2,1,0:T(8,128)S(1)}, f32[2,4,24,128]{3,2,1,0:T(8,128)S(1)}, u32[]{:S(2)}, u32[]{:S(2)}) collective-permute-start(f32[2,4,24,128]{3,2,1,0:T(8,128)S(1)} %get-tuple-element.39), channel_id=1, source_target_pairs={{1,0},{2,1},{3,2},{4,3},{5,4},{6,5},{7,6},{9,8},{10,9},{11,10},{12... | collective-permute-start | bytes 294920 | tf_op jit(solution)/shard_map/ppermute | solution.py:633
  58.2 6.2 %blend_inner.1.inner_ref = f32[4,64,128]{2,1,0:T(8,128)S(1)} custom-call(s32[3,128]{1,0:T(4,128)S(1)} %get-tuple-element.26.bound_ref, f32[4,16,16,128]{3,2,1,0:T(8,128)S(1)} %get-tuple-element.30.mean_ref, f32[4,2,16,128]{3,2,1,0:T(8,128)S(1)} %collective-permute-done.hi_ref, f32[8,64,128]{2,1,0:T(8,128)S(1)} %get-tuple-element.32.xs_ref), custom_call_target="tpu_custom_call" | custom-call | flops 8000000000 | bytes 3000000 | tf_op jit(solution)/shard_map/blend_inner/pallas_call | solution.py:715
  64.4 0.0 collective-permute-done.2.ylo_ref
  64.4 0.0 collective-permute-done.3.yhi_ref
  64.5 14.8 %fields.1 = (f32[8,9,17,24,128]{4,3,2,1,0:T(8,128)}, f32[128,2,128]{2,1,0:T(2,128)}) custom-call(s32[2]{0:T(128)S(1)} %add_convert_fusion.last_ref, s32[3,128]{1,0:T(4,128)S(1)} %get-tuple-element.26.bound_ref, f32[8,16,1280]{2,1,0:T(8,128)S(1)} %all-to-all-done.2.wide_ref, f32[4,16,16,128]{3,2,1,0:T(8,128)S(1)} %get-tuple-element.30.mean_ref, ...), custom_call_target="tpu_custom_call" | custom-call | tf_op jit(solution)/shard_map/fields/pallas_call | solution.py:731
  79.3 7.6 %all-to-all-start.3 = ((f32[128,2,128]{2,1,0:T(2,128)}), f32[128,2,128]{2,1,0:T(2,128)S(1)}, u32[]{:S(2)}, u32[]{:S(2)}) async-start(f32[128,2,128]{2,1,0:T(2,128)} %get-tuple-element.43), calls=%async_computation.3 | async-start | bytes 262144 | tf_op jit(solution)/shard_map/all_to_all | solution.py:637
  86.9 0.0 copy-start.5
  86.9 0.0 copy-start.6
  86.9 16.3 %update.1 = f32[4,16,16,16,128]{4,3,2,1,0:T(8,128)} custom-call(f32[4,16,16,16,128]{4,3,2,1,0:T(8,128)} %phi_ref.5, f32[3,16,16,16,128]{4,3,2,1,0:T(8,128)} %off_ref.3, s32[16,16,128]{2,1,0:T(8,128)} %count_ref.5, f32[8,9,17,24,128]{4,3,2,1,0:T(8,128)} %get-tuple-element.41.f_ref.f_next_ref.rise_ref.rise_next_ref, ...), custom_call_target="tpu_custom_call" | custom-call | flops 80000000 | bytes 25000000 | tf_op jit(solution)/shard_map/update/pallas_call | solution.py:763
  103.2 0.0 all-to-all-done.3.back_ref
  103.2 1.2 %collect.1 = f32[4,2048]{1,0:T(4,128)} custom-call(s32[1,2048]{1,0:T(1,128)S(1)} %bitcast.9, s32[1,2048]{1,0:T(1,128)S(1)} %copy-done.6, f32[128,2,128]{2,1,0:T(2,128)S(1)} %all-to-all-done.3.back_ref), custom_call_target="tpu_custom_call" | custom-call | tf_op jit(solution)/shard_map/collect/pallas_call | solution.py:775
  (9 shorter events, 0.0 us)
Async XLA Ops:
  0.6 31.0 %copy-start.2 = (s32[16,16,128]{2,1,0:T(8,128)S(1)}, s32[16,16,128]{2,1,0:T(8,128)}, u32[]{:S(2)}) copy-start(s32[16,16,128]{2,1,0:T(8,128)} %count_ref.5) | copy-start | bytes 393220
  4.7 22.4 %all-to-all-start = ((f32[128,4,128]{2,1,0:T(4,128)}), f32[128,4,128]{2,1,0:T(4,128)S(1)}, u32[]{:S(2)}, u32[]{:S(2)}) async-start(f32[128,4,128]{2,1,0:T(4,128)} %get-tuple-element.23), calls=%async_computation | async-start | bytes 524288 | tf_op jit(solution)/shard_map/all_to_all | solution.py:637
  16.2 1.0 copy-start.3
  17.2 0.9 copy-start.4
  19.2 3.4 %copy-start = (f32[4,16,16,16,128]{4,3,2,1,0:T(8,128)S(1)}, f32[4,16,16,16,128]{4,3,2,1,0:T(8,128)}, u32[]{:S(2)}) copy-start(f32[4,16,16,16,128]{4,3,2,1,0:T(8,128)} %phi_ref.5) | copy-start | bytes 25165828
  22.6 0.9 copy-start.1
  27.1 18.0 %all-to-all-start.1 = ((f32[16,24,512]{2,1,0:T(8,128)}), f32[16,24,512]{2,1,0:T(8,128)S(1)}, u32[]{:S(2)}, u32[]{:S(2)}) async-start(f32[16,24,512]{2,1,0:T(8,128)} %pencil_x.1), calls=%async_computation.1 | async-start | bytes 1572864 | tf_op jit(solution)/shard_map/all_to_all | solution.py:637
  38.2 14.5 %collective-permute-start.1 = (f32[4,1,16,128]{3,2,1,0:T(8,128)S(1)}, f32[4,1,16,128]{3,2,1,0:T(8,128)S(1)}, u32[]{:S(2)}, u32[]{:S(2)}) collective-permute-start(f32[4,1,16,128]{3,2,1,0:T(8,128)S(1)} %get-tuple-element.34), channel_id=1, source_target_pairs={{0,8},{8,16},{16,24},{24,32},{32,40},{40,48},{48,56},{56,64},{64,7... | collective-permute-start | bytes 98312 | tf_op jit(solution)/shard_map/ppermute | solution.py:633
  41.4 11.2 %collective-permute-start = (f32[4,2,16,128]{3,2,1,0:T(8,128)S(1)}, f32[4,2,16,128]{3,2,1,0:T(8,128)S(1)}, u32[]{:S(2)}, u32[]{:S(2)}) collective-permute-start(f32[4,2,16,128]{3,2,1,0:T(8,128)S(1)} %get-tuple-element.31), channel_id=1, source_target_pairs={{8,0},{16,8},{24,16},{32,24},{40,32},{48,40},{56,48},{64,56},{72,6... | collective-permute-start | bytes 196616 | tf_op jit(solution)/shard_map/ppermute | solution.py:633
  46.1 18.3 %all-to-all-start.2 = ((f32[8,16,1280]{2,1,0:T(8,128)}), f32[8,16,1280]{2,1,0:T(8,128)S(1)}, u32[]{:S(2)}, u32[]{:S(2)}) async-start(f32[8,16,1280]{2,1,0:T(8,128)} %pencil_y.1), calls=%async_computation.2 | async-start | bytes 1310720 | tf_op jit(solution)/shard_map/all_to_all | solution.py:637
  52.7 11.7 %collective-permute-start.2 = (f32[4,24,128]{2,1,0:T(8,128)S(1)}, f32[4,24,128]{2,1,0:T(8,128)S(1)}, u32[]{:S(2)}, u32[]{:S(2)}) collective-permute-start(f32[4,24,128]{2,1,0:T(8,128)S(1)} %get-tuple-element.38), channel_id=1, source_target_pairs={{0,1},{1,2},{2,3},{3,4},{4,5},{5,6},{6,7},{8,9},{9,10},{10,11},{11... | collective-permute-start | bytes 147464 | tf_op jit(solution)/shard_map/ppermute | solution.py:633
  56.3 8.2 %collective-permute-start.3 = (f32[2,4,24,128]{3,2,1,0:T(8,128)S(1)}, f32[2,4,24,128]{3,2,1,0:T(8,128)S(1)}, u32[]{:S(2)}, u32[]{:S(2)}) collective-permute-start(f32[2,4,24,128]{3,2,1,0:T(8,128)S(1)} %get-tuple-element.39), channel_id=1, source_target_pairs={{1,0},{2,1},{3,2},{4,3},{5,4},{6,5},{7,6},{9,8},{10,9},{11,10},{12... | collective-permute-start | bytes 294920 | tf_op jit(solution)/shard_map/ppermute | solution.py:633
  79.3 23.9 %all-to-all-start.3 = ((f32[128,2,128]{2,1,0:T(2,128)}), f32[128,2,128]{2,1,0:T(2,128)S(1)}, u32[]{:S(2)}, u32[]{:S(2)}) async-start(f32[128,2,128]{2,1,0:T(2,128)} %get-tuple-element.43), calls=%async_computation.3 | async-start | bytes 262144 | tf_op jit(solution)/shard_map/all_to_all | solution.py:637
  86.9 16.3 %copy-start.5 = (s32[2048,1]{0,1:T(1,128)S(1)}, s32[2048,1]{0,1:T(1,128)}, u32[]{:S(2)}) copy-start(s32[2048,1]{0,1:T(1,128)} %param.16) | copy-start | bytes 24580
  86.9 16.3 %copy-start.6 = (s32[1,2048]{1,0:T(1,128)S(1)}, s32[1,2048]{1,0:T(1,128)}, u32[]{:S(2)}) copy-start(s32[1,2048]{1,0:T(1,128)} %get-tuple-element.42.rank_ref) | copy-start | bytes 24580

commit v4 on v3

--- a/solution.py
+++ b/solution.py
@@ -11,7 +11,7 @@
 mix_coeff = 0.5
 span = 8
 further = 4
-tiles_held = 8
+tiles_held = 16
 f32 = jnp.float32
 bf16 = jnp.bfloat16
 MB = 2**20
@@ -160,13 +160,13 @@
     spots = places(256, 128)
 
     def step(i, carry):
-        at = pl.multiple_of(i * 16, 16)
-        cell = xs_ref[7, pl.ds(at, 16), :].astype(jnp.int32) - 1
+        at = pl.multiple_of(i * 32, 32)
+        cell = xs_ref[7, pl.ds(at, 32), :].astype(jnp.int32) - 1
         plane = (cell >> 7).astype(f32)
         depth = (cell & 127).astype(f32)
-        parts = [split(xs_ref[c, pl.ds(at, 16), :]) for c in range(4)]
+        parts = [split(xs_ref[c, pl.ds(at, 32), :]) for c in range(4)]
         lefts, rights = [], []
-        for u in range(16):
+        for u in range(32):
             rights.append(marked(spots, plane[u : u + 1]))
             at_z = marked(spots[0:128], depth[u : u + 1])
             pieces = [at_z]
@@ -179,7 +179,7 @@
         )
         return carry
 
-    lax.fori_loop(0, half // 16, step, 0)
+    lax.fori_loop(0, half // 32, step, 0)
     wx, wy = count_ref.shape[0], count_ref.shape[1]
     number = acc_ref[0:128, :].T.reshape(wx, wy, 128)
     share = 1.0 / (count_ref[...].astype(f32) + number)

time: 105 us -> 104 us (level)
  Pallas kernels: 52.7 us -> 51.6 us
where the time goes in v4:
time: 104 us; the launch traced here: 103 us
  Pallas kernels  51.6 us (50%)
  starting transfers between devices  39.8 us (38%)
  local copies, waits for them, and re-layouts  6.2 us (6%)
  waiting for transfers between devices  5.01 us (5%)
    all_to_all x4, starting transfers between devices, exchange(): return lax.all_to_all(value, axis, split_axis=0, concat_axis=0, tiled=True)  29.8 us
    pallas_call x1, Pallas kernels, shards(): pl.pallas_call(update_body, out_shape=jax.ShapeDtypeStruct(phi.shape, f32...  16.3 us
    pallas_call x1, Pallas kernels, shards(): pl.pallas_call(fields_body, out_shape=(jax.ShapeDtypeStruct((8, 9, 17, 24...  14.4 us
    ppermute x4, starting transfers between devices, shifted(): return lax.ppermute(value, axis, pairs)  10 us
    unnamed x14, local copies, waits for them, and re-layouts  6.2 us
    pallas_call x1, Pallas kernels, shards(): call(scatter_body, [((4, wx, wy, depth), f32), ((8, cap, 128), f32), ((3,...  6.13 us
    pallas_call x1, Pallas kernels, shards(): call(blend_inner_body, [((4, cap, 128), f32)], [SCALARS] + [WHOLE] * 3, [...  6.04 us
    all_to_all x4, waiting for transfers between devices, exchange(): return lax.all_to_all(value, axis, split_axis=0, concat_axis=0, tiled=True)  5 us
  transfers between devices with their start and end apart: 8, of which 2 were waited for; matrix products, arithmetic and copies ran while one was open for 0% of the time, Pallas kernels for 31%

profile of v4, /device:TPU:1, one launch (start us, length us, event | category | flops | bytes accessed | tf_op | source)
XLA Modules:
  0.0 103.5 jit_solution(13965663371146874251)
XLA Ops:
  0.6 0.0 copy-start.2
  0.6 4.1 %dispatch.1 = (f32[128,4,128]{2,1,0:T(4,128)}, s32[1,2048]{1,0:T(1,128)}) custom-call(s32[1,2048]{1,0:T(1,128)} %bitcast.8, s32[1,2048]{1,0:T(1,128)} %bitcast.10, f32[4,2048]{1,0:T(4,128)} %phi_ref.3, f32[3,2048]{1,0:T(4,128)} %off_ref.2), custom_call_target="tpu_custom_call" | custom-call | tf_op jit(solution)/shard_map/dispatch/pallas_call | solution.py:649
  4.7 11.5 %all-to-all-start = ((f32[128,4,128]{2,1,0:T(4,128)}), f32[128,4,128]{2,1,0:T(4,128)S(1)}, u32[]{:S(2)}, u32[]{:S(2)}) async-start(f32[128,4,128]{2,1,0:T(4,128)} %get-tuple-element.23), calls=%async_computation | async-start | bytes 524288 | tf_op jit(solution)/shard_map/all_to_all | solution.py:637
  16.2 0.0 copy-start.3
  16.2 1.0 copy-done.3
  17.2 0.9 copy-done.4
  18.1 1.1 %pencil_x.1 = f32[16,24,512]{2,1,0:T(8,128)} custom-call(f32[3,8,16,256]{3,2,1,0:T(8,128)S(1)} %bitcast.6, f32[8,16,256]{2,1,0:T(8,128)S(1)} %bitcast.7), custom_call_target="tpu_custom_call" | custom-call | tf_op jit(solution)/shard_map/pencil_x/pallas_call | solution.py:658
  19.2 3.4 %copy-done = f32[4,16,16,16,128]{4,3,2,1,0:T(8,128)S(1)} copy-done((f32[4,16,16,16,128]{4,3,2,1,0:T(8,128)S(1)}, f32[4,16,16,16,128]{4,3,2,1,0:T(8,128)}, u32[]{:S(2)}) %copy-start) | copy-done | bytes 8388632
  22.6 0.9 copy-done.1
  23.5 1.3 %local_sum.1.local_ref = f32[4,16,16,128]{3,2,1,0:T(8,128)S(1)} custom-call(f32[4,16,16,16,128]{4,3,2,1,0:T(8,128)S(1)} %copy-done, s32[16,16,128]{2,1,0:T(8,128)S(1)} %copy-done.1), custom_call_target="tpu_custom_call" | custom-call | flops 4000000 | bytes 9000000 | tf_op jit(solution)/shard_map/local_sum/pallas_call | solution.py:667
  24.9 2.3 %all-to-all-done.arr_ref = f32[128,4,128]{2,1,0:T(4,128)S(1)} async-done(((f32[128,4,128]{2,1,0:T(4,128)}), f32[128,4,128]{2,1,0:T(4,128)S(1)}, u32[]{:S(2)}, u32[]{:S(2)}) %all-to-all-start) | async-done | bytes 262176 | tf_op jit(solution)/shard_map/all_to_all | solution.py:637
  27.1 4.5 %all-to-all-start.1 = ((f32[16,24,512]{2,1,0:T(8,128)}), f32[16,24,512]{2,1,0:T(8,128)S(1)}, u32[]{:S(2)}, u32[]{:S(2)}) async-start(f32[16,24,512]{2,1,0:T(8,128)} %pencil_x.1), calls=%async_computation.1 | async-start | bytes 1572864 | tf_op jit(solution)/shard_map/all_to_all | solution.py:637
  31.6 6.1 %scatter.1 = (f32[4,16,16,128]{3,2,1,0:T(8,128)S(1)}, f32[8,64,128]{2,1,0:T(8,128)S(1)}, s32[3,128]{1,0:T(4,128)S(1)}, f32[4,1,16,128]{3,2,1,0:T(8,128)S(1)}, f3...) custom-call(f32[128,4,128]{2,1,0:T(4,128)S(1)} %all-to-all-done.arr_ref, ...), custom_call_target="tpu_custom_call" | custom-call | flops 4000000000 | bytes 2000000 | tf_op jit(solution)/shard_map/scatter/pallas_call | solution.py:680
  37.7 3.3 %collective-permute-start.1 = (f32[4,1,16,128]{3,2,1,0:T(8,128)S(1)}, f32[4,1,16,128]{3,2,1,0:T(8,128)S(1)}, u32[]{:S(2)}, u32[]{:S(2)}) collective-permute-start(f32[4,1,16,128]{3,2,1,0:T(8,128)S(1)} %get-tuple-element.34), channel_id=1, source_target_pairs={{0,8},{8,16},{16,24},{24,32},{32,40},{40,48},{48,56},{56,64},{64,7... | collective-permute-start | bytes 98312 | tf_op jit(solution)/shard_map/ppermute | solution.py:633
  41.0 1.3 %collective-permute-start = (f32[4,2,16,128]{3,2,1,0:T(8,128)S(1)}, f32[4,2,16,128]{3,2,1,0:T(8,128)S(1)}, u32[]{:S(2)}, u32[]{:S(2)}) collective-permute-start(f32[4,2,16,128]{3,2,1,0:T(8,128)S(1)} %get-tuple-element.31), channel_id=1, source_target_pairs={{8,0},{16,8},{24,16},{32,24},{40,32},{48,40},{56,48},{64,56},{72,6... | collective-permute-start | bytes 196616 | tf_op jit(solution)/shard_map/ppermute | solution.py:633
  42.3 0.1 add_convert_fusion.last_ref
  42.4 2.7 %all-to-all-done.1.in_ref = f32[16,24,512]{2,1,0:T(8,128)S(1)} async-done(((f32[16,24,512]{2,1,0:T(8,128)}), f32[16,24,512]{2,1,0:T(8,128)S(1)}, u32[]{:S(2)}, u32[]{:S(2)}) %all-to-all-start.1) | async-done | bytes 786464 | tf_op jit(solution)/shard_map/all_to_all | solution.py:637
  45.1 1.0 pencil_y.1
  46.1 6.5 %all-to-all-start.2 = ((f32[8,16,1280]{2,1,0:T(8,128)}), f32[8,16,1280]{2,1,0:T(8,128)S(1)}, u32[]{:S(2)}, u32[]{:S(2)}) async-start(f32[8,16,1280]{2,1,0:T(8,128)} %pencil_y.1), calls=%async_computation.2 | async-start | bytes 1310720 | tf_op jit(solution)/shard_map/all_to_all | solution.py:637
  52.7 0.0 collective-permute-done.1.lo_ref
  52.7 0.0 collective-permute-done.hi_ref
  52.7 3.5 %collective-permute-start.2 = (f32[4,24,128]{2,1,0:T(8,128)S(1)}, f32[4,24,128]{2,1,0:T(8,128)S(1)}, u32[]{:S(2)}, u32[]{:S(2)}) collective-permute-start(f32[4,24,128]{2,1,0:T(8,128)S(1)} %get-tuple-element.38), channel_id=1, source_target_pairs={{0,1},{1,2},{2,3},{3,4},{4,5},{5,6},{6,7},{8,9},{9,10},{10,11},{11... | collective-permute-start | bytes 147464 | tf_op jit(solution)/shard_map/ppermute | solution.py:633
  56.3 1.9 %collective-permute-start.3 = (f32[2,4,24,128]{3,2,1,0:T(8,128)S(1)}, f32[2,4,24,128]{3,2,1,0:T(8,128)S(1)}, u32[]{:S(2)}, u32[]{:S(2)}) collective-permute-start(f32[2,4,24,128]{3,2,1,0:T(8,128)S(1)} %get-tuple-element.39), channel_id=1, source_target_pairs={{1,0},{2,1},{3,2},{4,3},{5,4},{6,5},{7,6},{9,8},{10,9},{11,10},{12... | collective-permute-start | bytes 294920 | tf_op jit(solution)/shard_map/ppermute | solution.py:633
  58.2 6.0 %blend_inner.1.inner_ref = f32[4,64,128]{2,1,0:T(8,128)S(1)} custom-call(s32[3,128]{1,0:T(4,128)S(1)} %get-tuple-element.26.bound_ref, f32[4,16,16,128]{3,2,1,0:T(8,128)S(1)} %get-tuple-element.30.mean_ref, f32[4,2,16,128]{3,2,1,0:T(8,128)S(1)} %collective-permute-done.hi_ref, f32[8,64,128]{2,1,0:T(8,128)S(1)} %get-tuple-element.32.xs_ref), custom_call_target="tpu_custom_call" | custom-call | flops 8000000000 | bytes 3000000 | tf_op jit(solution)/shard_map/blend_inner/pallas_call | solution.py:715
  64.2 0.0 all-to-all-done.2.wide_ref
  64.2 0.0 collective-permute-done.2.ylo_ref
  64.3 14.4 %fields.1 = (f32[8,9,17,24,128]{4,3,2,1,0:T(8,128)}, f32[128,2,128]{2,1,0:T(2,128)}) custom-call(s32[2]{0:T(128)S(1)} %add_convert_fusion.last_ref, s32[3,128]{1,0:T(4,128)S(1)} %get-tuple-element.26.bound_ref, f32[8,16,1280]{2,1,0:T(8,128)S(1)} %all-to-all-done.2.wide_ref, f32[4,16,16,128]{3,2,1,0:T(8,128)S(1)} %get-tuple-element.30.mean_ref, ...), custom_call_target="tpu_custom_call" | custom-call | tf_op jit(solution)/shard_map/fields/pallas_call | solution.py:731
  78.7 7.3 %all-to-all-start.3 = ((f32[128,2,128]{2,1,0:T(2,128)}), f32[128,2,128]{2,1,0:T(2,128)S(1)}, u32[]{:S(2)}, u32[]{:S(2)}) async-start(f32[128,2,128]{2,1,0:T(2,128)} %get-tuple-element.43), calls=%async_computation.3 | async-start | bytes 262144 | tf_op jit(solution)/shard_map/all_to_all | solution.py:637
  85.9 0.0 copy-start.5
  86.0 0.0 copy-start.6
  86.0 16.3 %update.1 = f32[4,16,16,16,128]{4,3,2,1,0:T(8,128)} custom-call(f32[4,16,16,16,128]{4,3,2,1,0:T(8,128)} %phi_ref.5, f32[3,16,16,16,128]{4,3,2,1,0:T(8,128)} %off_ref.3, s32[16,16,128]{2,1,0:T(8,128)} %count_ref.5, f32[8,9,17,24,128]{4,3,2,1,0:T(8,128)} %get-tuple-element.41.f_ref.f_next_ref.rise_ref.rise_next_ref, ...), custom_call_target="tpu_custom_call" | custom-call | flops 80000000 | bytes 25000000 | tf_op jit(solution)/shard_map/update/pallas_call | solution.py:763
  102.3 1.2 %collect.1 = f32[4,2048]{1,0:T(4,128)} custom-call(s32[1,2048]{1,0:T(1,128)S(1)} %bitcast.9, s32[1,2048]{1,0:T(1,128)S(1)} %copy-done.6, f32[128,2,128]{2,1,0:T(2,128)S(1)} %all-to-all-done.3.back_ref), custom_call_target="tpu_custom_call" | custom-call | tf_op jit(solution)/shard_map/collect/pallas_call | solution.py:775
  (9 shorter events, 0.0 us)
Async XLA Ops:
  0.6 31.0 %copy-start.2 = (s32[16,16,128]{2,1,0:T(8,128)S(1)}, s32[16,16,128]{2,1,0:T(8,128)}, u32[]{:S(2)}) copy-start(s32[16,16,128]{2,1,0:T(8,128)} %count_ref.5) | copy-start | bytes 393220
  4.7 22.4 %all-to-all-start = ((f32[128,4,128]{2,1,0:T(4,128)}), f32[128,4,128]{2,1,0:T(4,128)S(1)}, u32[]{:S(2)}, u32[]{:S(2)}) async-start(f32[128,4,128]{2,1,0:T(4,128)} %get-tuple-element.23), calls=%async_computation | async-start | bytes 524288 | tf_op jit(solution)/shard_map/all_to_all | solution.py:637
  16.2 1.0 copy-start.3
  17.2 0.9 copy-start.4
  19.2 3.4 %copy-start = (f32[4,16,16,16,128]{4,3,2,1,0:T(8,128)S(1)}, f32[4,16,16,16,128]{4,3,2,1,0:T(8,128)}, u32[]{:S(2)}) copy-start(f32[4,16,16,16,128]{4,3,2,1,0:T(8,128)} %phi_ref.5) | copy-start | bytes 25165828
  22.6 0.9 copy-start.1
  27.1 18.0 %all-to-all-start.1 = ((f32[16,24,512]{2,1,0:T(8,128)}), f32[16,24,512]{2,1,0:T(8,128)S(1)}, u32[]{:S(2)}, u32[]{:S(2)}) async-start(f32[16,24,512]{2,1,0:T(8,128)} %pencil_x.1), calls=%async_computation.1 | async-start | bytes 1572864 | tf_op jit(solution)/shard_map/all_to_all | solution.py:637
  37.7 14.9 %collective-permute-start.1 = (f32[4,1,16,128]{3,2,1,0:T(8,128)S(1)}, f32[4,1,16,128]{3,2,1,0:T(8,128)S(1)}, u32[]{:S(2)}, u32[]{:S(2)}) collective-permute-start(f32[4,1,16,128]{3,2,1,0:T(8,128)S(1)} %get-tuple-element.34), channel_id=1, source_target_pairs={{0,8},{8,16},{16,24},{24,32},{32,40},{40,48},{48,56},{56,64},{64,7... | collective-permute-start | bytes 98312 | tf_op jit(solution)/shard_map/ppermute | solution.py:633
  41.0 11.7 %collective-permute-start = (f32[4,2,16,128]{3,2,1,0:T(8,128)S(1)}, f32[4,2,16,128]{3,2,1,0:T(8,128)S(1)}, u32[]{:S(2)}, u32[]{:S(2)}) collective-permute-start(f32[4,2,16,128]{3,2,1,0:T(8,128)S(1)} %get-tuple-element.31), channel_id=1, source_target_pairs={{8,0},{16,8},{24,16},{32,24},{40,32},{48,40},{56,48},{64,56},{72,6... | collective-permute-start | bytes 196616 | tf_op jit(solution)/shard_map/ppermute | solution.py:633
  46.1 18.1 %all-to-all-start.2 = ((f32[8,16,1280]{2,1,0:T(8,128)}), f32[8,16,1280]{2,1,0:T(8,128)S(1)}, u32[]{:S(2)}, u32[]{:S(2)}) async-start(f32[8,16,1280]{2,1,0:T(8,128)} %pencil_y.1), calls=%async_computation.2 | async-start | bytes 1310720 | tf_op jit(solution)/shard_map/all_to_all | solution.py:637
  52.7 11.5 %collective-permute-start.2 = (f32[4,24,128]{2,1,0:T(8,128)S(1)}, f32[4,24,128]{2,1,0:T(8,128)S(1)}, u32[]{:S(2)}, u32[]{:S(2)}) collective-permute-start(f32[4,24,128]{2,1,0:T(8,128)S(1)} %get-tuple-element.38), channel_id=1, source_target_pairs={{0,1},{1,2},{2,3},{3,4},{4,5},{5,6},{6,7},{8,9},{9,10},{10,11},{11... | collective-permute-start | bytes 147464 | tf_op jit(solution)/shard_map/ppermute | solution.py:633
  56.3 8.0 %collective-permute-start.3 = (f32[2,4,24,128]{3,2,1,0:T(8,128)S(1)}, f32[2,4,24,128]{3,2,1,0:T(8,128)S(1)}, u32[]{:S(2)}, u32[]{:S(2)}) collective-permute-start(f32[2,4,24,128]{3,2,1,0:T(8,128)S(1)} %get-tuple-element.39), channel_id=1, source_target_pairs={{1,0},{2,1},{3,2},{4,3},{5,4},{6,5},{7,6},{9,8},{10,9},{11,10},{12... | collective-permute-start | bytes 294920 | tf_op jit(solution)/shard_map/ppermute | solution.py:633
  78.7 23.6 %all-to-all-start.3 = ((f32[128,2,128]{2,1,0:T(2,128)}), f32[128,2,128]{2,1,0:T(2,128)S(1)}, u32[]{:S(2)}, u32[]{:S(2)}) async-start(f32[128,2,128]{2,1,0:T(2,128)} %get-tuple-element.43), calls=%async_computation.3 | async-start | bytes 262144 | tf_op jit(solution)/shard_map/all_to_all | solution.py:637
  85.9 16.3 %copy-start.5 = (s32[2048,1]{0,1:T(1,128)S(1)}, s32[2048,1]{0,1:T(1,128)}, u32[]{:S(2)}) copy-start(s32[2048,1]{0,1:T(1,128)} %param.16) | copy-start | bytes 24580
  86.0 16.3 %copy-start.6 = (s32[1,2048]{1,0:T(1,128)S(1)}, s32[1,2048]{1,0:T(1,128)}, u32[]{:S(2)}) copy-start(s32[1,2048]{1,0:T(1,128)} %get-tuple-element.42.rank_ref) | copy-start | bytes 24580

commit v5 on v4

--- a/solution.py
+++ b/solution.py
@@ -495,7 +495,13 @@
         rise_ref[8, x, 0:16, :] = gammas[2][0] - gamma
         return carry
 
-    lax.fori_loop(0, 17, plane, 0)
+    def several(i, carry):
+        for k in range(4):
+            plane(4 * i + k, carry)
+        return carry
+
+    lax.fori_loop(0, 4, several, 0)
+    plane(16, 0)
     row = iota((24, 128), 0)
 
     def x_up(value):

time: 104 us -> 103 us (level)
  Pallas kernels: 51.6 us -> 49.9 us
    pallas_call x1, Pallas kernels: 14.4 us -> 12.7 us  [shards(): pl.pallas_call(fields_body, out_shape=(jax.ShapeDtypeStruct((8, 9, 17, 24...]
where the time goes in v5:
time: 103 us; the launch traced here: 102 us
  Pallas kernels  49.9 us (48%)
  starting transfers between devices  39.7 us (39%)
  local copies, waits for them, and re-layouts  6.2 us (6%)
  waiting for transfers between devices  5.01 us (5%)
    all_to_all x4, starting transfers between devices, exchange(): return lax.all_to_all(value, axis, split_axis=0, concat_axis=0, tiled=True)  29.7 us
    pallas_call x1, Pallas kernels, shards(): pl.pallas_call(update_body, out_shape=jax.ShapeDtypeStruct(phi.shape, f32...  16.3 us
    pallas_call x1, Pallas kernels, shards(): pl.pallas_call(fields_body, out_shape=(jax.ShapeDtypeStruct((8, 9, 17, 24...  12.7 us
    ppermute x4, starting transfers between devices, shifted(): return lax.ppermute(value, axis, pairs)  10 us
    unnamed x14, local copies, waits for them, and re-layouts  6.2 us
    pallas_call x1, Pallas kernels, shards(): call(scatter_body, [((4, wx, wy, depth), f32), ((8, cap, 128), f32), ((3,...  6.13 us
    pallas_call x1, Pallas kernels, shards(): call(blend_inner_body, [((4, cap, 128), f32)], [SCALARS] + [WHOLE] * 3, [...  6.04 us
    all_to_all x4, waiting for transfers between devices, exchange(): return lax.all_to_all(value, axis, split_axis=0, concat_axis=0, tiled=True)  5 us
  transfers between devices with their start and end apart: 8, of which 2 were waited for; matrix products, arithmetic and copies ran while one was open for 0% of the time, Pallas kernels for 31%

profile of v5, /device:TPU:1, one launch (start us, length us, event | category | flops | bytes accessed | tf_op | source)
XLA Modules:
  0.0 101.7 jit_solution(2457642144354948062)
XLA Ops:
  0.6 0.0 copy-start.2
  0.6 4.1 %dispatch.1 = (f32[128,4,128]{2,1,0:T(4,128)}, s32[1,2048]{1,0:T(1,128)}) custom-call(s32[1,2048]{1,0:T(1,128)} %bitcast.8, s32[1,2048]{1,0:T(1,128)} %bitcast.10, f32[4,2048]{1,0:T(4,128)} %phi_ref.3, f32[3,2048]{1,0:T(4,128)} %off_ref.2), custom_call_target="tpu_custom_call" | custom-call | tf_op jit(solution)/shard_map/dispatch/pallas_call | solution.py:655
  4.7 11.5 %all-to-all-start = ((f32[128,4,128]{2,1,0:T(4,128)}), f32[128,4,128]{2,1,0:T(4,128)S(1)}, u32[]{:S(2)}, u32[]{:S(2)}) async-start(f32[128,4,128]{2,1,0:T(4,128)} %get-tuple-element.23), calls=%async_computation | async-start | bytes 524288 | tf_op jit(solution)/shard_map/all_to_all | solution.py:643
  16.2 0.0 copy-start.3
  16.2 1.0 copy-done.3
  17.2 0.9 copy-done.4
  18.1 1.1 %pencil_x.1 = f32[16,24,512]{2,1,0:T(8,128)} custom-call(f32[3,8,16,256]{3,2,1,0:T(8,128)S(1)} %bitcast.6, f32[8,16,256]{2,1,0:T(8,128)S(1)} %bitcast.7), custom_call_target="tpu_custom_call" | custom-call | tf_op jit(solution)/shard_map/pencil_x/pallas_call | solution.py:664
  19.2 3.4 %copy-done = f32[4,16,16,16,128]{4,3,2,1,0:T(8,128)S(1)} copy-done((f32[4,16,16,16,128]{4,3,2,1,0:T(8,128)S(1)}, f32[4,16,16,16,128]{4,3,2,1,0:T(8,128)}, u32[]{:S(2)}) %copy-start) | copy-done | bytes 8388632
  22.6 0.9 copy-done.1
  23.5 1.3 %local_sum.1.local_ref = f32[4,16,16,128]{3,2,1,0:T(8,128)S(1)} custom-call(f32[4,16,16,16,128]{4,3,2,1,0:T(8,128)S(1)} %copy-done, s32[16,16,128]{2,1,0:T(8,128)S(1)} %copy-done.1), custom_call_target="tpu_custom_call" | custom-call | flops 4000000 | bytes 9000000 | tf_op jit(solution)/shard_map/local_sum/pallas_call | solution.py:673
  24.9 2.3 %all-to-all-done.arr_ref = f32[128,4,128]{2,1,0:T(4,128)S(1)} async-done(((f32[128,4,128]{2,1,0:T(4,128)}), f32[128,4,128]{2,1,0:T(4,128)S(1)}, u32[]{:S(2)}, u32[]{:S(2)}) %all-to-all-start) | async-done | bytes 262176 | tf_op jit(solution)/shard_map/all_to_all | solution.py:643
  27.1 4.5 %all-to-all-start.1 = ((f32[16,24,512]{2,1,0:T(8,128)}), f32[16,24,512]{2,1,0:T(8,128)S(1)}, u32[]{:S(2)}, u32[]{:S(2)}) async-start(f32[16,24,512]{2,1,0:T(8,128)} %pencil_x.1), calls=%async_computation.1 | async-start | bytes 1572864 | tf_op jit(solution)/shard_map/all_to_all | solution.py:643
  31.6 6.1 %scatter.1 = (f32[4,16,16,128]{3,2,1,0:T(8,128)S(1)}, f32[8,64,128]{2,1,0:T(8,128)S(1)}, s32[3,128]{1,0:T(4,128)S(1)}, f32[4,1,16,128]{3,2,1,0:T(8,128)S(1)}, f3...) custom-call(f32[128,4,128]{2,1,0:T(4,128)S(1)} %all-to-all-done.arr_ref, ...), custom_call_target="tpu_custom_call" | custom-call | flops 4000000000 | bytes 2000000 | tf_op jit(solution)/shard_map/scatter/pallas_call | solution.py:686
  37.7 3.3 %collective-permute-start.1 = (f32[4,1,16,128]{3,2,1,0:T(8,128)S(1)}, f32[4,1,16,128]{3,2,1,0:T(8,128)S(1)}, u32[]{:S(2)}, u32[]{:S(2)}) collective-permute-start(f32[4,1,16,128]{3,2,1,0:T(8,128)S(1)} %get-tuple-element.34), channel_id=1, source_target_pairs={{0,8},{8,16},{16,24},{24,32},{32,40},{40,48},{48,56},{56,64},{64,7... | collective-permute-start | bytes 98312 | tf_op jit(solution)/shard_map/ppermute | solution.py:639
  41.0 1.3 %collective-permute-start = (f32[4,2,16,128]{3,2,1,0:T(8,128)S(1)}, f32[4,2,16,128]{3,2,1,0:T(8,128)S(1)}, u32[]{:S(2)}, u32[]{:S(2)}) collective-permute-start(f32[4,2,16,128]{3,2,1,0:T(8,128)S(1)} %get-tuple-element.31), channel_id=1, source_target_pairs={{8,0},{16,8},{24,16},{32,24},{40,32},{48,40},{56,48},{64,56},{72,6... | collective-permute-start | bytes 196616 | tf_op jit(solution)/shard_map/ppermute | solution.py:639
  42.3 0.1 add_convert_fusion.last_ref
  42.4 2.7 %all-to-all-done.1.in_ref = f32[16,24,512]{2,1,0:T(8,128)S(1)} async-done(((f32[16,24,512]{2,1,0:T(8,128)}), f32[16,24,512]{2,1,0:T(8,128)S(1)}, u32[]{:S(2)}, u32[]{:S(2)}) %all-to-all-start.1) | async-done | bytes 786464 | tf_op jit(solution)/shard_map/all_to_all | solution.py:643
  45.1 1.0 pencil_y.1
  46.1 6.5 %all-to-all-start.2 = ((f32[8,16,1280]{2,1,0:T(8,128)}), f32[8,16,1280]{2,1,0:T(8,128)S(1)}, u32[]{:S(2)}, u32[]{:S(2)}) async-start(f32[8,16,1280]{2,1,0:T(8,128)} %pencil_y.1), calls=%async_computation.2 | async-start | bytes 1310720 | tf_op jit(solution)/shard_map/all_to_all | solution.py:643
  52.7 0.0 collective-permute-done.1.lo_ref
  52.7 0.0 collective-permute-done.hi_ref
  52.7 3.5 %collective-permute-start.2 = (f32[4,24,128]{2,1,0:T(8,128)S(1)}, f32[4,24,128]{2,1,0:T(8,128)S(1)}, u32[]{:S(2)}, u32[]{:S(2)}) collective-permute-start(f32[4,24,128]{2,1,0:T(8,128)S(1)} %get-tuple-element.38), channel_id=1, source_target_pairs={{0,1},{1,2},{2,3},{3,4},{4,5},{5,6},{6,7},{8,9},{9,10},{10,11},{11... | collective-permute-start | bytes 147464 | tf_op jit(solution)/shard_map/ppermute | solution.py:639
  56.3 1.9 %collective-permute-start.3 = (f32[2,4,24,128]{3,2,1,0:T(8,128)S(1)}, f32[2,4,24,128]{3,2,1,0:T(8,128)S(1)}, u32[]{:S(2)}, u32[]{:S(2)}) collective-permute-start(f32[2,4,24,128]{3,2,1,0:T(8,128)S(1)} %get-tuple-element.39), channel_id=1, source_target_pairs={{1,0},{2,1},{3,2},{4,3},{5,4},{6,5},{7,6},{9,8},{10,9},{11,10},{12... | collective-permute-start | bytes 294920 | tf_op jit(solution)/shard_map/ppermute | solution.py:639
  58.2 6.0 %blend_inner.1.inner_ref = f32[4,64,128]{2,1,0:T(8,128)S(1)} custom-call(s32[3,128]{1,0:T(4,128)S(1)} %get-tuple-element.26.bound_ref, f32[4,16,16,128]{3,2,1,0:T(8,128)S(1)} %get-tuple-element.30.mean_ref, f32[4,2,16,128]{3,2,1,0:T(8,128)S(1)} %collective-permute-done.hi_ref, f32[8,64,128]{2,1,0:T(8,128)S(1)} %get-tuple-element.32.xs_ref), custom_call_target="tpu_custom_call" | custom-call | flops 8000000000 | bytes 3000000 | tf_op jit(solution)/shard_map/blend_inner/pallas_call | solution.py:721
  64.2 0.0 collective-permute-done.2.ylo_ref
  64.3 12.7 %fields.1 = (f32[8,9,17,24,128]{4,3,2,1,0:T(8,128)}, f32[128,2,128]{2,1,0:T(2,128)}) custom-call(s32[2]{0:T(128)S(1)} %add_convert_fusion.last_ref, s32[3,128]{1,0:T(4,128)S(1)} %get-tuple-element.26.bound_ref, f32[8,16,1280]{2,1,0:T(8,128)S(1)} %all-to-all-done.2.wide_ref, f32[4,16,16,128]{3,2,1,0:T(8,128)S(1)} %get-tuple-element.30.mean_ref, ...), custom_call_target="tpu_custom_call" | custom-call | tf_op jit(solution)/shard_map/fields/pallas_call | solution.py:737
  77.0 7.2 %all-to-all-start.3 = ((f32[128,2,128]{2,1,0:T(2,128)}), f32[128,2,128]{2,1,0:T(2,128)S(1)}, u32[]{:S(2)}, u32[]{:S(2)}) async-start(f32[128,2,128]{2,1,0:T(2,128)} %get-tuple-element.43), calls=%async_computation.3 | async-start | bytes 262144 | tf_op jit(solution)/shard_map/all_to_all | solution.py:643
  84.2 0.0 copy-start.5
  84.2 0.0 copy-start.6
  84.2 16.3 %update.1 = f32[4,16,16,16,128]{4,3,2,1,0:T(8,128)} custom-call(f32[4,16,16,16,128]{4,3,2,1,0:T(8,128)} %phi_ref.5, f32[3,16,16,16,128]{4,3,2,1,0:T(8,128)} %off_ref.3, s32[16,16,128]{2,1,0:T(8,128)} %count_ref.5, f32[8,9,17,24,128]{4,3,2,1,0:T(8,128)} %get-tuple-element.41.f_ref.f_next_ref.rise_ref.rise_next_ref, ...), custom_call_target="tpu_custom_call" | custom-call | flops 80000000 | bytes 25000000 | tf_op jit(solution)/shard_map/update/pallas_call | solution.py:769
  100.5 0.0 all-to-all-done.3.back_ref
  100.5 1.2 %collect.1 = f32[4,2048]{1,0:T(4,128)} custom-call(s32[1,2048]{1,0:T(1,128)S(1)} %bitcast.9, s32[1,2048]{1,0:T(1,128)S(1)} %copy-done.6, f32[128,2,128]{2,1,0:T(2,128)S(1)} %all-to-all-done.3.back_ref), custom_call_target="tpu_custom_call" | custom-call | tf_op jit(solution)/shard_map/collect/pallas_call | solution.py:781
  (9 shorter events, 0.0 us)
Async XLA Ops:
  0.6 31.0 %copy-start.2 = (s32[16,16,128]{2,1,0:T(8,128)S(1)}, s32[16,16,128]{2,1,0:T(8,128)}, u32[]{:S(2)}) copy-start(s32[16,16,128]{2,1,0:T(8,128)} %count_ref.5) | copy-start | bytes 393220
  4.7 22.4 %all-to-all-start = ((f32[128,4,128]{2,1,0:T(4,128)}), f32[128,4,128]{2,1,0:T(4,128)S(1)}, u32[]{:S(2)}, u32[]{:S(2)}) async-start(f32[128,4,128]{2,1,0:T(4,128)} %get-tuple-element.23), calls=%async_computation | async-start | bytes 524288 | tf_op jit(solution)/shard_map/all_to_all | solution.py:643
  16.2 1.0 copy-start.3
  17.2 0.9 copy-start.4
  19.2 3.4 %copy-start = (f32[4,16,16,16,128]{4,3,2,1,0:T(8,128)S(1)}, f32[4,16,16,16,128]{4,3,2,1,0:T(8,128)}, u32[]{:S(2)}) copy-start(f32[4,16,16,16,128]{4,3,2,1,0:T(8,128)} %phi_ref.5) | copy-start | bytes 25165828
  22.6 0.9 copy-start.1
  27.1 18.0 %all-to-all-start.1 = ((f32[16,24,512]{2,1,0:T(8,128)}), f32[16,24,512]{2,1,0:T(8,128)S(1)}, u32[]{:S(2)}, u32[]{:S(2)}) async-start(f32[16,24,512]{2,1,0:T(8,128)} %pencil_x.1), calls=%async_computation.1 | async-start | bytes 1572864 | tf_op jit(solution)/shard_map/all_to_all | solution.py:643
  37.7 14.9 %collective-permute-start.1 = (f32[4,1,16,128]{3,2,1,0:T(8,128)S(1)}, f32[4,1,16,128]{3,2,1,0:T(8,128)S(1)}, u32[]{:S(2)}, u32[]{:S(2)}) collective-permute-start(f32[4,1,16,128]{3,2,1,0:T(8,128)S(1)} %get-tuple-element.34), channel_id=1, source_target_pairs={{0,8},{8,16},{16,24},{24,32},{32,40},{40,48},{48,56},{56,64},{64,7... | collective-permute-start | bytes 98312 | tf_op jit(solution)/shard_map/ppermute | solution.py:639
  41.0 11.7 %collective-permute-start = (f32[4,2,16,128]{3,2,1,0:T(8,128)S(1)}, f32[4,2,16,128]{3,2,1,0:T(8,128)S(1)}, u32[]{:S(2)}, u32[]{:S(2)}) collective-permute-start(f32[4,2,16,128]{3,2,1,0:T(8,128)S(1)} %get-tuple-element.31), channel_id=1, source_target_pairs={{8,0},{16,8},{24,16},{32,24},{40,32},{48,40},{56,48},{64,56},{72,6... | collective-permute-start | bytes 196616 | tf_op jit(solution)/shard_map/ppermute | solution.py:639
  46.1 18.1 %all-to-all-start.2 = ((f32[8,16,1280]{2,1,0:T(8,128)}), f32[8,16,1280]{2,1,0:T(8,128)S(1)}, u32[]{:S(2)}, u32[]{:S(2)}) async-start(f32[8,16,1280]{2,1,0:T(8,128)} %pencil_y.1), calls=%async_computation.2 | async-start | bytes 1310720 | tf_op jit(solution)/shard_map/all_to_all | solution.py:643
  52.7 11.5 %collective-permute-start.2 = (f32[4,24,128]{2,1,0:T(8,128)S(1)}, f32[4,24,128]{2,1,0:T(8,128)S(1)}, u32[]{:S(2)}, u32[]{:S(2)}) collective-permute-start(f32[4,24,128]{2,1,0:T(8,128)S(1)} %get-tuple-element.38), channel_id=1, source_target_pairs={{0,1},{1,2},{2,3},{3,4},{4,5},{5,6},{6,7},{8,9},{9,10},{10,11},{11... | collective-permute-start | bytes 147464 | tf_op jit(solution)/shard_map/ppermute | solution.py:639
  56.3 8.0 %collective-permute-start.3 = (f32[2,4,24,128]{3,2,1,0:T(8,128)S(1)}, f32[2,4,24,128]{3,2,1,0:T(8,128)S(1)}, u32[]{:S(2)}, u32[]{:S(2)}) collective-permute-start(f32[2,4,24,128]{3,2,1,0:T(8,128)S(1)} %get-tuple-element.39), channel_id=1, source_target_pairs={{1,0},{2,1},{3,2},{4,3},{5,4},{6,5},{7,6},{9,8},{10,9},{11,10},{12... | collective-permute-start | bytes 294920 | tf_op jit(solution)/shard_map/ppermute | solution.py:639
  77.0 23.5 %all-to-all-start.3 = ((f32[128,2,128]{2,1,0:T(2,128)}), f32[128,2,128]{2,1,0:T(2,128)S(1)}, u32[]{:S(2)}, u32[]{:S(2)}) async-start(f32[128,2,128]{2,1,0:T(2,128)} %get-tuple-element.43), calls=%async_computation.3 | async-start | bytes 262144 | tf_op jit(solution)/shard_map/all_to_all | solution.py:643
  84.2 16.3 %copy-start.5 = (s32[2048,1]{0,1:T(1,128)S(1)}, s32[2048,1]{0,1:T(1,128)}, u32[]{:S(2)}) copy-start(s32[2048,1]{0,1:T(1,128)} %param.16) | copy-start | bytes 24580
  84.2 16.3 %copy-start.6 = (s32[1,2048]{1,0:T(1,128)S(1)}, s32[1,2048]{1,0:T(1,128)}, u32[]{:S(2)}) copy-start(s32[1,2048]{1,0:T(1,128)} %get-tuple-element.42.rank_ref) | copy-start | bytes 24580
